TPU v7x, 512 devices: a whole 4x4x16 slice. The times are simulated.
512 devices in a mesh: ctx: 32 (over z, x_lo), exp: 8 (over x_hi, y), rep: 2 (over core).
Axes of the slice: x: 4 (x_hi: 2, x_lo: 2; x = x_hi * 2 + x_lo), y: 4, z: 16, core: 2. Of those that a mesh axis runs over, the one named last changes fastest.
Arguments:
- queries: bfloat16 [2, 4096, 8, 512], P('rep', 'ctx', 'exp'), may hold values from -36 to 36
- latents: bfloat16 [2, 4096, 512], P('rep', 'ctx'), may hold values from -6 to 6
- tokens: bfloat16 [2, 4096, 2048], P('rep', 'ctx', 'exp'), may hold values from -12 to 12
- block_mask: int32 [8, 32, 32], P('exp'), may hold values 0 or 1
- uv_weight: bfloat16 [8, 512, 128], P('exp'), may hold values from -0.25 to 0.25
- out_weight: bfloat16 [8, 128, 2048], P('exp'), may hold values from -0.5 to 0.5
- norm_gain: bfloat16 [2048], P('exp'), may hold values from 0.099609375 to 1.8984375
- router_matrix: bfloat16 [64, 2048], P(None, 'exp'), may hold values from -0.25 to 0.25
- routes: int32 [2, 4096, 6], P('rep', 'ctx'), may hold values from 0 to 63, all different within a row; in each aligned block of 128 rows (0 to 127, 128 to 255, ..., all dimensions but the last counted through in order) at most 16 rows name the same one
- gate_weight: bfloat16 [64, 1408, 2048], P(('ctx', 'rep'), 'exp'), may hold values from -0.125 to 0.125
- up_weight: bfloat16 [64, 1408, 2048], P(('ctx', 'rep'), 'exp'), may hold values from -0.125 to 0.125
- down_weight: bfloat16 [64, 1408, 2048], P(('ctx', 'rep'), None, 'exp'), may hold values from -0.15625 to 0.15625
Outputs:
- hidden: bfloat16 [2, 4096, 2048], P('rep', 'ctx', 'exp')
- routed: bfloat16 [2, 4096, 2048], P('rep', 'ctx', 'exp')
Inputs may be any that keep to these rules, and one draw needn't show every extreme that they name: `routes`: in each aligned block of 128 tokens (one sequence's positions on one index of ctx) no expert is named more than 16 times, a bound that some block reaches; the 6 experts of a token differ.
All inputs are finite; a program needn't handle non-finite values. No bound on the sum of `block_mask` on one device may be relied on, other than what follows from the above.
Results may differ from a plain program's by a relative error of at most 0.029.
Values may be sent and summed in bfloat16 or wider, within the bound.
No kernel may reach another device: no remote copies, remote signals or barrier semaphores. Data moves between devices by JAX's collectives and lax.ppermute only.
A program may use at most 64 MiB of HBM per device.

v0:
```python
import jax
import jax.numpy as jnp
from jax import lax
from jax.sharding import PartitionSpec as P

score_scale = 192.0 ** (-0.5)
epsilon = 1e-06


def body(
    queries,
    latents,
    tokens,
    block_mask,
    uv_weight,
    out_weight,
    norm_gain,
    router_matrix,
    routes,
    gate_weight,
    up_weight,
    down_weight,
):
    seq_rows = queries.shape[1]
    local_heads = queries.shape[2]
    width_slice = tokens.shape[2]
    experts = router_matrix.shape[0]
    top_routes = routes.shape[2]
    capacity = 4 * seq_rows * top_routes // (3 * experts)
    ctx_place = lax.axis_index("ctx")
    query_pos = ctx_place * seq_rows + jnp.arange(seq_rows, dtype=jnp.int32)
    mask_row = lax.dynamic_index_in_dim(block_mask, ctx_place, 1, keepdims=False)
    block_ids = jnp.arange(block_mask.shape[1], dtype=jnp.int32)
    query_local = queries[0]
    start_state = (
        jnp.full((local_heads, seq_rows), -1e30, jnp.float32),
        jnp.zeros((local_heads, seq_rows), jnp.float32),
        jnp.zeros((local_heads, seq_rows, latents.shape[2]), jnp.float32),
    )
    key_rows = lax.all_gather(latents, "ctx", axis=1, tiled=True)[0]
    length = key_rows.shape[0]
    key_pos = jnp.arange(length, dtype=jnp.int32)
    key_blocks = key_pos // seq_rows
    chosen = jnp.sum(
        mask_row[:, :, None]
        * (key_blocks[None, None, :] == block_ids[None, :, None]).astype(jnp.int32),
        axis=1,
    )
    same_block = (key_blocks == ctx_place)[None, None, :] & (
        key_pos[None, None, :] <= query_pos[None, :, None]
    )
    earlier = (key_blocks < ctx_place)[None, None, :] & (chosen[:, None, :] == 1)
    allowed = same_block | earlier

    def update(state):
        highest, totals, accum = state
        scores = (
            jnp.einsum("shl,nl->hsn", query_local, key_rows, preferred_element_type=jnp.float32)
            * score_scale
        )
        masked = jnp.where(allowed, scores, -1e30)
        new_high = jnp.maximum(highest, jnp.max(masked, axis=-1))
        probs = jnp.where(allowed, jnp.exp(masked - new_high[..., None]), 0.0)
        new_totals = jnp.sum(probs, axis=-1)
        product = jnp.einsum(
            "hsn,nl->hsl", probs.astype(jnp.bfloat16), key_rows, preferred_element_type=jnp.float32
        )
        return (new_high, new_totals, product)

    def keep(state):
        return state

    highest, totals, accum = lax.cond(jnp.any(allowed), update, keep, start_state)
    latent_out = (accum / totals[..., None]).astype(jnp.bfloat16)
    head_values = jnp.einsum(
        "hsl,hlv->hsv", latent_out, uv_weight, preferred_element_type=jnp.float32
    ).astype(jnp.bfloat16)
    attention = lax.psum_scatter(
        jnp.einsum(
            "hsv,hvc->cs", head_values, out_weight, preferred_element_type=jnp.float32
        ).astype(jnp.bfloat16),
        "exp",
        scatter_dimension=0,
        tiled=True,
    ).astype(jnp.float32)
    hidden = (tokens[0].astype(jnp.float32) + attention.T).astype(jnp.bfloat16)
    flat_routes = routes[0].reshape(-1)
    onehot = (flat_routes[:, None] == jnp.arange(experts, dtype=jnp.int32)[None, :]).astype(
        jnp.int32
    )
    slot = jnp.sum(onehot * (jnp.cumsum(onehot, axis=0) - 1), axis=1)
    place = flat_routes * capacity + slot
    token_ids = jnp.arange(seq_rows * top_routes, dtype=jnp.int32) // top_routes
    token_lookup = jnp.zeros((experts * capacity,), jnp.int32).at[place].set(token_ids)
    filled = jnp.zeros((experts * capacity,), jnp.int32).at[place].set(1)
    gate_rows = gate_weight[0]
    up_rows = up_weight[0]
    down_rows = down_weight[0]
    slot_count = experts * capacity
    contract_rows = (((1,), (1,)), ((), ()))
    full_hidden, full_router, full_gain = (
        lax.all_gather(hidden, "exp", axis=1, tiled=True),
        lax.all_gather(router_matrix, "exp", axis=1, tiled=True),
        lax.all_gather(norm_gain[None, :], "exp", axis=1, tiled=True),
    )
    expanded_hidden = full_hidden.astype(jnp.float32)
    inverse_root_mean = lax.rsqrt(jnp.mean(expanded_hidden * expanded_hidden, axis=-1) + epsilon)
    rescaled_rows = expanded_hidden * full_gain.astype(jnp.float32)
    normed = (rescaled_rows * inverse_root_mean[:, None]).astype(jnp.bfloat16)
    router_scores = inverse_root_mean[:, None] * jnp.dot(
        rescaled_rows, full_router.astype(jnp.float32).T, precision=lax.Precision.HIGHEST
    )
    picked_rows = jnp.where(filled[:, None] == 1, normed[token_lookup], jnp.zeros((), normed.dtype))
    received = lax.all_to_all(
        picked_rows.reshape(experts, capacity, normed.shape[1]),
        ("ctx", "rep"),
        split_axis=0,
        concat_axis=0,
        tiled=True,
    )
    slots_in = received.reshape(slot_count, received.shape[2])
    gate_proj = lax.dot_general(
        slots_in, gate_rows, contract_rows, preferred_element_type=jnp.float32
    )
    up_proj = lax.dot_general(slots_in, up_rows, contract_rows, preferred_element_type=jnp.float32)
    activation = (jax.nn.silu(gate_proj) * up_proj).astype(jnp.bfloat16)
    expert_out = jnp.dot(
        lax.all_gather(activation, "exp", axis=1, tiled=True),
        down_rows,
        preferred_element_type=jnp.float32,
    ).astype(jnp.bfloat16)
    returned = lax.all_to_all(
        expert_out.reshape(experts, capacity, width_slice),
        ("ctx", "rep"),
        split_axis=0,
        concat_axis=0,
        tiled=True,
    )
    returned_rows = returned.reshape(slot_count, width_slice)
    picked_logits = jnp.take_along_axis(router_scores, routes[0], axis=1)
    gates = jax.nn.sigmoid(picked_logits)
    route_weight = gates / jnp.sum(gates, axis=1, keepdims=True)
    values = returned_rows[place].reshape(seq_rows, top_routes, width_slice).astype(jnp.float32)
    routed = jnp.sum(route_weight[..., None] * values, axis=1).astype(jnp.bfloat16)
    return (hidden[None], routed[None])


def solution(mesh):
    placed = (
        P("rep", "ctx", "exp", None),
        P("rep", "ctx", None),
        P("rep", "ctx", "exp"),
        P("exp", None, None),
        P("exp", None, None),
        P("exp", None, None),
        P("exp"),
        P(None, "exp"),
        P("rep", "ctx", None),
        P(("ctx", "rep"), "exp", None),
        P(("ctx", "rep"), "exp", None),
        P(("ctx", "rep"), None, "exp"),
    )
    return jax.shard_map(
        body,
        mesh=mesh,
        in_specs=placed,
        out_specs=(P("rep", "ctx", "exp"), P("rep", "ctx", "exp")),
        check_vma=False,
    )
```

profile of v0, /device:TPU:7, one launch (start us, length us, event | category | flops | bytes accessed | tf_op | source)
XLA Modules:
  0.0 626.6 jit_solution(8626739550930851257)
XLA Ops:
  7.2 0.7 all-gather.5.cloned.1.call-update
  8.0 0.8 copy.39
  9.0 0.7 reshape.434
  9.7 18.2 %all-gather.1 = bf16[8,1,256]{2,1,0:T(2,128)(2,1)S(1)} all-gather(bf16[1,1,256]{2,1,0:T(2,128)(2,1)S(1)} %reshape.434), channel_id=2, replica_groups=mesh['ctx'=32,'exp'=8,'rep'=2] {'exp'}, dimensions={0}, use_global_device_ids=true | all-gather | bytes 4608 | tf_op jit(solution)/shard_map/all_gather | solution.py:104
  27.9 0.7 broadcast_multiply_fusion
  28.9 0.7 dynamic-slice_bitcast_fusion
  29.7 2.0 fusion.18
  32.4 103.4 %all-gather.5.cloned.1.call-done = bf16[1,4096,512]{2,1,0:T(8,128)(2,1)} async-done(((bf16[1,128,512]{2,1,0:T(8,128)(2,1)}), bf16[1,4096,512]{2,1,0:T(8,128)(2,1)}) %all-gather.5.cloned.1.call-update) | async-done | bytes 4194320 | tf_op jit(solution)/shard_map/all_gather | solution.py:40
  135.8 5.3 conditional.1
  135.8 3.6 fusion.55
  139.4 0.9 fusion.7
  140.3 0.7 fusion.6
  141.1 1.3 fusion.16
  142.5 1.8 reduce-window.6
  144.7 3.4 scatter_custom_fusion.1
  148.1 3.4 scatter_custom_fusion
  151.6 90.3 %reduce-scatter.2.cloned.1.call-done = bf16[256,128]{0,1:T(8,128)(2,1)} async-done(((bf16[2048,128]{0,1:T(8,128)(2,1)}), bf16[256,128]{0,1:T(8,128)(2,1)}) %reduce-scatter.2.cloned.1.call-update) | async-done | bytes 65552 | tf_op jit(solution)/shard_map/reduce_scatter | solution.py:78
  241.9 0.9 fusion.34
  242.8 29.2 %all_gather.16 = bf16[128,2048]{1,0:T(8,128)(2,1)S(1)} all-gather(bf16[128,256]{1,0:T(8,128)(2,1)S(1)} %fusion.34), channel_id=1, replica_groups=mesh['ctx'=32,'exp'=8,'rep'=2] {'exp'}, dimensions={1}, use_global_device_ids=true | all-gather | bytes 589824 | tf_op jit(solution)/shard_map/all_gather | solution.py:102
  272.4 6.0 gather_fusion
  278.5 2.5 broadcast_select_fusion
  281.0 211.8 %all_to_all.10 = bf16[64,16,2048]{2,1,0:T(8,128)(2,1)S(1)} all-to-all(bf16[64,16,2048]{2,1,0:T(8,128)(2,1)S(1)} %broadcast_select_fusion), channel_id=1, replica_groups=mesh['ctx'=32,'exp'=8,'rep'=2] {'ctx','rep'}, dimensions={0} | all-to-all | bytes 8388608 | tf_op jit(solution)/shard_map/all_to_all | solution.py:114
  492.8 1.5 fusion.27
  494.4 2.3 fusion.21
  496.8 64.4 %all-gather.7.cloned.1.call-done = bf16[1024,1408]{0,1:T(8,128)(2,1)} async-done(((bf16[1024,176]{0,1:T(8,128)(2,1)}), bf16[1024,1408]{0,1:T(8,128)(2,1)}) %all-gather.7.cloned.1.call-update) | async-done | bytes 2883600 | tf_op jit(solution)/shard_map/all_gather | solution.py:128
  561.2 3.7 convolution_convert_fusion.1
  564.8 14.9 %all-to-all-start.1 = ((bf16[64,16,256]{2,1,0:T(8,128)(2,1)}), bf16[64,16,256]{2,1,0:T(8,128)(2,1)S(1)}, u32[]{:S(2)}, u32[]{:S(2)}) async-start(bf16[64,16,256]{2,1,0:T(8,128)(2,1)} %bitcast.24), calls=%async_computation.2 | async-start | bytes 1048576 | tf_op jit(solution)/shard_map/all_to_all | solution.py:132
  580.0 29.9 %all_gather.18 = bf16[64,2048]{1,0:T(8,128)(2,1)S(1)} all-gather(bf16[64,256]{1,0:T(8,128)(2,1)S(1)} %copy-done.7), channel_id=1, replica_groups=mesh['ctx'=32,'exp'=8,'rep'=2] {'exp'}, dimensions={1}, use_global_device_ids=true | all-gather | bytes 294912 | tf_op jit(solution)/shard_map/all_gather | solution.py:103
  610.0 0.8 fusion.22
  610.7 5.1 gather_fusion.2
  616.3 2.7 gather_fusion.1
  619.0 1.0 multiply_reduce_fusion
  (59 shorter events, 2.6 us)
Async XLA Ops:
  7.2 554.0 %copy-start = (bf16[1,1408,256]{2,1,0:T(8,128)(2,1)S(1)}, bf16[1,1408,256]{2,1,0:T(8,128)(2,1)}, u32[]{:S(2)}) copy-start(bf16[1,1408,256]{2,1,0:T(8,128)(2,1)} %param.25) | copy-start | bytes 2162692
  7.2 128.6 %all-gather.5.cloned.1.call-start = ((), (), s32[]{:S(2)}) async-start(), calls=%async_computation.3 | async-start | bytes 4325376 | tf_op jit(solution)/shard_map/all_gather | solution.py:40
  7.9 234.0 %reduce-scatter.2.cloned.1.call-start = ((), (), s32[]{:S(2)}) async-start(), calls=%async_computation.4 | async-start | bytes 589824 | tf_op jit(solution)/shard_map/reduce_scatter | solution.py:78
  135.8 5.3 copy-start.2
  135.8 5.3 copy-start.4
  135.8 3.6 copy-start.1
  141.1 100.9 %copy-start.6 = (bf16[1,128,256]{2,1,0:T(8,128)(2,1)S(1)}, bf16[1,128,256]{2,1,0:T(8,128)(2,1)}, u32[]{:S(2)}) copy-start(bf16[1,128,256]{2,1,0:T(8,128)(2,1)} %param.16) | copy-start | bytes 196612
  142.4 418.8 %all-gather.7.cloned.1.call-start = ((), (), s32[]{:S(2)}) async-start(), calls=%async_computation.5 | async-start | bytes 3244032 | tf_op jit(solution)/shard_map/all_gather | solution.py:128
  242.8 35.7 %copy-start.3 = (bf16[128,256]{1,0:T(8,128)(2,1)}, bf16[128,256]{1,0:T(8,128)(2,1)S(1)}, u32[]{:S(2)}) copy-start(bf16[128,256]{1,0:T(8,128)(2,1)S(1)} %fusion.34) | copy-start | bytes 196612
  281.0 211.8 %copy-start.8 = (bf16[1,176,2048]{2,1,0:T(8,128)(2,1)S(1)}, bf16[1,176,2048]{2,1,0:T(8,128)(2,1)}, u32[]{:S(2)}) copy-start(bf16[1,176,2048]{2,1,0:T(8,128)(2,1)} %param.23) | copy-start | bytes 2162692
  492.8 1.6 copy-start.9
  496.7 83.0 %copy-start.5 = (s32[1,128,6]{1,0,2:T(1,128)S(1)}, s32[1,128,6]{1,0,2:T(1,128)}, u32[]{:S(2)}) copy-start(s32[1,128,6]{1,0,2:T(1,128)} %param.22) | copy-start | bytes 9220
  496.7 83.3 %copy-start.7 = (bf16[64,256]{1,0:T(8,128)(2,1)S(1)}, bf16[64,256]{1,0:T(8,128)(2,1)}, u32[]{:S(2)}) copy-start(bf16[64,256]{1,0:T(8,128)(2,1)} %param.21) | copy-start | bytes 98308
  564.8 51.5 %all-to-all-start.1 = ((bf16[64,16,256]{2,1,0:T(8,128)(2,1)}), bf16[64,16,256]{2,1,0:T(8,128)(2,1)S(1)}, u32[]{:S(2)}, u32[]{:S(2)}) async-start(bf16[64,16,256]{2,1,0:T(8,128)(2,1)} %bitcast.24), calls=%async_computation.2 | async-start | bytes 1048576 | tf_op jit(solution)/shard_map/all_to_all | solution.py:132
Sparse Core Ops, SparseCore 0:
  10.1 125.6 all-gather.4
  142.5 99.3 reduce-scatter.1
  496.9 64.2 all-gather.6
where the time goes:
time: 632 us; the launch traced here: 627 us
  blocking collectives  289 us (46%)
  waiting for transfers between devices  259 us (41%)
  local copies, waits for them, and re-layouts  24.3 us (4%)
  starting transfers between devices  15 us (2%)
  between operations  14.7 us (2%)
  matrix products  14.1 us (2%)
  other arithmetic  10.5 us (2%)
    all_to_all x1, blocking collectives, body(): lax.all_to_all(picked_rows.reshape(experts, capacity, normed.shape[1]), (...  212 us
    all_gather x1, waiting for transfers between devices, body(): key_rows = lax.all_gather(latents, 'ctx', axis=1, tiled=True)[0]  103 us
    reduce_scatter x1, waiting for transfers between devices, body(): lax.psum_scatter(jnp.einsum('hsv,hvc->cs', head_values, out_weight, prefe...  90.3 us
    all_gather x1, waiting for transfers between devices, body(): lax.all_gather(activation, 'exp', axis=1, tiled=True)  64.4 us
    all_gather x1, blocking collectives, body(): lax.all_gather(router_matrix, 'exp', axis=1, tiled=True)  29.9 us
    all_gather x1, blocking collectives, body(): lax.all_gather(hidden, 'exp', axis=1, tiled=True)  29.2 us
    all_gather x1, blocking collectives, body(): lax.all_gather(norm_gain[None, :], 'exp', axis=1, tiled=True)  18.2 us
    all_to_all x1, starting transfers between devices, body(): lax.all_to_all(expert_out.reshape(experts, capacity, width_slice), ('ctx'...  14.9 us
  transfers between devices with their start and end apart: 4, of which 3 were waited for; matrix products, arithmetic and copies ran while one was open for 3% of the time, Pallas kernels for 0%

commit v1 on v0

v1 whole, which is shorter than its diff:
```python
import jax
import jax.numpy as jnp
from jax import lax
from jax.experimental import pallas as pl
from jax.experimental.pallas import tpu as pltpu
from jax.sharding import Mesh, PartitionSpec as P

score_scale = 192.0 ** (-0.5)
epsilon = 1e-06
never = 1 << 20

f32 = jnp.float32
bf16 = jnp.bfloat16

in_vmem = pl.BlockSpec(memory_space=pltpu.VMEM)
in_smem = pl.BlockSpec(memory_space=pltpu.SMEM)


def iota(shape, dim):
    return lax.broadcasted_iota(jnp.int32, shape, dim)


def dot(a, b, ca, cb, **kw):
    return lax.dot_general(a, b, (((ca,), (cb,)), ((), ())), preferred_element_type=f32, **kw)


def call(kernel, outs, *operands, specs=None, scratch=(), limit=24):
    many = isinstance(outs, list)
    return pl.pallas_call(
        kernel,
        out_shape=outs,
        in_specs=specs or [in_vmem] * len(operands),
        out_specs=[in_vmem] * len(outs) if many else in_vmem,
        scratch_shapes=list(scratch),
        compiler_params=pltpu.CompilerParams(vmem_limit_bytes=limit << 20),
    )(*operands)


def membership(routes, experts):
    lane = iota((routes.shape[0], experts), 1)
    member = routes[:, 0:1] == lane
    for k in range(1, routes.shape[1]):
        member = member | (routes[:, k : k + 1] == lane)
    return member


def repeat_matrix(experts, capacity):
    wide = (experts, experts * capacity)
    return (iota(wide, 1) // capacity == iota(wide, 0)).astype(f32).astype(bf16)


def place_kernel(experts, capacity, routes_ref, place_ref):
    rows = routes_ref.shape[0]
    member = membership(routes_ref[...], experts)
    earlier = (iota((rows, rows), 1) < iota((rows, rows), 0)).astype(f32).astype(bf16)
    count = dot(earlier, member.astype(f32).astype(bf16), 1, 0)
    code = jnp.where(member, count, -1.0).astype(bf16)
    spread = dot(code, repeat_matrix(experts, capacity), 1, 0)
    slot = iota((rows, experts * capacity), 1) % capacity
    place_ref[...] = (spread == slot.astype(f32)).astype(f32).astype(bf16)


def attend_kernel(rows, part_rows, at_ref, query_ref, key_ref, out_ref):
    own_block, own_part = at_ref[0], at_ref[1]
    heads = query_ref.shape[0]
    keys = key_ref[...]
    count = keys.shape[0]
    lane = iota((count, 128), 1)
    block = iota((count, 128), 0) // part_rows
    earlier = ((block == lane) & (lane < own_block)).astype(f32).astype(bf16)
    key_row = iota((count, 1), 0)
    is_own = key_row // part_rows == own_block
    own_pos = own_part * part_rows + key_row % part_rows
    query_pos = iota((count, rows), 1)
    for h in range(heads):
        chosen = dot(earlier, query_ref[h, rows : rows + 16, 256:384], 1, 1)[:, 0:1]
        first = jnp.where(is_own, own_pos, jnp.where(chosen > 0.5, -1, never))
        allowed = first <= query_pos
        scores = dot(keys, query_ref[h, 0:rows, :], 1, 1) * score_scale
        scores = jnp.where(allowed, scores, -1e30)
        top = jnp.max(scores, axis=0, keepdims=True)
        probs = jnp.where(allowed, jnp.exp(scores - top), 0.0)
        total = jnp.sum(probs, axis=0, keepdims=True)
        some = total > 0.0
        scale = jnp.where(some, 1.0 / jnp.where(some, total, 1.0), 0.0)
        low = (probs * scale).astype(bf16)
        out_ref[h, 0:rows, :] = dot(low, keys, 0, 0).astype(bf16)
        level = jnp.where(some, top + jnp.log(jnp.where(some, total, 1.0)), -1e30)
        high = level.astype(bf16).astype(f32)
        middle = (level - high).astype(bf16).astype(f32)
        rest = level - high - middle
        at = iota((16, rows), 0)
        stats = jnp.where(at == 0, high, jnp.where(at == 1, middle, jnp.where(at == 2, rest, 0.0)))
        out_ref[h, rows : rows + 16, 0:rows] = stats.astype(bf16)
        out_ref[h, rows : rows + 16, rows:] = jnp.zeros((16, keys.shape[1] - rows), bf16)


def project_kernel(rows, part_ref, uv_ref, out_weight_ref, out_ref):
    parts = part_ref.shape[0]
    levels = []
    for s in range(parts):
        stats = part_ref[s, rows : rows + 16, 0:rows].astype(f32)
        levels.append(stats[0:1] + stats[1:2] + stats[2:3])
    top = levels[0]
    for level in levels[1:]:
        top = jnp.maximum(top, level)
    shares = [jnp.exp(level - top) for level in levels]
    total = shares[0]
    for share in shares[1:]:
        total = total + share
    scale = 1.0 / total
    at = iota((rows, rows), 0)
    square = jnp.zeros((rows, rows), f32)
    for s in range(parts):
        square = jnp.where(at == s, shares[s] * scale, square)
    columns = square.T
    latent = columns[:, 0:1] * part_ref[0, 0:rows, :].astype(f32)
    for s in range(1, parts):
        latent = latent + columns[:, s : s + 1] * part_ref[s, 0:rows, :].astype(f32)
    values = dot(latent.astype(bf16), uv_ref[...], 1, 0).astype(bf16)
    width = out_ref.shape[2]
    for d in range(out_ref.shape[0]):
        out_ref[d] = dot(values, out_weight_ref[:, d * width : (d + 1) * width], 1, 0).astype(bf16)


def hidden_kernel(
    part_ref, token_ref, place_ref, router_ref, gain_ref, hidden_ref, rows_ref, logit_ref
):
    attention = part_ref[0].astype(f32)
    for s in range(1, part_ref.shape[0]):
        attention = attention + part_ref[s].astype(f32)
    hidden = (token_ref[...].astype(f32) + attention).astype(bf16)
    hidden_ref[...] = hidden
    rows_ref[...] = dot(place_ref[...], hidden, 0, 0).astype(bf16)
    wide = hidden.astype(f32)
    experts, width = router_ref.shape
    lanes = logit_ref.shape[1]
    router = jnp.concatenate(
        [router_ref[...].astype(f32), jnp.zeros((lanes - experts, width), f32)], axis=0
    )
    logits = dot(wide * gain_ref[...].astype(f32), router, 1, 1, precision=lax.Precision.HIGHEST)
    squares = jnp.sum(wide * wide, axis=1, keepdims=True)
    logit_ref[...] = jnp.where(iota(logits.shape, 1) < experts, logits, squares)


def gate_kernel(rows_ref, gain_ref, gate_ref, up_ref, out_ref, normed_ref):
    parts, count, width = rows_ref.shape
    squares = jnp.zeros((count, 1), f32)
    for s in range(parts):
        wide = rows_ref[s].astype(f32)
        squares = squares + jnp.sum(wide * wide, axis=1, keepdims=True)
    inverse = lax.rsqrt(squares / (parts * width) + epsilon)
    for s in range(parts):
        scaled = rows_ref[s].astype(f32) * gain_ref[s].astype(f32)
        normed_ref[:, s * width : (s + 1) * width] = (scaled * inverse).astype(bf16)
    units = gate_ref.shape[1]
    for j in range(gate_ref.shape[0]):
        gate = dot(gate_ref[j], normed_ref[...], 1, 1)
        up = dot(up_ref[j], normed_ref[...], 1, 1)
        out_ref[j * units : (j + 1) * units, :] = (gate / (1.0 + jnp.exp(-gate)) * up).astype(bf16)


def down_kernel(act_ref, down_ref, out_ref):
    act = act_ref[...]
    for j in range(down_ref.shape[0]):
        out_ref[j] = dot(act, down_ref[j], 0, 0).astype(bf16)


def combine_kernel(experts, capacity, features, logit_ref, routes_ref, place_ref, back_ref, out_ref):
    total = logit_ref[0]
    for s in range(1, logit_ref.shape[0]):
        total = total + logit_ref[s]
    inverse = lax.rsqrt(total[:, experts : experts + 1] / features + epsilon)
    gates = 1.0 / (1.0 + jnp.exp(-(inverse * total[:, 0:experts])))
    gates = jnp.where(membership(routes_ref[...], experts), gates, 0.0)
    weight = gates / jnp.sum(gates, axis=1, keepdims=True)
    high = weight.astype(bf16)
    low = (weight - high.astype(f32)).astype(bf16)
    spread = repeat_matrix(experts, capacity)
    place = place_ref[...].astype(f32)
    back = back_ref[...]
    first = dot((dot(high, spread, 1, 0) * place).astype(bf16), back, 1, 0)
    second = dot((dot(low, spread, 1, 0) * place).astype(bf16), back, 1, 0)
    out_ref[...] = (first + second).astype(bf16)


def shape(*dims, dtype=bf16):
    return jax.ShapeDtypeStruct(dims, dtype)


def swap(x, axes):
    return lax.all_to_all(x, axes, split_axis=0, concat_axis=0, tiled=True)


def copies(x, n):
    return jnp.broadcast_to(x[None], (n,) + x.shape)


CTX, EXP = ("z", "xl"), ("xh", "y")


def body(
    queries,
    latents,
    tokens,
    block_mask,
    uv_weight,
    out_weight,
    norm_gain,
    router_matrix,
    routes,
    gate_weight,
    up_weight,
    down_weight,
):
    rows, latent_width = queries.shape[1], queries.shape[3]
    width = tokens.shape[2]
    experts = router_matrix.shape[0]
    capacity = 4 * rows * routes.shape[2] // (3 * experts)
    blocks = block_mask.shape[1]
    n_exp = lax.axis_size(EXP)
    n_y, n_xh = lax.axis_size("y"), lax.axis_size("xh")
    ctx_place, exp_place = lax.axis_index(CTX), lax.axis_index(EXP)
    part_rows = rows // n_exp
    features = width * n_exp
    slots = experts * capacity
    units = gate_weight.shape[1]

    mask_row = lax.dynamic_index_in_dim(block_mask[0], ctx_place, 0, keepdims=True)
    extra = jnp.concatenate(
        [
            norm_gain[None, :],
            mask_row.astype(bf16),
            jnp.zeros((1, latent_width - width - blocks), bf16),
        ],
        axis=1,
    )
    sent = jnp.concatenate([queries[0, :, 0, :], extra, jnp.zeros((15, latent_width), bf16)], axis=0)
    own_keys = lax.dynamic_slice_in_dim(latents[0], exp_place * part_rows, part_rows, 0)
    keys = swap(copies(own_keys, blocks), CTX).reshape(blocks * part_rows, latent_width)
    all_queries = swap(copies(sent, n_exp), EXP)

    gate_rows = lax.all_gather(gate_weight[0], "y")
    up_rows = lax.all_gather(up_weight[0], "y")
    down_rows = lax.all_gather(down_weight[0], "y")

    place = call(
        lambda *refs: place_kernel(experts, capacity, *refs), shape(rows, slots), routes[0]
    )
    partial = call(
        lambda *refs: attend_kernel(rows, part_rows, *refs),
        shape(n_exp, rows + 16, latent_width),
        jnp.stack([ctx_place, exp_place]).astype(jnp.int32),
        all_queries,
        keys,
        specs=[in_smem, in_vmem, in_vmem],
    )
    partial = swap(partial, EXP)
    terms = call(
        lambda *refs: project_kernel(rows, *refs),
        shape(n_exp, rows, width),
        partial,
        uv_weight[0],
        out_weight[0],
    )
    terms = swap(terms, EXP)
    hidden, picked, logits = call(
        hidden_kernel,
        [shape(rows, width), shape(slots, width), shape(rows, 128, dtype=f32)],
        terms,
        tokens[0],
        place,
        router_matrix,
        norm_gain[None, :],
    )
    received = swap(picked.reshape(experts, capacity, width), CTX + ("rep",))
    logits = swap(copies(logits, n_exp), EXP)
    groups = received.reshape(1, n_y, slots // n_y, width)
    groups = jnp.broadcast_to(groups, (n_xh,) + groups.shape[1:]).reshape(n_exp, -1, width)
    full_rows = swap(groups, EXP)
    gains = all_queries[:, rows : rows + 1, 0:width]
    count = slots // n_y
    act = call(
        gate_kernel,
        shape(n_y * units, count),
        full_rows,
        gains,
        gate_rows,
        up_rows,
        scratch=[pltpu.VMEM((count, features), bf16)],
    )
    act = swap(copies(act, n_xh), "xh").reshape(n_exp * units, count)
    out = call(down_kernel, shape(n_y, count, width), act, down_rows)
    out = swap(out, "y")
    back = swap(out.reshape(experts, capacity, width), CTX + ("rep",)).reshape(slots, width)
    routed = call(
        lambda *refs: combine_kernel(experts, capacity, features, *refs),
        shape(rows, width),
        logits,
        routes[0],
        place,
        back,
    )
    return (hidden[None], routed[None])


def solution(mesh):
    sizes = mesh.shape
    fine = Mesh(
        mesh.devices.reshape(sizes["ctx"] // 2, 2, 2, sizes["exp"] // 2, sizes["rep"]),
        ("z", "xl", "xh", "y", "rep"),
    )
    placed = (
        P("rep", CTX, EXP, None),
        P("rep", CTX, None),
        P("rep", CTX, EXP),
        P(EXP, None, None),
        P(EXP, None, None),
        P(EXP, None, None),
        P(EXP),
        P(None, EXP),
        P("rep", CTX, None),
        P(CTX + ("rep",), EXP, None),
        P(CTX + ("rep",), EXP, None),
        P(CTX + ("rep",), None, EXP),
    )
    return jax.shard_map(
        body,
        mesh=fine,
        in_specs=placed,
        out_specs=(P("rep", CTX, EXP), P("rep", CTX, EXP)),
        check_vma=False,
    )
```

time: 632 us -> 289 us (0.46)
  blocking collectives: 289 us -> 105 us
  waiting for transfers between devices: 259 us -> 91.3 us
  starting transfers between devices: 15 us -> 50.2 us
  Pallas kernels: 0 us -> 15.3 us
  matrix products: 14.1 us -> 0 us
  local copies, waits for them, and re-layouts: 24.3 us -> 10.6 us
  other arithmetic: 10.5 us -> 0.86 us
    all_gather x2 -> x3, waiting for transfers between devices: 168 us -> 0.04 us  [the longest x1 0.02 us: body(): gate_rows = lax.all_gather(gate_weight[0], 'y')]
    all_to_all x1 -> x4, blocking collectives: 212 us -> 105 us  [swap(): return lax.all_to_all(x, axes, split_axis=0, concat_axis=0, tiled=True)]
    reduce_scatter x1 -> x0, waiting for transfers between devices: 90.3 us -> none  [body(): lax.psum_scatter(jnp.einsum('hsv,hvc->cs', head_values, out_weight, prefe...]
    all_to_all x1 -> x6, waiting for transfers between devices: 0.01 us -> 89.2 us  [swap(): return lax.all_to_all(x, axes, split_axis=0, concat_axis=0, tiled=True)]
    all_gather x3 -> x0, blocking collectives: 77.3 us -> none  [the longest x1 29.9 us: body(): lax.all_gather(router_matrix, 'exp', axis=1, tiled=True)]
    all_to_all x1 -> x6, starting transfers between devices: 14.9 us -> 50.1 us  [swap(): return lax.all_to_all(x, axes, split_axis=0, concat_axis=0, tiled=True)]
    pallas_call x0 -> x7, Pallas kernels: none -> 15.3 us  [call(): pl.pallas_call(kernel, out_shape=outs, in_specs=specs or [in_vmem] * len(...]
    gather x7 -> x0, local copies, waits for them, and re-layouts: 14.2 us -> none  [the longest x1 6.02 us: body(): normed[token_lookup]]
  transfers between devices with their start and end apart: 4 -> 9, of which waited for: 3 -> 6; matrix products, arithmetic and copies ran while one was open for 3% -> 2% of each run, Pallas kernels for 0% -> 5%
where the time goes in v1:
time: 289 us; the launch traced here: 287 us
  blocking collectives  105 us (36%)
  waiting for transfers between devices  91.3 us (32%)
  starting transfers between devices  50.2 us (17%)
  Pallas kernels  15.3 us (5%)
  between operations  13.9 us (5%)
  local copies, waits for them, and re-layouts  10.6 us (4%)
    all_to_all x4, blocking collectives, swap(): return lax.all_to_all(x, axes, split_axis=0, concat_axis=0, tiled=True)  105 us
    all_to_all x6, waiting for transfers between devices, swap(): return lax.all_to_all(x, axes, split_axis=0, concat_axis=0, tiled=True)  89.2 us
    all_to_all x6, starting transfers between devices, swap(): return lax.all_to_all(x, axes, split_axis=0, concat_axis=0, tiled=True)  50.1 us
    pallas_call x7, Pallas kernels, call(): pl.pallas_call(kernel, out_shape=outs, in_specs=specs or [in_vmem] * len(...  15.3 us
    unnamed x25, local copies, waits for them, and re-layouts  6.58 us
  transfers between devices with their start and end apart: 9, of which 6 were waited for; matrix products, arithmetic and copies ran while one was open for 2% of the time, Pallas kernels for 5%

profile of v1, /device:TPU:7, one launch (start us, length us, event | category | flops | bytes accessed | tf_op | source)
XLA Modules:
  0.0 286.9 jit_solution(13638397009411372985)
XLA Ops:
  8.0 0.7 all-gather.6.cloned.1.call-update
  9.6 1.1 broadcast_in_dim.52
  10.7 6.9 %all-to-all-start = ((bf16[8,144,512]{2,1,0:T(8,128)(2,1)}), bf16[8,144,512]{2,1,0:T(8,128)(2,1)S(1)}, u32[]{:S(2)}, u32[]{:S(2)}) async-start(bf16[8,144,512]{2,1,0:T(8,128)(2,1)} %broadcast_in_dim.52), calls=%async_computation | async-start | bytes 2359296 | tf_op jit(solution)/shard_map/all_to_all | solution.py:192
  17.6 16.0 %all-to-all-done.refs_1_ = bf16[8,144,512]{2,1,0:T(8,128)(2,1)S(1)} async-done(((bf16[8,144,512]{2,1,0:T(8,128)(2,1)}), bf16[8,144,512]{2,1,0:T(8,128)(2,1)S(1)}, u32[]{:S(2)}, u32[]{:S(2)}) %all-to-all-start) | async-done | bytes 1179680 | tf_op jit(solution)/shard_map/all_to_all | solution.py:192
  33.6 0.9 broadcast_in_dim.54
  34.5 16.2 %all-to-all-start.1 = ((bf16[32,16,512]{2,1,0:T(8,128)(2,1)}), bf16[32,16,512]{2,1,0:T(8,128)(2,1)S(1)}, u32[]{:S(2)}, u32[]{:S(2)}) async-start(bf16[32,16,512]{2,1,0:T(8,128)(2,1)} %broadcast_in_dim.54), calls=%async_computation.1 | async-start | bytes 1048576 | tf_op jit(solution)/shard_map/all_to_all | solution.py:192
  50.8 29.2 %all-to-all-done.1 = bf16[32,16,512]{2,1,0:T(8,128)(2,1)S(1)} async-done(((bf16[32,16,512]{2,1,0:T(8,128)(2,1)}), bf16[32,16,512]{2,1,0:T(8,128)(2,1)S(1)}, u32[]{:S(2)}, u32[]{:S(2)}) %all-to-all-start.1) | async-done | bytes 524320 | tf_op jit(solution)/shard_map/all_to_all | solution.py:192
  80.0 6.6 %shard_map.131 = bf16[8,144,512]{2,1,0:T(8,128)(2,1)S(1)} custom-call(s32[2]{0:T(128)S(1)} %pad_add_fusion.refs_0_, bf16[8,144,512]{2,1,0:T(8,128)(2,1)S(1)} %all-to-all-done.refs_1_, bf16[512,512]{1,0:T(8,128)(2,1)S(1)} %bitcast.21), custom_call_target="tpu_custom_call" | custom-call | tf_op jit(solution)/shard_map/pallas_call | solution.py:29
  86.7 1.0 copy-done.1
  87.7 6.7 %all-to-all-start.2 = ((bf16[8,144,512]{2,1,0:T(8,128)(2,1)}), bf16[8,144,512]{2,1,0:T(8,128)(2,1)S(1)}, u32[]{:S(2)}, u32[]{:S(2)}) async-start(bf16[8,144,512]{2,1,0:T(8,128)(2,1)} %copy-done.1), calls=%async_computation.2 | async-start | bytes 2359296 | tf_op jit(solution)/shard_map/all_to_all | solution.py:192
  94.4 0.7 all-gather.8.cloned.1.call-update
  95.1 18.5 %all-to-all-done.2.refs_0_ = bf16[8,144,512]{2,1,0:T(8,128)(2,1)S(1)} async-done(((bf16[8,144,512]{2,1,0:T(8,128)(2,1)}), bf16[8,144,512]{2,1,0:T(8,128)(2,1)S(1)}, u32[]{:S(2)}, u32[]{:S(2)}) %all-to-all-start.2) | async-done | bytes 1179680 | tf_op jit(solution)/shard_map/all_to_all | solution.py:192
  113.6 1.6 shard_map.132
  115.2 8.4 %all-to-all-start.3 = ((bf16[8,128,256]{2,1,0:T(8,128)(2,1)}), bf16[8,128,256]{2,1,0:T(8,128)(2,1)S(1)}, u32[]{:S(2)}, u32[]{:S(2)}) async-start(bf16[8,128,256]{2,1,0:T(8,128)(2,1)} %shard_map.132), calls=%async_computation.3 | async-start | bytes 1048576 | tf_op jit(solution)/shard_map/all_to_all | solution.py:192
  124.4 6.6 %all-to-all-done.3.part_ref = bf16[8,128,256]{2,1,0:T(8,128)(2,1)S(1)} async-done(((bf16[8,128,256]{2,1,0:T(8,128)(2,1)}), bf16[8,128,256]{2,1,0:T(8,128)(2,1)S(1)}, u32[]{:S(2)}, u32[]{:S(2)}) %all-to-all-start.3) | async-done | bytes 524320 | tf_op jit(solution)/shard_map/all_to_all | solution.py:192
  131.0 0.7 shard_map.134
  131.7 41.3 %all_to_all.50 = bf16[64,16,256]{2,1,0:T(8,128)(2,1)S(1)} all-to-all(bf16[64,16,256]{2,1,0:T(8,128)(2,1)S(1)} %bitcast.25), channel_id=1, replica_groups=mesh['z'=16,'xl'=2,'xh'=2,'y'=4,'rep'=2] {'z','xl','rep'}, dimensions={0} | all-to-all | bytes 1048576 | tf_op jit(solution)/shard_map/all_to_all | solution.py:192
  173.0 1.0 broadcast_in_dim.58
  174.0 5.8 %all-to-all-start.6 = ((bf16[8,256,256]{2,1,0:T(8,128)(2,1)}), bf16[8,256,256]{2,1,0:T(8,128)(2,1)S(1)}, u32[]{:S(2)}, u32[]{:S(2)}) async-start(bf16[8,256,256]{2,1,0:T(8,128)(2,1)} %bitcast.29), calls=%async_computation.6 | async-start | bytes 2097152 | tf_op jit(solution)/shard_map/all_to_all | solution.py:192
  179.9 14.6 %all-to-all-done.6.rows_ref = bf16[8,256,256]{2,1,0:T(8,128)(2,1)S(1)} async-done(((bf16[8,256,256]{2,1,0:T(8,128)(2,1)}), bf16[8,256,256]{2,1,0:T(8,128)(2,1)S(1)}, u32[]{:S(2)}, u32[]{:S(2)}) %all-to-all-start.6) | async-done | bytes 1048608 | tf_op jit(solution)/shard_map/all_to_all | solution.py:192
  194.5 1.8 copy-done.2
  196.3 1.8 copy-done.3
  198.1 3.2 %shard_map.135 = bf16[704,256]{1,0:T(8,128)(2,1)S(1)} custom-call(bf16[8,256,256]{2,1,0:T(8,128)(2,1)S(1)} %all-to-all-done.6.rows_ref, bf16[8,1,256]{2,1,0:T(2,128)(2,1)S(1)} %slice.4.gain_ref, bf16[4,176,2048]{2,1,0:T(8,128)(2,1)S(1)} %copy-done.2, bf16[4,176,2048]{2,1,0:T(8,128)(2,1)S(1)} %copy-done.3), custom_call_target="tpu_custom_call" | custom-call | tf_op jit(solution)/shard_map/pallas_call | solution.py:29
  201.3 11.9 %all_to_all.51 = bf16[2,704,256]{2,1,0:T(8,128)(2,1)S(1)} all-to-all(bf16[2,704,256]{2,1,0:T(8,128)(2,1)S(1)} %broadcast_in_dim.59), channel_id=1, replica_groups=mesh['z'=16,'xl'=2,'xh'=2,'y'=4,'rep'=2] {'xh'}, dimensions={0} | all-to-all | bytes 1441792 | tf_op jit(solution)/shard_map/all_to_all | solution.py:192
  213.2 0.8 broadcast_in_dim.56
  214.0 6.1 %all-to-all-start.4 = ((f32[8,128,128]{2,1,0:T(8,128)}), f32[8,128,128]{2,1,0:T(8,128)S(1)}, u32[]{:S(2)}, u32[]{:S(2)}) async-start(f32[8,128,128]{2,1,0:T(8,128)} %broadcast_in_dim.56), calls=%async_computation.4 | async-start | bytes 1048576 | tf_op jit(solution)/shard_map/all_to_all | solution.py:192
  220.1 1.8 copy-done.4
  221.9 1.0 shard_map.136
  222.9 4.2 %all-to-all-done.4.refs_0_ = f32[8,128,128]{2,1,0:T(8,128)S(1)} async-done(((f32[8,128,128]{2,1,0:T(8,128)}), f32[8,128,128]{2,1,0:T(8,128)S(1)}, u32[]{:S(2)}, u32[]{:S(2)}) %all-to-all-start.4) | async-done | bytes 524320 | tf_op jit(solution)/shard_map/all_to_all | solution.py:192
  227.2 11.3 %all_to_all.52 = bf16[4,256,256]{2,1,0:T(8,128)(2,1)S(1)} all-to-all(bf16[4,256,256]{2,1,0:T(8,128)(2,1)S(1)} %shard_map.136), channel_id=1, replica_groups=mesh['z'=16,'xl'=2,'xh'=2,'y'=4,'rep'=2] {'y'}, dimensions={0} | all-to-all | bytes 1048576 | tf_op jit(solution)/shard_map/all_to_all | solution.py:192
  238.5 40.3 %all_to_all.53 = bf16[64,16,256]{2,1,0:T(8,128)(2,1)S(1)} all-to-all(bf16[64,16,256]{2,1,0:T(8,128)(2,1)S(1)} %bitcast.31), channel_id=1, replica_groups=mesh['z'=16,'xl'=2,'xh'=2,'y'=4,'rep'=2] {'z','xl','rep'}, dimensions={0} | all-to-all | bytes 1048576 | tf_op jit(solution)/shard_map/all_to_all | solution.py:192
  278.8 1.6 shard_map.137
  (39 shorter events, 2.5 us)
Async XLA Ops:
  7.2 10.4 %copy-start = (bf16[1,128,512]{2,1,0:T(8,128)(2,1)S(1)}, bf16[1,128,512]{2,1,0:T(8,128)(2,1)}, u32[]{:S(2)}) copy-start(bf16[1,128,512]{2,1,0:T(8,128)(2,1)} %param.13) | copy-start | bytes 393220
  7.2 1.5 copy-start.11
  7.2 2.3 copy-start.9
  7.2 172.6 %all-gather.4.cloned.1.call-start = ((), (), s32[]{:S(2)}) async-start(), calls=%async_computation.10 | async-start | bytes 3604480 | tf_op jit(solution)/shard_map/all_gather | solution.py:243
  7.9 171.9 %all-gather.6.cloned.1.call-start = ((), (), s32[]{:S(2)}) async-start(), calls=%async_computation.11 | async-start | bytes 3604480 | tf_op jit(solution)/shard_map/all_gather | solution.py:244
  10.7 22.9 %all-to-all-start = ((bf16[8,144,512]{2,1,0:T(8,128)(2,1)}), bf16[8,144,512]{2,1,0:T(8,128)(2,1)S(1)}, u32[]{:S(2)}, u32[]{:S(2)}) async-start(bf16[8,144,512]{2,1,0:T(8,128)(2,1)} %broadcast_in_dim.52), calls=%async_computation | async-start | bytes 2359296 | tf_op jit(solution)/shard_map/all_to_all | solution.py:192
  34.5 45.5 %all-to-all-start.1 = ((bf16[32,16,512]{2,1,0:T(8,128)(2,1)}), bf16[32,16,512]{2,1,0:T(8,128)(2,1)S(1)}, u32[]{:S(2)}, u32[]{:S(2)}) async-start(bf16[32,16,512]{2,1,0:T(8,128)(2,1)} %broadcast_in_dim.54), calls=%async_computation.1 | async-start | bytes 1048576 | tf_op jit(solution)/shard_map/all_to_all | solution.py:192
  86.7 1.0 copy-start.1
  87.7 25.9 %copy-start.5 = (bf16[1,128,2048]{2,1,0:T(8,128)(2,1)S(1)}, bf16[1,128,2048]{2,1,0:T(8,128)(2,1)}, u32[]{:S(2)}) copy-start(bf16[1,128,2048]{2,1,0:T(8,128)(2,1)} %param.17) | copy-start | bytes 1572868
  87.7 25.9 %copy-start.6 = (bf16[1,512,128]{2,1,0:T(8,128)(2,1)S(1)}, bf16[1,512,128]{2,1,0:T(8,128)(2,1)}, u32[]{:S(2)}) copy-start(bf16[1,512,128]{2,1,0:T(8,128)(2,1)} %param.16) | copy-start | bytes 393220
  87.7 25.9 %all-to-all-start.2 = ((bf16[8,144,512]{2,1,0:T(8,128)(2,1)}), bf16[8,144,512]{2,1,0:T(8,128)(2,1)S(1)}, u32[]{:S(2)}, u32[]{:S(2)}) async-start(bf16[8,144,512]{2,1,0:T(8,128)(2,1)} %copy-done.1), calls=%async_computation.2 | async-start | bytes 2359296 | tf_op jit(solution)/shard_map/all_to_all | solution.py:192
  94.4 125.7 %all-gather.8.cloned.1.call-start = ((), (), s32[]{:S(2)}) async-start(), calls=%async_computation.12 | async-start | bytes 3604480 | tf_op jit(solution)/shard_map/all_gather | solution.py:245
  113.6 10.1 %copy-start.10 = (s32[1,128,6]{1,0,2:T(1,128)S(1)}, s32[1,128,6]{1,0,2:T(1,128)}, u32[]{:S(2)}) copy-start(s32[1,128,6]{1,0,2:T(1,128)} %param.20) | copy-start | bytes 9220
  115.2 15.7 %copy-start.7 = (bf16[1,128,256]{2,1,0:T(8,128)(2,1)S(1)}, bf16[1,128,256]{2,1,0:T(8,128)(2,1)}, u32[]{:S(2)}) copy-start(bf16[1,128,256]{2,1,0:T(8,128)(2,1)} %param.14) | copy-start | bytes 196612
  115.2 15.7 %copy-start.8 = (bf16[64,256]{1,0:T(8,128)(2,1)S(1)}, bf16[64,256]{1,0:T(8,128)(2,1)}, u32[]{:S(2)}) copy-start(bf16[64,256]{1,0:T(8,128)(2,1)} %router_ref.1) | copy-start | bytes 98308
  115.2 15.7 %all-to-all-start.3 = ((bf16[8,128,256]{2,1,0:T(8,128)(2,1)}), bf16[8,128,256]{2,1,0:T(8,128)(2,1)S(1)}, u32[]{:S(2)}, u32[]{:S(2)}) async-start(bf16[8,128,256]{2,1,0:T(8,128)(2,1)} %shard_map.132), calls=%async_computation.3 | async-start | bytes 1048576 | tf_op jit(solution)/shard_map/all_to_all | solution.py:192
  174.0 20.4 %all-to-all-start.6 = ((bf16[8,256,256]{2,1,0:T(8,128)(2,1)}), bf16[8,256,256]{2,1,0:T(8,128)(2,1)S(1)}, u32[]{:S(2)}, u32[]{:S(2)}) async-start(bf16[8,256,256]{2,1,0:T(8,128)(2,1)} %bitcast.29), calls=%async_computation.6 | async-start | bytes 2097152 | tf_op jit(solution)/shard_map/all_to_all | solution.py:192
  194.4 1.8 copy-start.2
  196.3 1.8 copy-start.3
  214.0 13.1 %all-to-all-start.4 = ((f32[8,128,128]{2,1,0:T(8,128)}), f32[8,128,128]{2,1,0:T(8,128)S(1)}, u32[]{:S(2)}, u32[]{:S(2)}) async-start(f32[8,128,128]{2,1,0:T(8,128)} %broadcast_in_dim.56), calls=%async_computation.4 | async-start | bytes 1048576 | tf_op jit(solution)/shard_map/all_to_all | solution.py:192
  220.1 1.8 copy-start.4
Sparse Core Ops, SparseCore 0:
  10.1 49.4 all-gather.3
  61.7 58.0 all-gather.5
  122.0 49.2 all-gather.7

commit v2 on v1

v2 whole, which is shorter than its diff:
```python
import jax
import jax.numpy as jnp
from jax import lax
from jax.experimental import pallas as pl
from jax.experimental.pallas import tpu as pltpu
from jax.sharding import Mesh, PartitionSpec as P

score_scale = 192.0 ** (-0.5)
epsilon = 1e-06
never = 1 << 20

f32 = jnp.float32
bf16 = jnp.bfloat16

in_vmem = pl.BlockSpec(memory_space=pltpu.VMEM)
in_smem = pl.BlockSpec(memory_space=pltpu.SMEM)


def iota(shape, dim):
    return lax.broadcasted_iota(jnp.int32, shape, dim)


def dot(a, b, ca, cb, **kw):
    return lax.dot_general(a, b, (((ca,), (cb,)), ((), ())), preferred_element_type=f32, **kw)


def call(kernel, outs, *operands, specs=None, limit=24):
    many = isinstance(outs, list)
    return pl.pallas_call(
        kernel,
        out_shape=outs,
        in_specs=specs or [in_vmem] * len(operands),
        out_specs=[in_vmem] * len(outs) if many else in_vmem,
        compiler_params=pltpu.CompilerParams(vmem_limit_bytes=limit << 20),
    )(*operands)


def three_terms(x):
    high = x.astype(bf16).astype(f32)
    middle = (x - high).astype(bf16).astype(f32)
    return high, middle, x - high - middle


def repeat_matrix(experts, capacity):
    tall = (experts * capacity, experts)
    return (iota(tall, 0) // capacity == iota(tall, 1)).astype(f32).astype(bf16)


def place_kernel(experts, capacity, routes_ref, place_ref):
    top, rows = routes_ref.shape
    routes = routes_ref[...]
    expert = iota((experts, rows), 0)
    member = routes[0:1] == expert
    for k in range(1, top):
        member = member | (routes[k : k + 1] == expert)
    earlier = (iota((rows, rows), 0) < iota((rows, rows), 1)).astype(f32).astype(bf16)
    count = dot(member.astype(f32).astype(bf16), earlier, 1, 0)
    code = jnp.where(member, count, -1.0).astype(bf16)
    spread = dot(repeat_matrix(experts, capacity), code, 1, 0)
    slot = iota((experts * capacity, rows), 0) % capacity
    place_ref[...] = (spread == slot.astype(f32)).astype(f32).astype(bf16)


def attend_kernel(rows, part_rows, values, at_ref, key_ref, *refs):
    query_refs, out_ref, gain_ref = refs[:-2], refs[-2], refs[-1]
    own_block, own_part, own_half, own_y = at_ref[0], at_ref[1], at_ref[2], at_ref[3]
    heads = len(query_refs)
    keys = key_ref[...]
    count = keys.shape[0]
    lane = iota((count, 128), 1)
    block = iota((count, 128), 0) // part_rows
    earlier = ((block == lane) & (lane < own_block)).astype(f32).astype(bf16)
    key_row = iota((count, 1), 0)
    is_own = key_row // part_rows == own_block
    own_pos = own_part * part_rows + key_row % part_rows
    query_pos = iota((count, rows), 1)
    width = gain_ref.shape[2]
    extra = rows + values
    n_y = heads // 2
    for n, ref in enumerate(query_refs):
        half, shift = n // n_y, n % n_y
        head = (own_half ^ half) * n_y + (own_y + n_y - shift) % n_y
        chosen = dot(earlier, ref[extra : extra + 16, width : width + 128], 1, 1)[:, 0:1]
        first = jnp.where(is_own, own_pos, jnp.where(chosen > 0.5, -1, never))
        allowed = first <= query_pos
        scores = dot(keys, ref[0:rows, :], 1, 1) * score_scale
        scores = jnp.where(allowed, scores, -1e30)
        top = jnp.max(scores, axis=0, keepdims=True)
        probs = jnp.where(allowed, jnp.exp(scores - top), 0.0)
        total = jnp.sum(probs, axis=0, keepdims=True)
        some = total > 0.0
        scale = jnp.where(some, 1.0 / jnp.where(some, total, 1.0), 0.0)
        latent = dot((probs * scale).astype(bf16), keys, 0, 0).astype(bf16)
        out_ref[head, 0:rows, :] = dot(latent, ref[rows:extra, :], 1, 1).astype(bf16)
        level = jnp.where(some, top + jnp.log(jnp.where(some, total, 1.0)), -1e30)
        terms = three_terms(level)
        at = iota((16, rows), 0)
        stats = jnp.zeros((16, rows), f32)
        for k, term in enumerate(terms):
            stats = jnp.where(at == k, term, stats)
        out_ref[head, rows : rows + 16, :] = stats.astype(bf16)
        gain_ref[head] = ref[extra : extra + 16, 0:width]


def project_kernel(rows, part_ref, out_weight_ref, out_ref):
    parts = part_ref.shape[0]
    levels = []
    for s in range(parts):
        stats = part_ref[s, rows : rows + 16, :].astype(f32)
        levels.append(stats[0:1] + stats[1:2] + stats[2:3])
    top = levels[0]
    for level in levels[1:]:
        top = jnp.maximum(top, level)
    shares = [jnp.exp(level - top) for level in levels]
    total = shares[0]
    for share in shares[1:]:
        total = total + share
    scale = 1.0 / total
    at = iota((rows, rows), 0)
    square = jnp.zeros((rows, rows), f32)
    for s in range(parts):
        square = jnp.where(at == s, shares[s] * scale, square)
    columns = square.T
    values = columns[:, 0:1] * part_ref[0, 0:rows, :].astype(f32)
    for s in range(1, parts):
        values = values + columns[:, s : s + 1] * part_ref[s, 0:rows, :].astype(f32)
    values = values.astype(bf16)
    width = out_ref.shape[2]
    for d in range(out_ref.shape[0]):
        out_ref[d] = dot(values, out_weight_ref[:, d * width : (d + 1) * width], 1, 0).astype(bf16)


def hidden_kernel(
    part_ref, token_ref, place_ref, router_ref, gain_ref, routes_ref, hidden_ref, rows_ref, pick_ref
):
    attention = part_ref[0].astype(f32)
    for s in range(1, part_ref.shape[0]):
        attention = attention + part_ref[s].astype(f32)
    hidden = (token_ref[...].astype(f32) + attention).astype(bf16)
    hidden_ref[...] = hidden
    rows_ref[...] = dot(place_ref[...], hidden, 1, 0).astype(bf16)
    wide = hidden.astype(f32)
    exact = dict(precision=lax.Precision.HIGHEST)
    scaled = wide * gain_ref[...].astype(f32)
    logits = dot(router_ref[...].astype(f32), scaled, 1, 1, **exact)
    picks = dot(jnp.ones((8, wide.shape[1]), f32), wide * wide, 1, 1, **exact)
    routes = routes_ref[...]
    expert, at = iota(logits.shape, 0), iota(picks.shape, 0)
    for k in range(routes.shape[0]):
        pick = jnp.sum(jnp.where(routes[k : k + 1] == expert, logits, 0.0), axis=0, keepdims=True)
        picks = jnp.where(at == k, pick, picks)
    high, middle, rest = three_terms(picks)
    upper = jnp.concatenate([high, middle], axis=1)
    lower = jnp.concatenate([rest, jnp.zeros_like(rest)], axis=1)
    pick_ref[...] = jnp.concatenate([upper, lower], axis=0).astype(bf16)


def gate_kernel(rows_ref, gain_ref, gate_ref, up_ref, out_ref, normed_ref):
    parts, _, width = rows_ref.shape
    count = normed_ref.shape[0]

    @pl.when(pl.program_id(0) == 0)
    def _():
        squares = jnp.zeros((count, 1), f32)
        for s in range(parts):
            wide = rows_ref[s, 0:count, :].astype(f32)
            squares = squares + jnp.sum(wide * wide, axis=1, keepdims=True)
        inverse = lax.rsqrt(squares / (parts * width) + epsilon)
        for s in range(parts):
            scaled = rows_ref[s, 0:count, :].astype(f32) * gain_ref[s, 0:1, :].astype(f32)
            normed_ref[:, s * width : (s + 1) * width] = (scaled * inverse).astype(bf16)

    gate = dot(gate_ref[0], normed_ref[...], 1, 1)
    up = dot(up_ref[0], normed_ref[...], 1, 1)
    out_ref[...] = (gate / (1.0 + jnp.exp(-gate)) * up).astype(bf16)


def down_kernel(half_ref, act_ref, down_ref, out_ref):
    width = out_ref.shape[3]
    for k in range(2):
        down = down_ref[0, :, k * width : (k + 1) * width]
        out_ref[half_ref[0] ^ k, 0] = dot(act_ref[...], down, 0, 0).astype(bf16)


def combine_kernel(experts, capacity, features, row_ref, routes_ref, place_ref, back_ref, out_ref):
    rows = out_ref.shape[0]
    count = row_ref.shape[1] - 16
    total = jnp.zeros((8, rows), f32)
    for s in range(row_ref.shape[0]):
        terms = row_ref[s, count : count + 16, :].astype(f32)
        total = total + (terms[0:8, 0:rows] + terms[0:8, rows:] + terms[8:16, 0:rows])
    routes = routes_ref[...]
    top = routes.shape[0]
    inverse = lax.rsqrt(total[top : top + 1] / features + epsilon)
    gates = 1.0 / (1.0 + jnp.exp(-(inverse * total[0:top])))
    gates = gates / jnp.sum(gates, axis=0, keepdims=True)
    expert = iota((experts, rows), 0)
    weight = jnp.zeros((experts, rows), f32)
    for k in range(top):
        weight = jnp.where(routes[k : k + 1] == expert, gates[k : k + 1], weight)
    high = weight.astype(bf16)
    low = (weight - high.astype(f32)).astype(bf16)
    spread = repeat_matrix(experts, capacity)
    place = place_ref[...].astype(f32)
    back = back_ref[...]
    first = dot((dot(spread, high, 1, 0) * place).astype(bf16), back, 0, 0)
    second = dot((dot(spread, low, 1, 0) * place).astype(bf16), back, 0, 0)
    out_ref[...] = (first + second).astype(bf16)


def shape(*dims, dtype=bf16):
    return jax.ShapeDtypeStruct(dims, dtype)


def swap(x, axes):
    return lax.all_to_all(x, axes, split_axis=0, concat_axis=0, tiled=True)


def copies(x, n):
    return jnp.broadcast_to(x[None], (n,) + x.shape)


CTX, EXP = ("z", "xl"), ("xh", "y")


def body(
    queries,
    latents,
    tokens,
    block_mask,
    uv_weight,
    out_weight,
    norm_gain,
    router_matrix,
    routes,
    gate_weight,
    up_weight,
    down_weight,
):
    rows, latent_width = queries.shape[1], queries.shape[3]
    width = tokens.shape[2]
    experts = router_matrix.shape[0]
    capacity = 4 * rows * routes.shape[2] // (3 * experts)
    blocks = block_mask.shape[1]
    values = uv_weight.shape[2]
    n_exp = lax.axis_size(EXP)
    n_y, n_xh = lax.axis_size("y"), lax.axis_size("xh")
    ctx_place, exp_place = lax.axis_index(CTX), lax.axis_index(EXP)
    half = lax.axis_index("xh")
    part_rows = rows // n_exp
    features = width * n_exp
    slots = experts * capacity
    count = slots // n_y
    units = gate_weight.shape[1]
    half_units = units * n_y

    own_keys = lax.dynamic_slice_in_dim(latents[0], exp_place * part_rows, part_rows, 0)
    keys = swap(copies(own_keys, blocks), CTX).reshape(blocks * part_rows, latent_width)
    mask_row = lax.dynamic_index_in_dim(block_mask[0], ctx_place, 0, keepdims=True)
    extra = jnp.concatenate(
        [
            norm_gain[None, :],
            mask_row.astype(bf16),
            jnp.zeros((1, latent_width - width - blocks), bf16),
        ],
        axis=1,
    )
    sent = jnp.concatenate(
        [queries[0, :, 0, :], uv_weight[0].T, extra, jnp.zeros((15, latent_width), bf16)], axis=0
    )
    all_queries = [sent]
    for n in range(1, n_exp):
        a, k = n // n_y, n % n_y
        to = [(x * n_y + y, (x ^ a) * n_y + (y + k) % n_y) for x in range(n_xh) for y in range(n_y)]
        all_queries.append(lax.ppermute(sent, EXP, to))

    gate_rows = lax.all_gather(gate_weight[0], "y")
    up_rows = lax.all_gather(up_weight[0], "y")
    down = down_weight[0]
    down_own = lax.dynamic_slice_in_dim(down, half * half_units, half_units, 0)
    down_other = lax.dynamic_slice_in_dim(down, (1 - half) * half_units, half_units, 0)
    down_other = lax.ppermute(down_other, "xh", [(0, 1), (1, 0)])
    down_rows = lax.all_gather(jnp.concatenate([down_own, down_other], axis=1), "y")

    routes_t = routes[0].T
    place = call(
        lambda *refs: place_kernel(experts, capacity, *refs), shape(slots, rows), routes_t
    )
    at = jnp.stack([ctx_place, exp_place, half, lax.axis_index("y")]).astype(jnp.int32)
    partial, gains = call(
        lambda *refs: attend_kernel(rows, part_rows, values, *refs),
        [shape(n_exp, rows + 16, values), shape(n_exp, 16, width)],
        at,
        keys,
        *all_queries,
        specs=[in_smem] + [in_vmem] * (1 + n_exp),
    )
    terms = call(
        lambda *refs: project_kernel(rows, *refs),
        shape(n_exp, rows, width),
        swap(partial, EXP),
        out_weight[0],
    )
    hidden, picked, picks = call(
        hidden_kernel,
        [shape(rows, width), shape(slots, width), shape(16, width)],
        swap(terms, EXP),
        tokens[0],
        place,
        router_matrix,
        norm_gain[None, :],
        routes_t,
    )
    received = swap(picked.reshape(experts, capacity, width), CTX + ("rep",))
    groups = jnp.concatenate(
        [received.reshape(n_y, count, width), copies(picks, n_y)], axis=1
    )
    groups = copies(groups, n_xh).reshape(n_exp, count + 16, width)
    full_rows = swap(groups, EXP)
    whole = lambda j: (0, 0, 0)
    act = pl.pallas_call(
        gate_kernel,
        grid=(n_y,),
        out_shape=shape(half_units, count),
        in_specs=[
            pl.BlockSpec((n_exp, count + 16, width), whole),
            pl.BlockSpec((n_exp, 16, width), whole),
            pl.BlockSpec((1, units, features), lambda j: (j, 0, 0)),
            pl.BlockSpec((1, units, features), lambda j: (j, 0, 0)),
        ],
        out_specs=pl.BlockSpec((units, count), lambda j: (j, 0)),
        scratch_shapes=[pltpu.VMEM((count, features), bf16)],
        compiler_params=pltpu.CompilerParams(vmem_limit_bytes=24 << 20),
    )(full_rows, gains, gate_rows, up_rows)
    out = pl.pallas_call(
        down_kernel,
        grid=(n_y,),
        out_shape=shape(n_xh, n_y, count, width),
        in_specs=[
            in_smem,
            pl.BlockSpec((half_units, count), lambda j: (0, 0)),
            pl.BlockSpec((1, half_units, n_xh * width), lambda j: (j, 0, 0)),
        ],
        out_specs=pl.BlockSpec((n_xh, 1, count, width), lambda j: (0, j, 0, 0)),
        compiler_params=pltpu.CompilerParams(vmem_limit_bytes=24 << 20),
    )(half.reshape(1).astype(jnp.int32), act, down_rows)
    out = swap(out.reshape(n_exp, count, width), EXP).reshape(n_xh, n_y, count, width)
    out = jnp.sum(out.astype(f32), axis=0).astype(bf16)
    back = swap(out.reshape(experts, capacity, width), CTX + ("rep",)).reshape(slots, width)
    routed = call(
        lambda *refs: combine_kernel(experts, capacity, features, *refs),
        shape(rows, width),
        full_rows,
        routes_t,
        place,
        back,
    )
    return (hidden[None], routed[None])


def solution(mesh):
    sizes = mesh.shape
    fine = Mesh(
        mesh.devices.reshape(sizes["ctx"] // 2, 2, 2, sizes["exp"] // 2, sizes["rep"]),
        ("z", "xl", "xh", "y", "rep"),
    )
    placed = (
        P("rep", CTX, EXP, None),
        P("rep", CTX, None),
        P("rep", CTX, EXP),
        P(EXP, None, None),
        P(EXP, None, None),
        P(EXP, None, None),
        P(EXP),
        P(None, EXP),
        P("rep", CTX, None),
        P(CTX + ("rep",), EXP, None),
        P(CTX + ("rep",), EXP, None),
        P(CTX + ("rep",), None, EXP),
    )
    return jax.shard_map(
        body,
        mesh=fine,
        in_specs=placed,
        out_specs=(P("rep", CTX, EXP), P("rep", CTX, EXP)),
        check_vma=False,
    )
```

time: 289 us -> 279 us (0.965)
  waiting for transfers between devices: 91.3 us -> 52.6 us
  blocking collectives: 105 us -> 126 us
  starting transfers between devices: 50.2 us -> 57.4 us
  local copies, waits for them, and re-layouts: 10.6 us -> 7.68 us
    all_to_all x6 -> x3, waiting for transfers between devices: 89.2 us -> 26 us  [swap(): return lax.all_to_all(x, axes, split_axis=0, concat_axis=0, tiled=True)]
    ppermute x0 -> x8, starting transfers between devices: none -> 28.2 us  [the longest x7 25.1 us: body(): all_queries.append(lax.ppermute(sent, EXP, to))]
    ppermute x0 -> x8, waiting for transfers between devices: none -> 25.2 us  [the longest x7 23.1 us: body(): all_queries.append(lax.ppermute(sent, EXP, to))]
    all_to_all x6 -> x3, starting transfers between devices: 50.1 us -> 29.1 us  [swap(): return lax.all_to_all(x, axes, split_axis=0, concat_axis=0, tiled=True)]
    all_to_all x4, blocking collectives: 105 us -> 126 us  [swap(): return lax.all_to_all(x, axes, split_axis=0, concat_axis=0, tiled=True)]
    pallas_call x0 -> x2, Pallas kernels: none -> 5.7 us  [the longest x1 3.96 us: body(): pl.pallas_call(gate_kernel, grid=(n_y,), out_shape=shape(half_units, coun...]
    pallas_call x7 -> x5, Pallas kernels: 15.3 us -> 10.3 us  [call(): pl.pallas_call(kernel, out_shape=outs, in_specs=specs or [in_vmem] * len(...]
    unnamed x25 -> x26, local copies, waits for them, and re-layouts: 6.58 us -> 5.6 us
  transfers between devices with their start and end apart: 9 -> 14, of which waited for: 6 -> 5; matrix products, arithmetic and copies ran while one was open for 2% -> 1% of each run, Pallas kernels for 5% -> 5%
where the time goes in v2:
time: 279 us; the launch traced here: 276 us
  blocking collectives  126 us (45%)
  starting transfers between devices  57.4 us (21%)
  waiting for transfers between devices  52.6 us (19%)
  Pallas kernels  16 us (6%)
  between operations  14 us (5%)
  local copies, waits for them, and re-layouts  7.68 us (3%)
    all_to_all x4, blocking collectives, swap(): return lax.all_to_all(x, axes, split_axis=0, concat_axis=0, tiled=True)  126 us
    all_to_all x3, starting transfers between devices, swap(): return lax.all_to_all(x, axes, split_axis=0, concat_axis=0, tiled=True)  29.1 us
    all_to_all x3, waiting for transfers between devices, swap(): return lax.all_to_all(x, axes, split_axis=0, concat_axis=0, tiled=True)  26 us
    ppermute x7, starting transfers between devices, body(): all_queries.append(lax.ppermute(sent, EXP, to))  25.1 us
    ppermute x7, waiting for transfers between devices, body(): all_queries.append(lax.ppermute(sent, EXP, to))  23.1 us
    pallas_call x5, Pallas kernels, call(): pl.pallas_call(kernel, out_shape=outs, in_specs=specs or [in_vmem] * len(...  10.3 us
    unnamed x26, local copies, waits for them, and re-layouts  5.6 us
  transfers between devices with their start and end apart: 14, of which 5 were waited for; matrix products, arithmetic and copies ran while one was open for 1% of the time, Pallas kernels for 5%

profile of v2, /device:TPU:7, one launch (start us, length us, event | category | flops | bytes accessed | tf_op | source)
XLA Modules:
  0.0 275.7 jit_solution(808085458929479717)
XLA Ops:
  8.7 0.9 broadcast_in_dim.37
  9.6 16.3 %all-to-all-start = ((bf16[32,16,512]{2,1,0:T(8,128)(2,1)}), bf16[32,16,512]{2,1,0:T(8,128)(2,1)S(1)}, u32[]{:S(2)}, u32[]{:S(2)}) async-start(bf16[32,16,512]{2,1,0:T(8,128)(2,1)} %broadcast_in_dim.37), calls=%async_computation | async-start | bytes 1048576 | tf_op jit(solution)/shard_map/all_to_all | solution.py:216
  26.0 3.0 %collective-permute-start.7 = (bf16[704,256]{1,0:T(8,128)(2,1)S(1)}, bf16[704,256]{1,0:T(8,128)(2,1)S(1)}, u32[]{:S(2)}, u32[]{:S(2)}) collective-permute-start(bf16[704,256]{1,0:T(8,128)(2,1)S(1)} %get-tuple-element.13), channel_id=1, source_target_pairs={{0,8},{8,0},{1,9},{9,1},{2,10},{10,2},{3,11},{11,3},{4,12},{12,4},... | collective-permute-start | bytes 1081352 | tf_op jit(solution)/shard_map/ppermute | solution.py:282
  30.1 3.2 %collective-permute-start = (bf16[272,512]{1,0:T(8,128)(2,1)S(1)}, bf16[272,512]{1,0:T(8,128)(2,1)S(1)}, u32[]{:S(2)}, u32[]{:S(2)}) collective-permute-start(bf16[272,512]{1,0:T(8,128)(2,1)S(1)} %maximum_maximum_fusion.refs_2_), channel_id=1, source_target_pairs={{0,2},{2,4},{4,6},{6,0},{8,10},{10,12},{12,14},{14,8},{1,3},{3,5},... | collective-permute-start | bytes 835592 | tf_op jit(solution)/shard_map/ppermute | solution.py:275
  33.3 4.5 %collective-permute-start.1 = (bf16[272,512]{1,0:T(8,128)(2,1)S(1)}, bf16[272,512]{1,0:T(8,128)(2,1)S(1)}, u32[]{:S(2)}, u32[]{:S(2)}) collective-permute-start(bf16[272,512]{1,0:T(8,128)(2,1)S(1)} %maximum_maximum_fusion.refs_2_), channel_id=1, source_target_pairs={{0,4},{2,6},{4,0},{6,2},{8,12},{10,14},{12,8},{14,10},{1,5},{3,7},... | collective-permute-start | bytes 835592 | tf_op jit(solution)/shard_map/ppermute | solution.py:275
  37.9 2.1 collective-permute-done.7
  40.0 0.9 pad_maximum_fusion
  41.0 4.6 %collective-permute-start.2 = (bf16[272,512]{1,0:T(8,128)(2,1)S(1)}, bf16[272,512]{1,0:T(8,128)(2,1)S(1)}, u32[]{:S(2)}, u32[]{:S(2)}) collective-permute-start(bf16[272,512]{1,0:T(8,128)(2,1)S(1)} %maximum_maximum_fusion.refs_2_), channel_id=1, source_target_pairs={{0,6},{2,0},{4,2},{6,4},{8,14},{10,8},{12,10},{14,12},{1,7},{3,1},... | collective-permute-start | bytes 835592 | tf_op jit(solution)/shard_map/ppermute | solution.py:275
  45.6 3.1 %collective-permute-start.3 = (bf16[272,512]{1,0:T(8,128)(2,1)S(1)}, bf16[272,512]{1,0:T(8,128)(2,1)S(1)}, u32[]{:S(2)}, u32[]{:S(2)}) collective-permute-start(bf16[272,512]{1,0:T(8,128)(2,1)S(1)} %maximum_maximum_fusion.refs_2_), channel_id=1, source_target_pairs={{0,8},{2,10},{4,12},{6,14},{8,0},{10,2},{12,4},{14,6},{1,9},{3,11}... | collective-permute-start | bytes 835592 | tf_op jit(solution)/shard_map/ppermute | solution.py:275
  48.7 2.2 collective-permute-start.4
  50.9 5.6 %collective-permute-start.5 = (bf16[272,512]{1,0:T(8,128)(2,1)S(1)}, bf16[272,512]{1,0:T(8,128)(2,1)S(1)}, u32[]{:S(2)}, u32[]{:S(2)}) collective-permute-start(bf16[272,512]{1,0:T(8,128)(2,1)S(1)} %maximum_maximum_fusion.refs_2_), channel_id=1, source_target_pairs={{0,12},{2,14},{4,8},{6,10},{8,4},{10,6},{12,0},{14,2},{1,13},{3,15... | collective-permute-start | bytes 835592 | tf_op jit(solution)/shard_map/ppermute | solution.py:275
  56.5 15.4 %collective-permute-done.1.refs_4_ = bf16[272,512]{1,0:T(8,128)(2,1)S(1)} collective-permute-done((bf16[272,512]{1,0:T(8,128)(2,1)S(1)}, bf16[272,512]{1,0:T(8,128)(2,1)S(1)}, u32[]{:S(2)}, u32[]{:S(2)}) %collective-permute-start.1) | collective-permute-done | bytes 278560 | tf_op jit(solution)/shard_map/ppermute | solution.py:275
  71.9 1.9 collective-permute-start.6
  73.9 7.7 %collective-permute-done.6.refs_9_ = bf16[272,512]{1,0:T(8,128)(2,1)S(1)} collective-permute-done((bf16[272,512]{1,0:T(8,128)(2,1)S(1)}, bf16[272,512]{1,0:T(8,128)(2,1)S(1)}, u32[]{:S(2)}, u32[]{:S(2)}) %collective-permute-start.6) | collective-permute-done | bytes 278560 | tf_op jit(solution)/shard_map/ppermute | solution.py:275
  81.6 6.3 %shard_map.131 = (bf16[8,144,128]{2,1,0:T(8,128)(2,1)S(1)}, bf16[8,16,256]{2,1,0:T(8,128)(2,1)S(1)}) custom-call(s32[4]{0:T(128)S(1)} %pad_add_fusion.refs_0_, bf16[512,512]{1,0:T(8,128)(2,1)S(1)} %bitcast.36, bf16[272,512]{1,0:T(8,128)(2,1)S(1)} %maximum_maximum_fusion.refs_2_, bf16[272,512]{1,0:T(8,128)(2,1)S(1)} %collective-permute-done.refs_3_, ...), custom_call_target="tpu_custom_call" | custom-call | tf_op jit(solution)/shard_map/pallas_call | solution.py:29
  87.9 10.2 %all_to_all.35.refs_0_ = bf16[8,144,128]{2,1,0:T(8,128)(2,1)S(1)} all-to-all(bf16[8,144,128]{2,1,0:T(8,128)(2,1)S(1)} %get-tuple-element.7), channel_id=1, replica_groups=mesh['z'=16,'xl'=2,'xh'=2,'y'=4,'rep'=2] {'xh','y'}, dimensions={0} | all-to-all | bytes 589824 | tf_op jit(solution)/shard_map/all_to_all | solution.py:216
  98.1 1.5 shard_map.132
  99.6 6.2 %all-to-all-start.2 = ((bf16[8,128,256]{2,1,0:T(8,128)(2,1)}), bf16[8,128,256]{2,1,0:T(8,128)(2,1)S(1)}, u32[]{:S(2)}, u32[]{:S(2)}) async-start(bf16[8,128,256]{2,1,0:T(8,128)(2,1)} %shard_map.132), calls=%async_computation.2 | async-start | bytes 1048576 | tf_op jit(solution)/shard_map/all_to_all | solution.py:216
  106.2 7.6 %all-to-all-done.2.part_ref = bf16[8,128,256]{2,1,0:T(8,128)(2,1)S(1)} async-done(((bf16[8,128,256]{2,1,0:T(8,128)(2,1)}), bf16[8,128,256]{2,1,0:T(8,128)(2,1)S(1)}, u32[]{:S(2)}, u32[]{:S(2)}) %all-to-all-start.2) | async-done | bytes 524320 | tf_op jit(solution)/shard_map/all_to_all | solution.py:216
  113.8 0.7 shard_map.134
  114.5 51.4 %all_to_all.36 = bf16[64,16,256]{2,1,0:T(8,128)(2,1)S(1)} all-to-all(bf16[64,16,256]{2,1,0:T(8,128)(2,1)S(1)} %bitcast.38), channel_id=1, replica_groups=mesh['z'=16,'xl'=2,'xh'=2,'y'=4,'rep'=2] {'z','xl','rep'}, dimensions={0} | all-to-all | bytes 1048576 | tf_op jit(solution)/shard_map/all_to_all | solution.py:216
  165.9 1.1 broadcast_in_dim.43
  167.0 6.6 %all-to-all-start.4 = ((bf16[8,272,256]{2,1,0:T(8,128)(2,1)}), bf16[8,272,256]{2,1,0:T(8,128)(2,1)S(1)}, u32[]{:S(2)}, u32[]{:S(2)}) async-start(bf16[8,272,256]{2,1,0:T(8,128)(2,1)} %bitcast.44), calls=%async_computation.4 | async-start | bytes 2228224 | tf_op jit(solution)/shard_map/all_to_all | solution.py:216
  173.6 18.4 %all-to-all-done.4.rows_ref.refs_0_ = bf16[8,272,256]{2,1,0:T(8,128)(2,1)S(1)} async-done(((bf16[8,272,256]{2,1,0:T(8,128)(2,1)}), bf16[8,272,256]{2,1,0:T(8,128)(2,1)S(1)}, u32[]{:S(2)}, u32[]{:S(2)}) %all-to-all-start.4) | async-done | bytes 1114144 | tf_op jit(solution)/shard_map/all_to_all | solution.py:216
  192.0 1.8 copy-done.1
  193.8 1.8 copy-done.2
  195.6 4.0 %shard_map.135.act_ref = bf16[704,256]{1,0:T(8,128)(2,1)S(1)} custom-call(bf16[8,272,256]{2,1,0:T(8,128)(2,1)S(1)} %all-to-all-done.4.rows_ref.refs_0_, bf16[8,16,256]{2,1,0:T(8,128)(2,1)S(1)} %get-tuple-element.11.gain_ref, bf16[4,176,2048]{2,1,0:T(8,128)(2,1)S(1)} %copy-done.1, bf16[4,176,2048]{2,1,0:T(8,128)(2,1)S(1)} %copy-done.2), custom_call_target="tpu_custom_call" | custom-call | tf_op jit(solution)/shard_map/pallas_call | solution.py:321
  199.6 1.8 copy-done.3
  201.4 1.7 shard_map.136
  203.2 21.6 %all_to_all.37 = bf16[8,256,256]{2,1,0:T(8,128)(2,1)S(1)} all-to-all(bf16[8,256,256]{2,1,0:T(8,128)(2,1)S(1)} %bitcast.34), channel_id=1, replica_groups=mesh['z'=16,'xl'=2,'xh'=2,'y'=4,'rep'=2] {'xh','y'}, dimensions={0} | all-to-all | bytes 2097152 | tf_op jit(solution)/shard_map/all_to_all | solution.py:216
  225.3 42.5 %all_to_all.38 = bf16[64,16,256]{2,1,0:T(8,128)(2,1)S(1)} all-to-all(bf16[64,16,256]{2,1,0:T(8,128)(2,1)S(1)} %bitcast.47), channel_id=1, replica_groups=mesh['z'=16,'xl'=2,'xh'=2,'y'=4,'rep'=2] {'z','xl','rep'}, dimensions={0} | all-to-all | bytes 1048576 | tf_op jit(solution)/shard_map/all_to_all | solution.py:216
  267.8 1.4 shard_map.137
  (51 shorter events, 3.6 us)
Async XLA Ops:
  7.2 1.5 copy-start
  7.2 18.8 %copy-start.7 = (bf16[1,1408,256]{2,1,0:T(8,128)(2,1)S(1)}, bf16[1,1408,256]{2,1,0:T(8,128)(2,1)}, u32[]{:S(2)}) copy-start(bf16[1,1408,256]{2,1,0:T(8,128)(2,1)} %param.23) | copy-start | bytes 2162692
  7.2 166.4 %all-gather.5.cloned.1.call-start = ((), (), s32[]{:S(2)}) async-start(), calls=%async_computation.7 | async-start | bytes 3604480 | tf_op jit(solution)/shard_map/all_gather | solution.py:277
  7.9 165.7 %all-gather.7.cloned.1.call-start = ((), (), s32[]{:S(2)}) async-start(), calls=%async_computation.8 | async-start | bytes 3604480 | tf_op jit(solution)/shard_map/all_gather | solution.py:278
  8.7 20.4 %copy-start.11 = (bf16[256]{0:T(256)(128)(2,1)S(1)}, bf16[256]{0:T(256)(128)(2,1)}, u32[]{:S(2)}) copy-start(bf16[256]{0:T(256)(128)(2,1)} %param.18) | copy-start | bytes 1540
  8.7 20.4 %copy-start.9 = (bf16[1,512,128]{2,1,0:T(8,128)(2,1)S(1)}, bf16[1,512,128]{2,1,0:T(8,128)(2,1)}, u32[]{:S(2)}) copy-start(bf16[1,512,128]{2,1,0:T(8,128)(2,1)} %param.16) | copy-start | bytes 393220
  9.6 20.4 %copy-start.8 = (bf16[1,128,1,512]{3,1,2,0:T(8,128)(2,1)S(1)}, bf16[1,128,1,512]{3,1,2,0:T(8,128)(2,1)}, u32[]{:S(2)}) copy-start(bf16[1,128,1,512]{3,1,2,0:T(8,128)(2,1)} %param.12) | copy-start | bytes 393220
  9.6 72.0 %all-to-all-start = ((bf16[32,16,512]{2,1,0:T(8,128)(2,1)}), bf16[32,16,512]{2,1,0:T(8,128)(2,1)S(1)}, u32[]{:S(2)}, u32[]{:S(2)}) async-start(bf16[32,16,512]{2,1,0:T(8,128)(2,1)} %broadcast_in_dim.37), calls=%async_computation | async-start | bytes 1048576 | tf_op jit(solution)/shard_map/all_to_all | solution.py:216
  25.9 173.7 %all-gather.9.cloned.1.call-start = ((), (), s32[]{:S(2)}) async-start(), calls=%async_computation.9 | async-start | bytes 3604480 | tf_op jit(solution)/shard_map/all_gather | solution.py:283
  26.0 14.0 %collective-permute-start.7 = (bf16[704,256]{1,0:T(8,128)(2,1)S(1)}, bf16[704,256]{1,0:T(8,128)(2,1)S(1)}, u32[]{:S(2)}, u32[]{:S(2)}) collective-permute-start(bf16[704,256]{1,0:T(8,128)(2,1)S(1)} %get-tuple-element.13), channel_id=1, source_target_pairs={{0,8},{8,0},{1,9},{9,1},{2,10},{10,2},{3,11},{11,3},{4,12},{12,4},... | collective-permute-start | bytes 1081352 | tf_op jit(solution)/shard_map/ppermute | solution.py:282
  30.1 20.7 %collective-permute-start = (bf16[272,512]{1,0:T(8,128)(2,1)S(1)}, bf16[272,512]{1,0:T(8,128)(2,1)S(1)}, u32[]{:S(2)}, u32[]{:S(2)}) collective-permute-start(bf16[272,512]{1,0:T(8,128)(2,1)S(1)} %maximum_maximum_fusion.refs_2_), channel_id=1, source_target_pairs={{0,2},{2,4},{4,6},{6,0},{8,10},{10,12},{12,14},{14,8},{1,3},{3,5},... | collective-permute-start | bytes 835592 | tf_op jit(solution)/shard_map/ppermute | solution.py:275
  33.3 38.6 %collective-permute-start.1 = (bf16[272,512]{1,0:T(8,128)(2,1)S(1)}, bf16[272,512]{1,0:T(8,128)(2,1)S(1)}, u32[]{:S(2)}, u32[]{:S(2)}) collective-permute-start(bf16[272,512]{1,0:T(8,128)(2,1)S(1)} %maximum_maximum_fusion.refs_2_), channel_id=1, source_target_pairs={{0,4},{2,6},{4,0},{6,2},{8,12},{10,14},{12,8},{14,10},{1,5},{3,7},... | collective-permute-start | bytes 835592 | tf_op jit(solution)/shard_map/ppermute | solution.py:275
  41.0 33.0 %collective-permute-start.2 = (bf16[272,512]{1,0:T(8,128)(2,1)S(1)}, bf16[272,512]{1,0:T(8,128)(2,1)S(1)}, u32[]{:S(2)}, u32[]{:S(2)}) collective-permute-start(bf16[272,512]{1,0:T(8,128)(2,1)S(1)} %maximum_maximum_fusion.refs_2_), channel_id=1, source_target_pairs={{0,6},{2,0},{4,2},{6,4},{8,14},{10,8},{12,10},{14,12},{1,7},{3,1},... | collective-permute-start | bytes 835592 | tf_op jit(solution)/shard_map/ppermute | solution.py:275
  45.6 28.3 %collective-permute-start.3 = (bf16[272,512]{1,0:T(8,128)(2,1)S(1)}, bf16[272,512]{1,0:T(8,128)(2,1)S(1)}, u32[]{:S(2)}, u32[]{:S(2)}) collective-permute-start(bf16[272,512]{1,0:T(8,128)(2,1)S(1)} %maximum_maximum_fusion.refs_2_), channel_id=1, source_target_pairs={{0,8},{2,10},{4,12},{6,14},{8,0},{10,2},{12,4},{14,6},{1,9},{3,11}... | collective-permute-start | bytes 835592 | tf_op jit(solution)/shard_map/ppermute | solution.py:275
  48.7 25.2 %collective-permute-start.4 = (bf16[272,512]{1,0:T(8,128)(2,1)S(1)}, bf16[272,512]{1,0:T(8,128)(2,1)S(1)}, u32[]{:S(2)}, u32[]{:S(2)}) collective-permute-start(bf16[272,512]{1,0:T(8,128)(2,1)S(1)} %maximum_maximum_fusion.refs_2_), channel_id=1, source_target_pairs={{0,10},{2,12},{4,14},{6,8},{8,2},{10,4},{12,6},{14,0},{1,11},{3,13... | collective-permute-start | bytes 835592 | tf_op jit(solution)/shard_map/ppermute | solution.py:275
  50.9 23.1 %collective-permute-start.5 = (bf16[272,512]{1,0:T(8,128)(2,1)S(1)}, bf16[272,512]{1,0:T(8,128)(2,1)S(1)}, u32[]{:S(2)}, u32[]{:S(2)}) collective-permute-start(bf16[272,512]{1,0:T(8,128)(2,1)S(1)} %maximum_maximum_fusion.refs_2_), channel_id=1, source_target_pairs={{0,12},{2,14},{4,8},{6,10},{8,4},{10,6},{12,0},{14,2},{1,13},{3,15... | collective-permute-start | bytes 835592 | tf_op jit(solution)/shard_map/ppermute | solution.py:275
  71.9 9.7 %collective-permute-start.6 = (bf16[272,512]{1,0:T(8,128)(2,1)S(1)}, bf16[272,512]{1,0:T(8,128)(2,1)S(1)}, u32[]{:S(2)}, u32[]{:S(2)}) collective-permute-start(bf16[272,512]{1,0:T(8,128)(2,1)S(1)} %maximum_maximum_fusion.refs_2_), channel_id=1, source_target_pairs={{0,14},{2,8},{4,10},{6,12},{8,6},{10,0},{12,2},{14,4},{1,15},{3,9}... | collective-permute-start | bytes 835592 | tf_op jit(solution)/shard_map/ppermute | solution.py:275
  81.6 16.5 %copy-start.4 = (bf16[1,128,2048]{2,1,0:T(8,128)(2,1)S(1)}, bf16[1,128,2048]{2,1,0:T(8,128)(2,1)}, u32[]{:S(2)}) copy-start(bf16[1,128,2048]{2,1,0:T(8,128)(2,1)} %param.17) | copy-start | bytes 1572868
  87.9 17.9 %copy-start.10 = (s32[1,128,6]{1,0,2:T(1,128)S(1)}, s32[1,128,6]{1,0,2:T(1,128)}, u32[]{:S(2)}) copy-start(s32[1,128,6]{1,0,2:T(1,128)} %param.20) | copy-start | bytes 9220
  98.1 15.6 %copy-start.5 = (bf16[1,128,256]{2,1,0:T(8,128)(2,1)S(1)}, bf16[1,128,256]{2,1,0:T(8,128)(2,1)}, u32[]{:S(2)}) copy-start(bf16[1,128,256]{2,1,0:T(8,128)(2,1)} %param.14) | copy-start | bytes 196612
  98.1 15.6 %copy-start.6 = (bf16[64,256]{1,0:T(8,128)(2,1)S(1)}, bf16[64,256]{1,0:T(8,128)(2,1)}, u32[]{:S(2)}) copy-start(bf16[64,256]{1,0:T(8,128)(2,1)} %router_ref.1) | copy-start | bytes 98308
  99.6 14.2 %all-to-all-start.2 = ((bf16[8,128,256]{2,1,0:T(8,128)(2,1)}), bf16[8,128,256]{2,1,0:T(8,128)(2,1)S(1)}, u32[]{:S(2)}, u32[]{:S(2)}) async-start(bf16[8,128,256]{2,1,0:T(8,128)(2,1)} %shard_map.132), calls=%async_computation.2 | async-start | bytes 1048576 | tf_op jit(solution)/shard_map/all_to_all | solution.py:216
  167.0 25.0 %all-to-all-start.4 = ((bf16[8,272,256]{2,1,0:T(8,128)(2,1)}), bf16[8,272,256]{2,1,0:T(8,128)(2,1)S(1)}, u32[]{:S(2)}, u32[]{:S(2)}) async-start(bf16[8,272,256]{2,1,0:T(8,128)(2,1)} %bitcast.44), calls=%async_computation.4 | async-start | bytes 2228224 | tf_op jit(solution)/shard_map/all_to_all | solution.py:216
  192.0 1.8 copy-start.1
  193.8 1.8 copy-start.2
  199.6 1.8 copy-start.3
Sparse Core Ops, SparseCore 0:
  10.1 73.9 all-gather.4
  86.2 52.0 all-gather.6
  140.5 56.2 all-gather.8

commit v3 on v2

v3 whole, which is shorter than its diff:
```python
import jax
import jax.numpy as jnp
from jax import lax
from jax.experimental import pallas as pl
from jax.experimental.pallas import tpu as pltpu
from jax.sharding import Mesh, PartitionSpec as P

score_scale = 192.0 ** (-0.5)
epsilon = 1e-06
never = 1 << 20

f32 = jnp.float32
bf16 = jnp.bfloat16

in_vmem = pl.BlockSpec(memory_space=pltpu.VMEM)
in_smem = pl.BlockSpec(memory_space=pltpu.SMEM)


def iota(shape, dim):
    return lax.broadcasted_iota(jnp.int32, shape, dim)


def dot(a, b, ca, cb, **kw):
    return lax.dot_general(a, b, (((ca,), (cb,)), ((), ())), preferred_element_type=f32, **kw)


def call(kernel, outs, *operands, specs=None, scratch=(), limit=24):
    many = isinstance(outs, list)
    return pl.pallas_call(
        kernel,
        out_shape=outs,
        in_specs=specs or [in_vmem] * len(operands),
        out_specs=[in_vmem] * len(outs) if many else in_vmem,
        scratch_shapes=list(scratch),
        compiler_params=pltpu.CompilerParams(vmem_limit_bytes=limit << 20),
    )(*operands)


def three_terms(x):
    high = x.astype(bf16).astype(f32)
    middle = (x - high).astype(bf16).astype(f32)
    return high, middle, x - high - middle


def repeat_matrix(experts, capacity):
    tall = (experts * capacity, experts)
    return (iota(tall, 0) // capacity == iota(tall, 1)).astype(f32).astype(bf16)


def place_kernel(experts, capacity, routes_ref, place_ref):
    top, rows = routes_ref.shape
    routes = routes_ref[...]
    expert = iota((experts, rows), 0)
    member = routes[0:1] == expert
    for k in range(1, top):
        member = member | (routes[k : k + 1] == expert)
    earlier = (iota((rows, rows), 0) < iota((rows, rows), 1)).astype(f32).astype(bf16)
    count = dot(member.astype(f32).astype(bf16), earlier, 1, 0)
    code = jnp.where(member, count, -1.0).astype(bf16)
    spread = dot(repeat_matrix(experts, capacity), code, 1, 0)
    slot = iota((experts * capacity, rows), 0) % capacity
    place_ref[...] = (spread == slot.astype(f32)).astype(f32).astype(bf16)


def attend_kernel(rows, part_rows, at_ref, key_ref, *refs):
    pair_refs, out_ref, gain_ref = refs[:-2], refs[-2], refs[-1]
    own_block, own_part, own_half, own_y = at_ref[0], at_ref[1], at_ref[2], at_ref[3]
    n_y = len(pair_refs)
    keys = key_ref[...]
    count = keys.shape[0]
    lane = iota((count, 128), 1)
    block = iota((count, 128), 0) // part_rows
    earlier = ((block == lane) & (lane < own_block)).astype(f32).astype(bf16)
    key_row = iota((count, 1), 0)
    is_own = key_row // part_rows == own_block
    own_pos = own_part * part_rows + key_row % part_rows
    both = 2 * rows
    is_first = iota((1, both), 1) < rows
    query_pos = iota((count, both), 1) % rows
    width = gain_ref.shape[2]
    for shift in range(n_y):
        ref = pair_refs[shift]
        pair = jnp.concatenate([ref[0, 0:rows, :], ref[1, 0:rows, :]], axis=0)
        firsts = []
        for half in range(2):
            chosen = dot(earlier, ref[half, rows : rows + 16, width : width + 128], 1, 1)[:, 0:1]
            firsts.append(jnp.where(is_own, own_pos, jnp.where(chosen > 0.5, -1, never)))
        allowed = jnp.where(is_first, firsts[0], firsts[1]) <= query_pos
        scores = dot(keys, pair, 1, 1) * score_scale
        scores = jnp.where(allowed, scores, -1e30)
        top = jnp.max(scores, axis=0, keepdims=True)
        probs = jnp.where(allowed, jnp.exp(scores - top), 0.0)
        total = jnp.sum(probs, axis=0, keepdims=True)
        some = total > 0.0
        scale = jnp.where(some, 1.0 / jnp.where(some, total, 1.0), 0.0)
        latent = dot((probs * scale).astype(bf16), keys, 0, 0).astype(bf16)
        level = jnp.where(some, top + jnp.log(jnp.where(some, total, 1.0)), -1e30)
        terms = three_terms(level)
        at = iota((16, both), 0)
        stats = jnp.zeros((16, both), f32)
        for k, term in enumerate(terms):
            stats = jnp.where(at == k, term, stats)
        stats = stats.astype(bf16)
        for half in range(2):
            head = (own_half ^ half) * n_y + (own_y + n_y - shift) % n_y
            lanes = slice(half * rows, (half + 1) * rows)
            out_ref[head, 0:rows, :] = latent[lanes, :]
            out_ref[head, rows : rows + 16, 0:rows] = stats[:, lanes]
            out_ref[head, rows : rows + 16, rows:] = jnp.zeros((16, keys.shape[1] - rows), bf16)
            gain_ref[head] = ref[half, rows : rows + 16, 0:width]


def project_kernel(rows, part_ref, uv_ref, out_weight_ref, out_ref):
    parts = part_ref.shape[0]
    levels = []
    for s in range(parts):
        stats = part_ref[s, rows : rows + 16, 0:rows].astype(f32)
        levels.append(stats[0:1] + stats[1:2] + stats[2:3])
    top = levels[0]
    for level in levels[1:]:
        top = jnp.maximum(top, level)
    shares = [jnp.exp(level - top) for level in levels]
    total = shares[0]
    for share in shares[1:]:
        total = total + share
    scale = 1.0 / total
    at = iota((rows, rows), 0)
    square = jnp.zeros((rows, rows), f32)
    for s in range(parts):
        square = jnp.where(at == s, shares[s] * scale, square)
    columns = square.T
    latent = columns[:, 0:1] * part_ref[0, 0:rows, :].astype(f32)
    for s in range(1, parts):
        latent = latent + columns[:, s : s + 1] * part_ref[s, 0:rows, :].astype(f32)
    values = dot(latent.astype(bf16), uv_ref[...], 1, 0).astype(bf16)
    width = out_ref.shape[2]
    for d in range(out_ref.shape[0]):
        out_ref[d] = dot(values, out_weight_ref[:, d * width : (d + 1) * width], 1, 0).astype(bf16)


def hidden_kernel(
    part_ref, token_ref, place_ref, router_ref, gain_ref, routes_ref, hidden_ref, rows_ref, pick_ref
):
    attention = part_ref[0].astype(f32)
    for s in range(1, part_ref.shape[0]):
        attention = attention + part_ref[s].astype(f32)
    hidden = (token_ref[...].astype(f32) + attention).astype(bf16)
    hidden_ref[...] = hidden
    rows_ref[...] = dot(place_ref[...], hidden, 1, 0).astype(bf16)
    wide = hidden.astype(f32)
    exact = dict(precision=lax.Precision.HIGHEST)
    scaled = wide * gain_ref[...].astype(f32)
    logits = dot(router_ref[...].astype(f32), scaled, 1, 1, **exact)
    picks = dot(jnp.ones((8, wide.shape[1]), f32), wide * wide, 1, 1, **exact)
    routes = routes_ref[...]
    expert, at = iota(logits.shape, 0), iota(picks.shape, 0)
    for k in range(routes.shape[0]):
        pick = jnp.sum(jnp.where(routes[k : k + 1] == expert, logits, 0.0), axis=0, keepdims=True)
        picks = jnp.where(at == k, pick, picks)
    high, middle, rest = three_terms(picks)
    upper = jnp.concatenate([high, middle], axis=1)
    lower = jnp.concatenate([rest, jnp.zeros_like(rest)], axis=1)
    pick_ref[...] = jnp.concatenate([upper, lower], axis=0).astype(bf16)


def gate_kernel(at_ref, rows_ref, gain_ref, gate_ref, up_ref, gate2_ref, up2_ref, out_ref, normed_ref):
    n_y, _, width = rows_ref.shape
    count, features = normed_ref.shape
    half = at_ref[2]
    squares = jnp.zeros((count, 1), f32)
    for x in range(2):
        for y in range(n_y):
            wide = rows_ref[y, x * count : (x + 1) * count, :].astype(f32)
            squares = squares + jnp.sum(wide * wide, axis=1, keepdims=True)
    inverse = lax.rsqrt(squares / features + epsilon)
    for x in range(2):
        for y in range(n_y):
            s = x * n_y + y
            wide = rows_ref[y, x * count : (x + 1) * count, :].astype(f32)
            scaled = wide * gain_ref[s, 0:1, :].astype(f32)
            normed_ref[:, s * width : (s + 1) * width] = (scaled * inverse).astype(bf16)
    units = gate_ref.shape[0]
    for a, (g_ref, u_ref) in enumerate(((gate_ref, up_ref), (gate2_ref, up2_ref))):
        gate = dot(g_ref[...], normed_ref[...], 1, 1)
        up = dot(u_ref[...], normed_ref[...], 1, 1)
        act = (gate / (1.0 + jnp.exp(-gate)) * up).astype(bf16)
        out_ref[pl.ds(pl.multiple_of((half ^ a) * units, 16), units), :] = act


def down_kernel(at_ref, act_ref, down_ref, down2_ref, out_ref, act_all_ref):
    half = at_ref[2]
    n_y, both, _ = act_ref.shape
    units = both // 2
    for x in range(2):
        for y in range(n_y):
            at = (x * n_y + y) * units
            act_all_ref[at : at + units, :] = act_ref[y, x * units : (x + 1) * units, :]
    for a, ref in enumerate((down_ref, down2_ref)):
        out_ref[half ^ a] = dot(act_all_ref[...], ref[...], 0, 0).astype(bf16)


def combine_kernel(experts, capacity, features, row_ref, routes_ref, place_ref, back_ref, out_ref):
    rows = out_ref.shape[0]
    total = jnp.zeros((8, rows), f32)
    for s in range(row_ref.shape[0]):
        for at in range(experts * capacity, row_ref.shape[1], 16):
            terms = row_ref[s, at : at + 16, :].astype(f32)
            total = total + (terms[0:8, 0:rows] + terms[0:8, rows:] + terms[8:16, 0:rows])
    routes = routes_ref[...]
    top = routes.shape[0]
    inverse = lax.rsqrt(total[top : top + 1] / features + epsilon)
    gates = 1.0 / (1.0 + jnp.exp(-(inverse * total[0:top])))
    gates = gates / jnp.sum(gates, axis=0, keepdims=True)
    expert = iota((experts, rows), 0)
    weight = jnp.zeros((experts, rows), f32)
    for k in range(top):
        weight = jnp.where(routes[k : k + 1] == expert, gates[k : k + 1], weight)
    high = weight.astype(bf16)
    low = (weight - high.astype(f32)).astype(bf16)
    spread = repeat_matrix(experts, capacity)
    place = place_ref[...].astype(f32)
    back = back_ref[...]
    first = dot((dot(spread, high, 1, 0) * place).astype(bf16), back, 0, 0)
    second = dot((dot(spread, low, 1, 0) * place).astype(bf16), back, 0, 0)
    out_ref[...] = (first + second).astype(bf16)


def shape(*dims, dtype=bf16):
    return jax.ShapeDtypeStruct(dims, dtype)


def swap(x, axes):
    return lax.all_to_all(x, axes, split_axis=0, concat_axis=0, tiled=True)


def copies(x, n):
    return jnp.broadcast_to(x[None], (n,) + x.shape)


def all_shifts(x, n):
    turn = lambda k: [(y, (y + k) % n) for y in range(n)]
    return [x] + [lax.ppermute(x, "y", turn(k)) for k in range(1, n)]


def other_half(x):
    return lax.ppermute(x, "xh", [(0, 1), (1, 0)])


CTX, EXP = ("z", "xl"), ("xh", "y")
OWNERS = CTX + ("rep", "xh")


def body(
    queries,
    latents,
    tokens,
    block_mask,
    uv_weight,
    out_weight,
    norm_gain,
    router_matrix,
    routes,
    gate_weight,
    up_weight,
    down_weight,
):
    rows, latent_width = queries.shape[1], queries.shape[3]
    width = tokens.shape[2]
    experts = router_matrix.shape[0]
    capacity = 4 * rows * routes.shape[2] // (3 * experts)
    blocks = block_mask.shape[1]
    n_exp = lax.axis_size(EXP)
    n_y, n_xh = lax.axis_size("y"), lax.axis_size("xh")
    ctx_place, exp_place = lax.axis_index(CTX), lax.axis_index(EXP)
    half = lax.axis_index("xh")
    part_rows = rows // n_exp
    features = width * n_exp
    slots = experts * capacity
    count = slots // n_xh
    units = gate_weight.shape[1]

    own_keys = lax.dynamic_slice_in_dim(latents[0], exp_place * part_rows, part_rows, 0)
    keys = swap(copies(own_keys, blocks), CTX).reshape(blocks * part_rows, latent_width)
    mask_row = lax.dynamic_index_in_dim(block_mask[0], ctx_place, 0, keepdims=True)
    extra = jnp.concatenate(
        [
            norm_gain[None, :],
            mask_row.astype(bf16),
            jnp.zeros((1, latent_width - width - blocks), bf16),
        ],
        axis=1,
    )
    sent = jnp.concatenate(
        [queries[0, :, 0, :], extra, jnp.zeros((15, latent_width), bf16)], axis=0
    )
    all_queries = all_shifts(jnp.stack([sent, other_half(sent)]), n_y)

    gate2 = other_half(gate_weight[0])
    up2 = other_half(up_weight[0])
    down2 = other_half(down_weight[0])

    routes_t = routes[0].T
    place = call(
        lambda *refs: place_kernel(experts, capacity, *refs), shape(slots, rows), routes_t
    )
    at = jnp.stack([ctx_place, exp_place, half, lax.axis_index("y")]).astype(jnp.int32)
    partial, gains = call(
        lambda *refs: attend_kernel(rows, part_rows, *refs),
        [shape(n_exp, rows + 16, latent_width), shape(n_exp, 16, width)],
        at,
        keys,
        *all_queries,
        specs=[in_smem] + [in_vmem] * (1 + n_y),
    )
    partial = swap(partial, EXP)
    terms = call(
        lambda *refs: project_kernel(rows, *refs),
        shape(n_exp, rows, width),
        partial,
        uv_weight[0],
        out_weight[0],
    )
    terms = swap(terms, EXP)
    hidden, picked, picks = call(
        hidden_kernel,
        [shape(rows, width), shape(slots, width), shape(16, width)],
        terms,
        tokens[0],
        place,
        router_matrix,
        norm_gain[None, :],
        routes_t,
    )
    received = swap(picked.reshape(experts * n_xh, capacity // n_xh, width), OWNERS)
    received, gate2 = lax.optimization_barrier((received, gate2))
    received = received.reshape(experts, n_xh, capacity // n_xh, width).swapaxes(0, 1)
    mine = jnp.concatenate([received.reshape(slots, width), picks, other_half(picks)], axis=0)
    full_rows = swap(copies(mine, n_y), "y")
    act = call(
        gate_kernel,
        shape(n_xh * units, count),
        at,
        full_rows,
        gains,
        gate_weight[0],
        up_weight[0],
        gate2,
        up2,
        specs=[in_smem] + [in_vmem] * 6,
        scratch=[pltpu.VMEM((count, features), bf16)],
    )
    act = swap(copies(act, n_y), "y")
    out = call(
        down_kernel,
        shape(n_xh, count, width),
        at,
        act,
        down_weight[0],
        down2,
        specs=[in_smem] + [in_vmem] * 3,
        scratch=[pltpu.VMEM((n_exp * units, count), bf16)],
    )
    out = out.reshape(n_xh, experts, capacity // n_xh, width).swapaxes(0, 1)
    back = swap(out.reshape(experts * n_xh, capacity // n_xh, width), OWNERS)
    back = back.reshape(slots, width)
    routed = call(
        lambda *refs: combine_kernel(experts, capacity, features, *refs),
        shape(rows, width),
        full_rows,
        routes_t,
        place,
        back,
    )
    return (hidden[None], routed[None])


def solution(mesh):
    sizes = mesh.shape
    fine = Mesh(
        mesh.devices.reshape(sizes["ctx"] // 2, 2, 2, sizes["exp"] // 2, sizes["rep"]),
        ("z", "xl", "xh", "y", "rep"),
    )
    placed = (
        P("rep", CTX, EXP, None),
        P("rep", CTX, None),
        P("rep", CTX, EXP),
        P(EXP, None, None),
        P(EXP, None, None),
        P(EXP, None, None),
        P(EXP),
        P(None, EXP),
        P("rep", CTX, None),
        P(CTX + ("rep",), EXP, None),
        P(CTX + ("rep",), EXP, None),
        P(CTX + ("rep",), None, EXP),
    )
    return jax.shard_map(
        body,
        mesh=fine,
        in_specs=placed,
        out_specs=(P("rep", CTX, EXP), P("rep", CTX, EXP)),
        check_vma=False,
    )
```

time: 279 us -> 257 us (0.921)
  blocking collectives: 126 us -> 61.7 us
  waiting for transfers between devices: 52.6 us -> 91.3 us
  starting transfers between devices: 57.4 us -> 73.1 us
  between operations: 14 us -> 0.93 us
  local copies, waits for them, and re-layouts: 7.68 us -> 12.8 us
    all_to_all x4 -> x2, blocking collectives: 126 us -> 61.7 us  [swap(): return lax.all_to_all(x, axes, split_axis=0, concat_axis=0, tiled=True)]
    ppermute x8, waiting for transfers between devices: 25.2 us -> 68.5 us  [the longest x5 60.6 us: other_half(): return lax.ppermute(x, 'xh', [(0, 1), (1, 0)])]
    all_to_all x3 -> x5, starting transfers between devices: 29.1 us -> 48 us  [swap(): return lax.all_to_all(x, axes, split_axis=0, concat_axis=0, tiled=True)]
    pallas_call x2 -> x0, Pallas kernels: 5.7 us -> none  [the longest x1 3.96 us: body(): pl.pallas_call(gate_kernel, grid=(n_y,), out_shape=shape(half_units, coun...]
    pallas_call x5 -> x7, Pallas kernels: 10.3 us -> 14.8 us  [call(): pl.pallas_call(kernel, out_shape=outs, in_specs=specs or [in_vmem] * len(...]
    unnamed x26 -> x37, local copies, waits for them, and re-layouts: 5.6 us -> 9.05 us
    all_to_all x3 -> x5, waiting for transfers between devices: 26 us -> 22.8 us  [swap(): return lax.all_to_all(x, axes, split_axis=0, concat_axis=0, tiled=True)]
    ppermute x8, starting transfers between devices: 28.2 us -> 25.1 us  [the longest x5 14.4 us: other_half(): return lax.ppermute(x, 'xh', [(0, 1), (1, 0)])]
  transfers between devices with their start and end apart: 14 -> 13, of which waited for: 5 -> 10; matrix products, arithmetic and copies ran while one was open for 1% -> 0% of each run, Pallas kernels for 5% -> 0%
where the time goes in v3:
time: 257 us; the launch traced here: 256 us
  waiting for transfers between devices  91.3 us (36%)
  starting transfers between devices  73.1 us (28%)
  blocking collectives  61.7 us (24%)
  Pallas kernels  14.8 us (6%)
  local copies, waits for them, and re-layouts  12.8 us (5%)
    all_to_all x2, blocking collectives, swap(): return lax.all_to_all(x, axes, split_axis=0, concat_axis=0, tiled=True)  61.7 us
    ppermute x5, waiting for transfers between devices, other_half(): return lax.ppermute(x, 'xh', [(0, 1), (1, 0)])  60.6 us
    all_to_all x5, starting transfers between devices, swap(): return lax.all_to_all(x, axes, split_axis=0, concat_axis=0, tiled=True)  48 us
    all_to_all x5, waiting for transfers between devices, swap(): return lax.all_to_all(x, axes, split_axis=0, concat_axis=0, tiled=True)  22.8 us
    pallas_call x7, Pallas kernels, call(): pl.pallas_call(kernel, out_shape=outs, in_specs=specs or [in_vmem] * len(...  14.8 us
    ppermute x5, starting transfers between devices, other_half(): return lax.ppermute(x, 'xh', [(0, 1), (1, 0)])  14.4 us
    ppermute x3, starting transfers between devices, all_shifts(): return [x] + [lax.ppermute(x, 'y', turn(k)) for k in range(1, n)]  10.7 us
    unnamed x37, local copies, waits for them, and re-layouts  9.05 us
  transfers between devices with their start and end apart: 13, of which 10 were waited for; matrix products, arithmetic and copies ran while one was open for 0% of the time, Pallas kernels for 0%

profile of v3, /device:TPU:7, one launch (start us, length us, event | category | flops | bytes accessed | tf_op | source)
XLA Modules:
  0.0 255.6 jit_solution(10149318451726616928)
XLA Ops:
  2.4 16.1 %all-to-all-start = ((bf16[32,16,512]{2,1,0:T(8,128)(2,1)}), bf16[32,16,512]{2,1,0:T(8,128)(2,1)S(1)}, u32[]{:S(2)}, u32[]{:S(2)}) async-start(bf16[32,16,512]{2,1,0:T(8,128)(2,1)} %broadcast_in_dim.37), calls=%async_computation | async-start | bytes 1048576 | tf_op jit(solution)/shard_map/all_to_all | solution.py:233
  19.5 3.0 %collective-permute-start = (bf16[144,512]{1,0:T(8,128)(2,1)S(1)}, bf16[144,512]{1,0:T(8,128)(2,1)S(1)}, u32[]{:S(2)}, u32[]{:S(2)}) collective-permute-start(bf16[144,512]{1,0:T(8,128)(2,1)S(1)} %maximum_maximum_fusion), channel_id=1, source_target_pairs={{0,8},{8,0},{1,9},{9,1},{2,10},{10,2},{3,11},{11,3},{4,12},{12,4},... | collective-permute-start | bytes 442376 | tf_op jit(solution)/shard_map/ppermute | solution.py:246
  22.6 4.3 %collective-permute-done = bf16[144,512]{1,0:T(8,128)(2,1)S(1)} collective-permute-done((bf16[144,512]{1,0:T(8,128)(2,1)S(1)}, bf16[144,512]{1,0:T(8,128)(2,1)S(1)}, u32[]{:S(2)}, u32[]{:S(2)}) %collective-permute-start) | collective-permute-done | bytes 147488 | tf_op jit(solution)/shard_map/ppermute | solution.py:246
  26.9 3.2 %collective-permute-start.1 = (bf16[2,144,512]{2,1,0:T(8,128)(2,1)S(1)}, bf16[2,144,512]{2,1,0:T(8,128)(2,1)S(1)}, u32[]{:S(2)}, u32[]{:S(2)}) collective-permute-start(bf16[2,144,512]{2,1,0:T(8,128)(2,1)S(1)} %pad_maximum_fusion.1.refs_2_), channel_id=1, source_target_pairs={{0,2},{2,4},{4,6},{6,0},{1,3},{3,5},{5,7},{7,1},{8,10},{10,12},{12... | collective-permute-start | bytes 884744 | tf_op jit(solution)/shard_map/ppermute | solution.py:242
  30.1 4.5 %collective-permute-start.2 = (bf16[2,144,512]{2,1,0:T(8,128)(2,1)S(1)}, bf16[2,144,512]{2,1,0:T(8,128)(2,1)S(1)}, u32[]{:S(2)}, u32[]{:S(2)}) collective-permute-start(bf16[2,144,512]{2,1,0:T(8,128)(2,1)S(1)} %pad_maximum_fusion.1.refs_2_), channel_id=1, source_target_pairs={{0,4},{2,6},{4,0},{6,2},{1,5},{3,7},{5,1},{7,3},{8,12},{10,14},{12... | collective-permute-start | bytes 884744 | tf_op jit(solution)/shard_map/ppermute | solution.py:242
  34.7 3.0 %collective-permute-start.3 = (bf16[2,144,512]{2,1,0:T(8,128)(2,1)S(1)}, bf16[2,144,512]{2,1,0:T(8,128)(2,1)S(1)}, u32[]{:S(2)}, u32[]{:S(2)}) collective-permute-start(bf16[2,144,512]{2,1,0:T(8,128)(2,1)S(1)} %pad_maximum_fusion.1.refs_2_), channel_id=1, source_target_pairs={{0,6},{2,0},{4,2},{6,4},{1,7},{3,1},{5,3},{7,5},{8,14},{10,8},{12,... | collective-permute-start | bytes 884744 | tf_op jit(solution)/shard_map/ppermute | solution.py:242
  37.7 5.4 %collective-permute-done.2.refs_4_ = bf16[2,144,512]{2,1,0:T(8,128)(2,1)S(1)} collective-permute-done((bf16[2,144,512]{2,1,0:T(8,128)(2,1)S(1)}, bf16[2,144,512]{2,1,0:T(8,128)(2,1)S(1)}, u32[]{:S(2)}, u32[]{:S(2)}) %collective-permute-start.2) | collective-permute-done | bytes 294944 | tf_op jit(solution)/shard_map/ppermute | solution.py:242
  43.1 2.5 collective-permute-done.3.refs_5_
  45.6 4.9 %all-to-all-done = bf16[32,16,512]{2,1,0:T(8,128)(2,1)S(1)} async-done(((bf16[32,16,512]{2,1,0:T(8,128)(2,1)}), bf16[32,16,512]{2,1,0:T(8,128)(2,1)S(1)}, u32[]{:S(2)}, u32[]{:S(2)}) %all-to-all-start) | async-done | bytes 524320 | tf_op jit(solution)/shard_map/all_to_all | solution.py:233
  50.5 3.7 %shard_map.131 = (bf16[8,144,512]{2,1,0:T(8,128)(2,1)S(1)}, bf16[8,16,256]{2,1,0:T(8,128)(2,1)S(1)}) custom-call(s32[4]{0:T(128)S(1)} %pad_add_fusion.refs_0_.at_ref, bf16[512,512]{1,0:T(8,128)(2,1)S(1)} %bitcast.36, bf16[2,144,512]{2,1,0:T(8,128)(2,1)S(1)} %pad_maximum_fusion.1.refs_2_, bf16[2,144,512]{2,1,0:T(8,128)(2,1)S(1)} %collective-permute-done.1.refs_3_, ...), custom_call_target="tpu_custom_call" | custom-call | tf_op jit(solution)/shard_map/pallas_call | solution.py:29
  54.3 20.2 %all_to_all.35.refs_0_ = bf16[8,144,512]{2,1,0:T(8,128)(2,1)S(1)} all-to-all(bf16[8,144,512]{2,1,0:T(8,128)(2,1)S(1)} %get-tuple-element.9), channel_id=1, replica_groups=mesh['z'=16,'xl'=2,'xh'=2,'y'=4,'rep'=2] {'xh','y'}, dimensions={0} | all-to-all | bytes 2359296 | tf_op jit(solution)/shard_map/all_to_all | solution.py:233
  74.5 1.6 shard_map.132
  76.1 6.3 %all-to-all-start.2 = ((bf16[8,128,256]{2,1,0:T(8,128)(2,1)}), bf16[8,128,256]{2,1,0:T(8,128)(2,1)S(1)}, u32[]{:S(2)}, u32[]{:S(2)}) async-start(bf16[8,128,256]{2,1,0:T(8,128)(2,1)} %shard_map.132), calls=%async_computation.2 | async-start | bytes 1048576 | tf_op jit(solution)/shard_map/all_to_all | solution.py:233
  82.7 6.3 %all-to-all-done.2.part_ref = bf16[8,128,256]{2,1,0:T(8,128)(2,1)S(1)} async-done(((bf16[8,128,256]{2,1,0:T(8,128)(2,1)}), bf16[8,128,256]{2,1,0:T(8,128)(2,1)S(1)}, u32[]{:S(2)}, u32[]{:S(2)}) %all-to-all-start.2) | async-done | bytes 524320 | tf_op jit(solution)/shard_map/all_to_all | solution.py:233
  89.0 1.3 shard_map.134
  90.3 17.5 %all-to-all-start.3 = ((bf16[128,8,256]{2,1,0:T(8,128)(2,1)}), bf16[128,8,256]{2,1,0:T(8,128)(2,1)S(1)}, u32[]{:S(2)}, u32[]{:S(2)}) async-start(bf16[128,8,256]{2,1,0:T(8,128)(2,1)} %bitcast.15), calls=%async_computation.3 | async-start | bytes 1048576 | tf_op jit(solution)/shard_map/all_to_all | solution.py:233
  107.8 3.1 %collective-permute-start.4 = (bf16[176,2048]{1,0:T(8,128)(2,1)S(1)}, bf16[176,2048]{1,0:T(8,128)(2,1)S(1)}, u32[]{:S(2)}, u32[]{:S(2)}) collective-permute-start(bf16[176,2048]{1,0:T(8,128)(2,1)S(1)} %bitcast.39), channel_id=1, source_target_pairs={{0,8},{8,0},{1,9},{9,1},{2,10},{10,2},{3,11},{11,3},{4,12},{12,4},... | collective-permute-start | bytes 2162696 | tf_op jit(solution)/shard_map/ppermute | solution.py:246
  110.9 3.7 %collective-permute-start.5 = (bf16[16,256]{1,0:T(8,128)(2,1)S(1)}, bf16[16,256]{1,0:T(8,128)(2,1)S(1)}, u32[]{:S(2)}, u32[]{:S(2)}) collective-permute-start(bf16[16,256]{1,0:T(8,128)(2,1)S(1)} %get-tuple-element.13), channel_id=1, source_target_pairs={{0,8},{8,0},{1,9},{9,1},{2,10},{10,2},{3,11},{11,3},{4,12},{12,4},... | collective-permute-start | bytes 24584 | tf_op jit(solution)/shard_map/ppermute | solution.py:246
  114.6 18.7 %collective-permute-done.4.gate2_ref = bf16[176,2048]{1,0:T(8,128)(2,1)S(1)} collective-permute-done((bf16[176,2048]{1,0:T(8,128)(2,1)S(1)}, bf16[176,2048]{1,0:T(8,128)(2,1)S(1)}, u32[]{:S(2)}, u32[]{:S(2)}) %collective-permute-start.4) | collective-permute-done | bytes 720928 | tf_op jit(solution)/shard_map/ppermute | solution.py:246
  134.2 6.9 %all-to-all-done.3 = bf16[128,8,256]{2,1,0:T(8,128)(2,1)S(1)} async-done(((bf16[128,8,256]{2,1,0:T(8,128)(2,1)}), bf16[128,8,256]{2,1,0:T(8,128)(2,1)S(1)}, u32[]{:S(2)}, u32[]{:S(2)}) %all-to-all-start.3) | async-done | bytes 524320 | tf_op jit(solution)/shard_map/all_to_all | solution.py:233
  141.2 1.5 broadcast_in_dim.42
  142.7 3.6 %all-to-all-start.4 = ((bf16[4,1056,256]{2,1,0:T(8,128)(2,1)}), bf16[4,1056,256]{2,1,0:T(8,128)(2,1)S(1)}, u32[]{:S(2)}, u32[]{:S(2)}) async-start(bf16[4,1056,256]{2,1,0:T(8,128)(2,1)} %broadcast_in_dim.42), calls=%async_computation.4 | async-start | bytes 4325376 | tf_op jit(solution)/shard_map/all_to_all | solution.py:233
  146.4 2.5 collective-permute-start.6
  148.9 19.0 %collective-permute-done.6.up2_ref = bf16[176,2048]{1,0:T(8,128)(2,1)S(1)} collective-permute-done((bf16[176,2048]{1,0:T(8,128)(2,1)}, bf16[176,2048]{1,0:T(8,128)(2,1)S(1)}, u32[]{:S(2)}, u32[]{:S(2)}) %collective-permute-start.6) | collective-permute-done | bytes 720928 | tf_op jit(solution)/shard_map/ppermute | solution.py:246
  168.8 4.7 %all-to-all-done.4.rows_ref.refs_0_ = bf16[4,1056,256]{2,1,0:T(8,128)(2,1)S(1)} async-done(((bf16[4,1056,256]{2,1,0:T(8,128)(2,1)}), bf16[4,1056,256]{2,1,0:T(8,128)(2,1)S(1)}, u32[]{:S(2)}, u32[]{:S(2)}) %all-to-all-start.4) | async-done | bytes 2162720 | tf_op jit(solution)/shard_map/all_to_all | solution.py:233
  176.8 4.0 %shard_map.135 = bf16[352,512]{1,0:T(8,128)(2,1)S(1)} custom-call(s32[4]{0:T(128)S(1)} %pad_add_fusion.refs_0_.at_ref, bf16[4,1056,256]{2,1,0:T(8,128)(2,1)S(1)} %all-to-all-done.4.rows_ref.refs_0_, bf16[8,16,256]{2,1,0:T(8,128)(2,1)S(1)} %get-tuple-element.14.gain_ref, bf16[176,2048]{1,0:T(8,128)(2,1)S(1)} %bitcast.40, bf16[176,2048]{1,0:T(8,128)(2,1)S(1)} %bitcast.42, ...), custom_call_target="tpu_custom_call" | custom-call | tf_op jit(solution)/shard_map/pallas_call | solution.py:29
  182.0 4.5 %all-to-all-start.5 = ((bf16[4,352,512]{2,1,0:T(8,128)(2,1)}), bf16[4,352,512]{2,1,0:T(8,128)(2,1)}, u32[]{:S(2)}, u32[]{:S(2)}) async-start(bf16[4,352,512]{2,1,0:T(8,128)(2,1)} %broadcast_in_dim.43), calls=%async_computation.5 | async-start | bytes 2883584 | tf_op jit(solution)/shard_map/all_to_all | solution.py:233
  186.5 2.1 collective-permute-start.7
  188.6 18.6 %collective-permute-done.7.down2_ref = bf16[1408,256]{1,0:T(8,128)(2,1)S(1)} collective-permute-done((bf16[1408,256]{1,0:T(8,128)(2,1)S(1)}, bf16[1408,256]{1,0:T(8,128)(2,1)S(1)}, u32[]{:S(2)}, u32[]{:S(2)}) %collective-permute-start.7) | collective-permute-done | bytes 720928 | tf_op jit(solution)/shard_map/ppermute | solution.py:246
  210.3 2.4 shard_map.136
  212.7 41.5 %all_to_all.36 = bf16[128,8,256]{2,1,0:T(8,128)(2,1)S(1)} all-to-all(bf16[128,8,256]{2,1,0:T(8,128)(2,1)S(1)} %bitcast.53), channel_id=1, replica_groups=mesh['z'=16,'xl'=2,'xh'=2,'y'=4,'rep'=2] {'z','xl','rep','xh'}, dimensions={0} | all-to-all | bytes 1048576 | tf_op jit(solution)/shard_map/all_to_all | solution.py:233
  254.2 1.4 shard_map.137
  (56 shorter events, 12.7 us)
Async XLA Ops:
  0.6 0.9 copy-start
  0.6 17.9 %copy-start.17 = (bf16[256]{0:T(256)(128)(2,1)S(1)}, bf16[256]{0:T(256)(128)(2,1)}, u32[]{:S(2)}) copy-start(bf16[256]{0:T(256)(128)(2,1)} %param.18) | copy-start | bytes 1540
  0.7 18.7 %copy-start.15 = (bf16[1,128,1,512]{3,1,2,0:T(8,128)(2,1)S(1)}, bf16[1,128,1,512]{3,1,2,0:T(8,128)(2,1)}, u32[]{:S(2)}) copy-start(bf16[1,128,1,512]{3,1,2,0:T(8,128)(2,1)} %param.12) | copy-start | bytes 393220
  2.4 48.1 %all-to-all-start = ((bf16[32,16,512]{2,1,0:T(8,128)(2,1)}), bf16[32,16,512]{2,1,0:T(8,128)(2,1)S(1)}, u32[]{:S(2)}, u32[]{:S(2)}) async-start(bf16[32,16,512]{2,1,0:T(8,128)(2,1)} %broadcast_in_dim.37), calls=%async_computation | async-start | bytes 1048576 | tf_op jit(solution)/shard_map/all_to_all | solution.py:233
  19.5 7.4 %collective-permute-start = (bf16[144,512]{1,0:T(8,128)(2,1)S(1)}, bf16[144,512]{1,0:T(8,128)(2,1)S(1)}, u32[]{:S(2)}, u32[]{:S(2)}) collective-permute-start(bf16[144,512]{1,0:T(8,128)(2,1)S(1)} %maximum_maximum_fusion), channel_id=1, source_target_pairs={{0,8},{8,0},{1,9},{9,1},{2,10},{10,2},{3,11},{11,3},{4,12},{12,4},... | collective-permute-start | bytes 442376 | tf_op jit(solution)/shard_map/ppermute | solution.py:246
  26.9 10.8 %collective-permute-start.1 = (bf16[2,144,512]{2,1,0:T(8,128)(2,1)S(1)}, bf16[2,144,512]{2,1,0:T(8,128)(2,1)S(1)}, u32[]{:S(2)}, u32[]{:S(2)}) collective-permute-start(bf16[2,144,512]{2,1,0:T(8,128)(2,1)S(1)} %pad_maximum_fusion.1.refs_2_), channel_id=1, source_target_pairs={{0,2},{2,4},{4,6},{6,0},{1,3},{3,5},{5,7},{7,1},{8,10},{10,12},{12... | collective-permute-start | bytes 884744 | tf_op jit(solution)/shard_map/ppermute | solution.py:242
  30.1 13.0 %collective-permute-start.2 = (bf16[2,144,512]{2,1,0:T(8,128)(2,1)S(1)}, bf16[2,144,512]{2,1,0:T(8,128)(2,1)S(1)}, u32[]{:S(2)}, u32[]{:S(2)}) collective-permute-start(bf16[2,144,512]{2,1,0:T(8,128)(2,1)S(1)} %pad_maximum_fusion.1.refs_2_), channel_id=1, source_target_pairs={{0,4},{2,6},{4,0},{6,2},{1,5},{3,7},{5,1},{7,3},{8,12},{10,14},{12... | collective-permute-start | bytes 884744 | tf_op jit(solution)/shard_map/ppermute | solution.py:242
  34.7 10.9 %collective-permute-start.3 = (bf16[2,144,512]{2,1,0:T(8,128)(2,1)S(1)}, bf16[2,144,512]{2,1,0:T(8,128)(2,1)S(1)}, u32[]{:S(2)}, u32[]{:S(2)}) collective-permute-start(bf16[2,144,512]{2,1,0:T(8,128)(2,1)S(1)} %pad_maximum_fusion.1.refs_2_), channel_id=1, source_target_pairs={{0,6},{2,0},{4,2},{6,4},{1,7},{3,1},{5,3},{7,5},{8,14},{10,8},{12,... | collective-permute-start | bytes 884744 | tf_op jit(solution)/shard_map/ppermute | solution.py:242
  54.3 20.2 %copy-start.11 = (bf16[1,128,2048]{2,1,0:T(8,128)(2,1)S(1)}, bf16[1,128,2048]{2,1,0:T(8,128)(2,1)}, u32[]{:S(2)}) copy-start(bf16[1,128,2048]{2,1,0:T(8,128)(2,1)} %param.17) | copy-start | bytes 1572868
  54.3 20.2 %copy-start.12 = (bf16[1,512,128]{2,1,0:T(8,128)(2,1)S(1)}, bf16[1,512,128]{2,1,0:T(8,128)(2,1)}, u32[]{:S(2)}) copy-start(bf16[1,512,128]{2,1,0:T(8,128)(2,1)} %param.16) | copy-start | bytes 393220
  74.5 7.9 %copy-start.16 = (s32[1,128,6]{1,0,2:T(1,128)S(1)}, s32[1,128,6]{1,0,2:T(1,128)}, u32[]{:S(2)}) copy-start(s32[1,128,6]{1,0,2:T(1,128)} %param.20) | copy-start | bytes 9220
  76.1 12.9 %copy-start.13 = (bf16[1,128,256]{2,1,0:T(8,128)(2,1)S(1)}, bf16[1,128,256]{2,1,0:T(8,128)(2,1)}, u32[]{:S(2)}) copy-start(bf16[1,128,256]{2,1,0:T(8,128)(2,1)} %param.14) | copy-start | bytes 196612
  76.1 12.9 %copy-start.14 = (bf16[64,256]{1,0:T(8,128)(2,1)S(1)}, bf16[64,256]{1,0:T(8,128)(2,1)}, u32[]{:S(2)}) copy-start(bf16[64,256]{1,0:T(8,128)(2,1)} %router_ref.1) | copy-start | bytes 98308
  76.1 12.9 %all-to-all-start.2 = ((bf16[8,128,256]{2,1,0:T(8,128)(2,1)}), bf16[8,128,256]{2,1,0:T(8,128)(2,1)S(1)}, u32[]{:S(2)}, u32[]{:S(2)}) async-start(bf16[8,128,256]{2,1,0:T(8,128)(2,1)} %shard_map.132), calls=%async_computation.2 | async-start | bytes 1048576 | tf_op jit(solution)/shard_map/all_to_all | solution.py:233
  82.3 25.5 %copy-start.1 = (bf16[1,176,2048]{2,1,0:T(8,128)(2,1)S(1)}, bf16[1,176,2048]{2,1,0:T(8,128)(2,1)}, u32[]{:S(2)}) copy-start(bf16[1,176,2048]{2,1,0:T(8,128)(2,1)} %param.21) | copy-start | bytes 2162692
  90.3 50.8 %all-to-all-start.3 = ((bf16[128,8,256]{2,1,0:T(8,128)(2,1)}), bf16[128,8,256]{2,1,0:T(8,128)(2,1)S(1)}, u32[]{:S(2)}, u32[]{:S(2)}) async-start(bf16[128,8,256]{2,1,0:T(8,128)(2,1)} %bitcast.15), calls=%async_computation.3 | async-start | bytes 1048576 | tf_op jit(solution)/shard_map/all_to_all | solution.py:233
  107.8 25.5 %collective-permute-start.4 = (bf16[176,2048]{1,0:T(8,128)(2,1)S(1)}, bf16[176,2048]{1,0:T(8,128)(2,1)S(1)}, u32[]{:S(2)}, u32[]{:S(2)}) collective-permute-start(bf16[176,2048]{1,0:T(8,128)(2,1)S(1)} %bitcast.39), channel_id=1, source_target_pairs={{0,8},{8,0},{1,9},{9,1},{2,10},{10,2},{3,11},{11,3},{4,12},{12,4},... | collective-permute-start | bytes 2162696 | tf_op jit(solution)/shard_map/ppermute | solution.py:246
  110.9 30.3 %collective-permute-start.5 = (bf16[16,256]{1,0:T(8,128)(2,1)S(1)}, bf16[16,256]{1,0:T(8,128)(2,1)S(1)}, u32[]{:S(2)}, u32[]{:S(2)}) collective-permute-start(bf16[16,256]{1,0:T(8,128)(2,1)S(1)} %get-tuple-element.13), channel_id=1, source_target_pairs={{0,8},{8,0},{1,9},{9,1},{2,10},{10,2},{3,11},{11,3},{4,12},{12,4},... | collective-permute-start | bytes 24584 | tf_op jit(solution)/shard_map/ppermute | solution.py:246
  133.4 0.9 copy-start.5
  142.7 30.7 %all-to-all-start.4 = ((bf16[4,1056,256]{2,1,0:T(8,128)(2,1)}), bf16[4,1056,256]{2,1,0:T(8,128)(2,1)S(1)}, u32[]{:S(2)}, u32[]{:S(2)}) async-start(bf16[4,1056,256]{2,1,0:T(8,128)(2,1)} %broadcast_in_dim.42), calls=%async_computation.4 | async-start | bytes 4325376 | tf_op jit(solution)/shard_map/all_to_all | solution.py:233
  146.4 21.5 %collective-permute-start.6 = (bf16[176,2048]{1,0:T(8,128)(2,1)}, bf16[176,2048]{1,0:T(8,128)(2,1)S(1)}, u32[]{:S(2)}, u32[]{:S(2)}) collective-permute-start(bf16[176,2048]{1,0:T(8,128)(2,1)} %bitcast.41), channel_id=1, source_target_pairs={{0,8},{8,0},{1,9},{9,1},{2,10},{10,2},{3,11},{11,3},{4,12},{12,4},... | collective-permute-start | bytes 2162696 | tf_op jit(solution)/shard_map/ppermute | solution.py:246
  167.9 0.9 copy-start.7
  173.4 1.1 copy-start.2
  174.5 1.1 copy-start.6
  175.6 1.1 copy-start.8
  182.0 4.5 %copy-start.3 = (bf16[1,1408,256]{2,1,0:T(8,128)(2,1)S(1)}, bf16[1,1408,256]{2,1,0:T(8,128)(2,1)}, u32[]{:S(2)}) copy-start(bf16[1,1408,256]{2,1,0:T(8,128)(2,1)} %param.23) | copy-start | bytes 2162692
  182.0 26.1 %all-to-all-start.5 = ((bf16[4,352,512]{2,1,0:T(8,128)(2,1)}), bf16[4,352,512]{2,1,0:T(8,128)(2,1)}, u32[]{:S(2)}, u32[]{:S(2)}) async-start(bf16[4,352,512]{2,1,0:T(8,128)(2,1)} %broadcast_in_dim.43), calls=%async_computation.5 | async-start | bytes 2883584 | tf_op jit(solution)/shard_map/all_to_all | solution.py:233
  186.5 20.7 %collective-permute-start.7 = (bf16[1408,256]{1,0:T(8,128)(2,1)S(1)}, bf16[1408,256]{1,0:T(8,128)(2,1)S(1)}, u32[]{:S(2)}, u32[]{:S(2)}) collective-permute-start(bf16[1408,256]{1,0:T(8,128)(2,1)S(1)} %bitcast.43), channel_id=1, source_target_pairs={{0,8},{8,0},{1,9},{9,1},{2,10},{10,2},{3,11},{11,3},{4,12},{12,4},... | collective-permute-start | bytes 2162696 | tf_op jit(solution)/shard_map/ppermute | solution.py:246
  207.2 0.9 copy-start.9
  208.0 1.1 copy-start.4
  209.2 1.1 copy-start.10

commit v4 on v3

--- a/solution.py
+++ b/solution.py
@@ -293,11 +293,14 @@
     sent = jnp.concatenate(
         [queries[0, :, 0, :], extra, jnp.zeros((15, latent_width), bf16)], axis=0
     )
-    all_queries = all_shifts(jnp.stack([sent, other_half(sent)]), n_y)
-
-    gate2 = other_half(gate_weight[0])
+    other, gate = lax.optimization_barrier((other_half(sent), gate_weight[0]))
+    all_queries = all_shifts(jnp.stack([sent, other]), n_y)
+
+    gate2 = other_half(gate)
     up2 = other_half(up_weight[0])
     down2 = other_half(down_weight[0])
+
+    keys, gate2 = lax.optimization_barrier((keys, gate2))
 
     routes_t = routes[0].T
     place = call(
@@ -332,10 +335,10 @@
         routes_t,
     )
     received = swap(picked.reshape(experts * n_xh, capacity // n_xh, width), OWNERS)
-    received, gate2 = lax.optimization_barrier((received, gate2))
+    received, up2 = lax.optimization_barrier((received, up2))
     received = received.reshape(experts, n_xh, capacity // n_xh, width).swapaxes(0, 1)
     mine = jnp.concatenate([received.reshape(slots, width), picks, other_half(picks)], axis=0)
-    full_rows = swap(copies(mine, n_y), "y")
+    full_rows, down2 = lax.optimization_barrier((swap(copies(mine, n_y), "y"), down2))
     act = call(
         gate_kernel,
         shape(n_xh * units, count),

time: 257 us -> 250 us (0.973)
  waiting for transfers between devices: 91.3 us -> 67.9 us
  blocking collectives: 61.7 us -> 82.8 us
  local copies, waits for them, and re-layouts: 12.8 us -> 9.47 us
    all_to_all x2 -> x3, blocking collectives: 61.7 us -> 82.8 us  [swap(): return lax.all_to_all(x, axes, split_axis=0, concat_axis=0, tiled=True)]
    ppermute x5, waiting for transfers between devices: 60.6 us -> 49.6 us  [other_half(): return lax.ppermute(x, 'xh', [(0, 1), (1, 0)])]
    ppermute x3, waiting for transfers between devices: 7.85 us -> 0.01 us  [all_shifts(): return [x] + [lax.ppermute(x, 'y', turn(k)) for k in range(1, n)]]
    all_to_all x5 -> x4, waiting for transfers between devices: 22.8 us -> 18.3 us  [swap(): return lax.all_to_all(x, axes, split_axis=0, concat_axis=0, tiled=True)]
    all_to_all x5 -> x4, starting transfers between devices: 48 us -> 46.8 us  [swap(): return lax.all_to_all(x, axes, split_axis=0, concat_axis=0, tiled=True)]
  transfers between devices with their start and end apart: 13 -> 12, of which waited for: 10 -> 8; matrix products, arithmetic and copies ran while one was open for 0% -> 0% of each run, Pallas kernels for 0% -> 0%
where the time goes in v4:
time: 250 us; the launch traced here: 249 us
  blocking collectives  82.8 us (33%)
  starting transfers between devices  73.5 us (29%)
  waiting for transfers between devices  67.9 us (27%)
  Pallas kernels  13.8 us (6%)
  local copies, waits for them, and re-layouts  9.47 us (4%)
    all_to_all x3, blocking collectives, swap(): return lax.all_to_all(x, axes, split_axis=0, concat_axis=0, tiled=True)  82.8 us
    ppermute x5, waiting for transfers between devices, other_half(): return lax.ppermute(x, 'xh', [(0, 1), (1, 0)])  49.6 us
    all_to_all x4, starting transfers between devices, swap(): return lax.all_to_all(x, axes, split_axis=0, concat_axis=0, tiled=True)  46.8 us
    all_to_all x4, waiting for transfers between devices, swap(): return lax.all_to_all(x, axes, split_axis=0, concat_axis=0, tiled=True)  18.3 us
    ppermute x5, starting transfers between devices, other_half(): return lax.ppermute(x, 'xh', [(0, 1), (1, 0)])  16 us
    pallas_call x7, Pallas kernels, call(): pl.pallas_call(kernel, out_shape=outs, in_specs=specs or [in_vmem] * len(...  13.8 us
    ppermute x3, starting transfers between devices, all_shifts(): return [x] + [lax.ppermute(x, 'y', turn(k)) for k in range(1, n)]  10.7 us
    unnamed x37, local copies, waits for them, and re-layouts  6.83 us
  transfers between devices with their start and end apart: 12, of which 8 were waited for; matrix products, arithmetic and copies ran while one was open for 0% of the time, Pallas kernels for 0%

profile of v4, /device:TPU:7, one launch (start us, length us, event | category | flops | bytes accessed | tf_op | source)
XLA Modules:
  0.0 249.5 jit_solution(3402678345820549712)
XLA Ops:
  2.4 16.1 %all-to-all-start = ((bf16[32,16,512]{2,1,0:T(8,128)(2,1)}), bf16[32,16,512]{2,1,0:T(8,128)(2,1)S(1)}, u32[]{:S(2)}, u32[]{:S(2)}) async-start(bf16[32,16,512]{2,1,0:T(8,128)(2,1)} %broadcast_in_dim.37), calls=%async_computation | async-start | bytes 1048576 | tf_op jit(solution)/shard_map/all_to_all | solution.py:233
  19.5 3.0 %collective-permute-start = (bf16[144,512]{1,0:T(8,128)(2,1)S(1)}, bf16[144,512]{1,0:T(8,128)(2,1)S(1)}, u32[]{:S(2)}, u32[]{:S(2)}) collective-permute-start(bf16[144,512]{1,0:T(8,128)(2,1)S(1)} %maximum_maximum_fusion), channel_id=1, source_target_pairs={{0,8},{8,0},{1,9},{9,1},{2,10},{10,2},{3,11},{11,3},{4,12},{12,4},... | collective-permute-start | bytes 442376 | tf_op jit(solution)/shard_map/ppermute | solution.py:246
  22.5 4.4 %collective-permute-done = bf16[144,512]{1,0:T(8,128)(2,1)S(1)} collective-permute-done((bf16[144,512]{1,0:T(8,128)(2,1)S(1)}, bf16[144,512]{1,0:T(8,128)(2,1)S(1)}, u32[]{:S(2)}, u32[]{:S(2)}) %collective-permute-start) | collective-permute-done | bytes 147488 | tf_op jit(solution)/shard_map/ppermute | solution.py:246
  26.9 3.6 %collective-permute-start.1 = (bf16[176,2048]{1,0:T(8,128)(2,1)S(1)}, bf16[176,2048]{1,0:T(8,128)(2,1)S(1)}, u32[]{:S(2)}, u32[]{:S(2)}) collective-permute-start(bf16[176,2048]{1,0:T(8,128)(2,1)S(1)} %bitcast.39), channel_id=1, source_target_pairs={{0,8},{8,0},{1,9},{9,1},{2,10},{10,2},{3,11},{11,3},{4,12},{12,4},... | collective-permute-start | bytes 2162696 | tf_op jit(solution)/shard_map/ppermute | solution.py:246
  30.7 3.2 %collective-permute-start.2 = (bf16[2,144,512]{2,1,0:T(8,128)(2,1)S(1)}, bf16[2,144,512]{2,1,0:T(8,128)(2,1)S(1)}, u32[]{:S(2)}, u32[]{:S(2)}) collective-permute-start(bf16[2,144,512]{2,1,0:T(8,128)(2,1)S(1)} %pad_maximum_fusion.1.refs_2_), channel_id=1, source_target_pairs={{0,2},{2,4},{4,6},{6,0},{1,3},{3,5},{5,7},{7,1},{8,10},{10,12},{12... | collective-permute-start | bytes 884744 | tf_op jit(solution)/shard_map/ppermute | solution.py:242
  33.9 4.5 %collective-permute-start.3 = (bf16[2,144,512]{2,1,0:T(8,128)(2,1)S(1)}, bf16[2,144,512]{2,1,0:T(8,128)(2,1)S(1)}, u32[]{:S(2)}, u32[]{:S(2)}) collective-permute-start(bf16[2,144,512]{2,1,0:T(8,128)(2,1)S(1)} %pad_maximum_fusion.1.refs_2_), channel_id=1, source_target_pairs={{0,4},{2,6},{4,0},{6,2},{1,5},{3,7},{5,1},{7,3},{8,12},{10,14},{12... | collective-permute-start | bytes 884744 | tf_op jit(solution)/shard_map/ppermute | solution.py:242
  38.4 3.0 %collective-permute-start.4 = (bf16[2,144,512]{2,1,0:T(8,128)(2,1)S(1)}, bf16[2,144,512]{2,1,0:T(8,128)(2,1)S(1)}, u32[]{:S(2)}, u32[]{:S(2)}) collective-permute-start(bf16[2,144,512]{2,1,0:T(8,128)(2,1)S(1)} %pad_maximum_fusion.1.refs_2_), channel_id=1, source_target_pairs={{0,6},{2,0},{4,2},{6,4},{1,7},{3,1},{5,3},{7,5},{8,14},{10,8},{12,... | collective-permute-start | bytes 884744 | tf_op jit(solution)/shard_map/ppermute | solution.py:242
  41.5 7.4 %collective-permute-done.1.gate2_ref = bf16[176,2048]{1,0:T(8,128)(2,1)S(1)} collective-permute-done((bf16[176,2048]{1,0:T(8,128)(2,1)S(1)}, bf16[176,2048]{1,0:T(8,128)(2,1)S(1)}, u32[]{:S(2)}, u32[]{:S(2)}) %collective-permute-start.1) | collective-permute-done | bytes 720928 | tf_op jit(solution)/shard_map/ppermute | solution.py:246
  50.5 3.7 %shard_map.131 = (bf16[8,144,512]{2,1,0:T(8,128)(2,1)S(1)}, bf16[8,16,256]{2,1,0:T(8,128)(2,1)S(1)}) custom-call(s32[4]{0:T(128)S(1)} %pad_add_fusion.refs_0_.at_ref, bf16[512,512]{1,0:T(8,128)(2,1)S(1)} %bitcast.36, bf16[2,144,512]{2,1,0:T(8,128)(2,1)S(1)} %pad_maximum_fusion.1.refs_2_, bf16[2,144,512]{2,1,0:T(8,128)(2,1)S(1)} %collective-permute-done.2.refs_3_, ...), custom_call_target="tpu_custom_call" | custom-call | tf_op jit(solution)/shard_map/pallas_call | solution.py:29
  54.2 19.7 %all_to_all.35.refs_0_ = bf16[8,144,512]{2,1,0:T(8,128)(2,1)S(1)} all-to-all(bf16[8,144,512]{2,1,0:T(8,128)(2,1)S(1)} %get-tuple-element.18), channel_id=1, replica_groups=mesh['z'=16,'xl'=2,'xh'=2,'y'=4,'rep'=2] {'xh','y'}, dimensions={0} | all-to-all | bytes 2359296 | tf_op jit(solution)/shard_map/all_to_all | solution.py:233
  74.0 1.6 shard_map.132
  75.5 6.2 %all-to-all-start.2 = ((bf16[8,128,256]{2,1,0:T(8,128)(2,1)}), bf16[8,128,256]{2,1,0:T(8,128)(2,1)S(1)}, u32[]{:S(2)}, u32[]{:S(2)}) async-start(bf16[8,128,256]{2,1,0:T(8,128)(2,1)} %shard_map.132), calls=%async_computation.2 | async-start | bytes 1048576 | tf_op jit(solution)/shard_map/all_to_all | solution.py:233
  82.2 6.0 %all-to-all-done.2.part_ref = bf16[8,128,256]{2,1,0:T(8,128)(2,1)S(1)} async-done(((bf16[8,128,256]{2,1,0:T(8,128)(2,1)}), bf16[8,128,256]{2,1,0:T(8,128)(2,1)S(1)}, u32[]{:S(2)}, u32[]{:S(2)}) %all-to-all-start.2) | async-done | bytes 524320 | tf_op jit(solution)/shard_map/all_to_all | solution.py:233
  88.2 1.3 shard_map.134
  89.4 20.8 %all-to-all-start.3 = ((bf16[128,8,256]{2,1,0:T(8,128)(2,1)}), bf16[128,8,256]{2,1,0:T(8,128)(2,1)S(1)}, u32[]{:S(2)}, u32[]{:S(2)}) async-start(bf16[128,8,256]{2,1,0:T(8,128)(2,1)} %bitcast.16), calls=%async_computation.3 | async-start | bytes 1048576 | tf_op jit(solution)/shard_map/all_to_all | solution.py:233
  110.3 3.1 %collective-permute-start.5 = (bf16[176,2048]{1,0:T(8,128)(2,1)S(1)}, bf16[176,2048]{1,0:T(8,128)(2,1)S(1)}, u32[]{:S(2)}, u32[]{:S(2)}) collective-permute-start(bf16[176,2048]{1,0:T(8,128)(2,1)S(1)} %bitcast.41), channel_id=1, source_target_pairs={{0,8},{8,0},{1,9},{9,1},{2,10},{10,2},{3,11},{11,3},{4,12},{12,4},... | collective-permute-start | bytes 2162696 | tf_op jit(solution)/shard_map/ppermute | solution.py:246
  113.4 3.7 %collective-permute-start.6 = (bf16[16,256]{1,0:T(8,128)(2,1)S(1)}, bf16[16,256]{1,0:T(8,128)(2,1)S(1)}, u32[]{:S(2)}, u32[]{:S(2)}) collective-permute-start(bf16[16,256]{1,0:T(8,128)(2,1)S(1)} %get-tuple-element.22), channel_id=1, source_target_pairs={{0,8},{8,0},{1,9},{9,1},{2,10},{10,2},{3,11},{11,3},{4,12},{12,4},... | collective-permute-start | bytes 24584 | tf_op jit(solution)/shard_map/ppermute | solution.py:246
  117.1 18.7 %collective-permute-done.5.up2_ref = bf16[176,2048]{1,0:T(8,128)(2,1)S(1)} collective-permute-done((bf16[176,2048]{1,0:T(8,128)(2,1)S(1)}, bf16[176,2048]{1,0:T(8,128)(2,1)S(1)}, u32[]{:S(2)}, u32[]{:S(2)}) %collective-permute-start.5) | collective-permute-done | bytes 720928 | tf_op jit(solution)/shard_map/ppermute | solution.py:246
  136.7 6.9 %all-to-all-done.3 = bf16[128,8,256]{2,1,0:T(8,128)(2,1)S(1)} async-done(((bf16[128,8,256]{2,1,0:T(8,128)(2,1)}), bf16[128,8,256]{2,1,0:T(8,128)(2,1)S(1)}, u32[]{:S(2)}, u32[]{:S(2)}) %all-to-all-start.3) | async-done | bytes 524320 | tf_op jit(solution)/shard_map/all_to_all | solution.py:233
  143.7 1.5 broadcast_in_dim.42
  145.2 3.6 %all-to-all-start.4 = ((bf16[4,1056,256]{2,1,0:T(8,128)(2,1)}), bf16[4,1056,256]{2,1,0:T(8,128)(2,1)S(1)}, u32[]{:S(2)}, u32[]{:S(2)}) async-start(bf16[4,1056,256]{2,1,0:T(8,128)(2,1)} %broadcast_in_dim.42), calls=%async_computation.4 | async-start | bytes 4325376 | tf_op jit(solution)/shard_map/all_to_all | solution.py:233
  148.8 2.5 %collective-permute-start.7 = (bf16[1408,256]{1,0:T(8,128)(2,1)}, bf16[1408,256]{1,0:T(8,128)(2,1)S(1)}, u32[]{:S(2)}, u32[]{:S(2)}) collective-permute-start(bf16[1408,256]{1,0:T(8,128)(2,1)} %bitcast.43), channel_id=1, source_target_pairs={{0,8},{8,0},{1,9},{9,1},{2,10},{10,2},{3,11},{11,3},{4,12},{12,4},... | collective-permute-start | bytes 2162696 | tf_op jit(solution)/shard_map/ppermute | solution.py:246
  151.3 19.0 %collective-permute-done.7.down2_ref = bf16[1408,256]{1,0:T(8,128)(2,1)S(1)} collective-permute-done((bf16[1408,256]{1,0:T(8,128)(2,1)}, bf16[1408,256]{1,0:T(8,128)(2,1)S(1)}, u32[]{:S(2)}, u32[]{:S(2)}) %collective-permute-start.7) | collective-permute-done | bytes 720928 | tf_op jit(solution)/shard_map/ppermute | solution.py:246
  171.2 4.7 %all-to-all-done.4.rows_ref.refs_0_ = bf16[4,1056,256]{2,1,0:T(8,128)(2,1)S(1)} async-done(((bf16[4,1056,256]{2,1,0:T(8,128)(2,1)}), bf16[4,1056,256]{2,1,0:T(8,128)(2,1)S(1)}, u32[]{:S(2)}, u32[]{:S(2)}) %all-to-all-start.4) | async-done | bytes 2162720 | tf_op jit(solution)/shard_map/all_to_all | solution.py:233
  175.9 1.1 copy-done.3
  177.0 1.1 copy-done.6
  178.1 1.1 copy-done.8
  179.2 4.0 %shard_map.135 = bf16[352,512]{1,0:T(8,128)(2,1)S(1)} custom-call(s32[4]{0:T(128)S(1)} %pad_add_fusion.refs_0_.at_ref, bf16[4,1056,256]{2,1,0:T(8,128)(2,1)S(1)} %all-to-all-done.4.rows_ref.refs_0_, bf16[8,16,256]{2,1,0:T(8,128)(2,1)S(1)} %get-tuple-element.24.gain_ref, bf16[176,2048]{1,0:T(8,128)(2,1)S(1)} %bitcast.40, bf16[176,2048]{1,0:T(8,128)(2,1)S(1)} %bitcast.42, ...), custom_call_target="tpu_custom_call" | custom-call | tf_op jit(solution)/shard_map/pallas_call | solution.py:29
  183.3 21.6 %all_to_all.36.act_ref = bf16[4,352,512]{2,1,0:T(8,128)(2,1)S(1)} all-to-all(bf16[4,352,512]{2,1,0:T(8,128)(2,1)S(1)} %broadcast_in_dim.43), channel_id=1, replica_groups=mesh['z'=16,'xl'=2,'xh'=2,'y'=4,'rep'=2] {'y'}, dimensions={0} | all-to-all | bytes 2883584 | tf_op jit(solution)/shard_map/all_to_all | solution.py:233
  205.0 1.6 shard_map.136
  206.6 41.5 %all_to_all.37 = bf16[128,8,256]{2,1,0:T(8,128)(2,1)S(1)} all-to-all(bf16[128,8,256]{2,1,0:T(8,128)(2,1)S(1)} %bitcast.53), channel_id=1, replica_groups=mesh['z'=16,'xl'=2,'xh'=2,'y'=4,'rep'=2] {'z','xl','rep','xh'}, dimensions={0} | all-to-all | bytes 1048576 | tf_op jit(solution)/shard_map/all_to_all | solution.py:233
  248.1 1.4 shard_map.137
  (55 shorter events, 6.8 us)
Async XLA Ops:
  0.6 0.9 copy-start
  0.6 17.9 %copy-start.17 = (bf16[256]{0:T(256)(128)(2,1)S(1)}, bf16[256]{0:T(256)(128)(2,1)}, u32[]{:S(2)}) copy-start(bf16[256]{0:T(256)(128)(2,1)} %param.18) | copy-start | bytes 1540
  0.7 18.7 %copy-start.15 = (bf16[1,128,1,512]{3,1,2,0:T(8,128)(2,1)S(1)}, bf16[1,128,1,512]{3,1,2,0:T(8,128)(2,1)}, u32[]{:S(2)}) copy-start(bf16[1,128,1,512]{3,1,2,0:T(8,128)(2,1)} %param.12) | copy-start | bytes 393220
  0.7 26.2 %copy-start.1 = (bf16[1,176,2048]{2,1,0:T(8,128)(2,1)S(1)}, bf16[1,176,2048]{2,1,0:T(8,128)(2,1)}, u32[]{:S(2)}) copy-start(bf16[1,176,2048]{2,1,0:T(8,128)(2,1)} %param.21) | copy-start | bytes 2162692
  2.4 48.1 %all-to-all-start = ((bf16[32,16,512]{2,1,0:T(8,128)(2,1)}), bf16[32,16,512]{2,1,0:T(8,128)(2,1)S(1)}, u32[]{:S(2)}, u32[]{:S(2)}) async-start(bf16[32,16,512]{2,1,0:T(8,128)(2,1)} %broadcast_in_dim.37), calls=%async_computation | async-start | bytes 1048576 | tf_op jit(solution)/shard_map/all_to_all | solution.py:233
  19.5 7.4 %collective-permute-start = (bf16[144,512]{1,0:T(8,128)(2,1)S(1)}, bf16[144,512]{1,0:T(8,128)(2,1)S(1)}, u32[]{:S(2)}, u32[]{:S(2)}) collective-permute-start(bf16[144,512]{1,0:T(8,128)(2,1)S(1)} %maximum_maximum_fusion), channel_id=1, source_target_pairs={{0,8},{8,0},{1,9},{9,1},{2,10},{10,2},{3,11},{11,3},{4,12},{12,4},... | collective-permute-start | bytes 442376 | tf_op jit(solution)/shard_map/ppermute | solution.py:246
  26.9 22.0 %collective-permute-start.1 = (bf16[176,2048]{1,0:T(8,128)(2,1)S(1)}, bf16[176,2048]{1,0:T(8,128)(2,1)S(1)}, u32[]{:S(2)}, u32[]{:S(2)}) collective-permute-start(bf16[176,2048]{1,0:T(8,128)(2,1)S(1)} %bitcast.39), channel_id=1, source_target_pairs={{0,8},{8,0},{1,9},{9,1},{2,10},{10,2},{3,11},{11,3},{4,12},{12,4},... | collective-permute-start | bytes 2162696 | tf_op jit(solution)/shard_map/ppermute | solution.py:246
  30.7 19.8 %collective-permute-start.2 = (bf16[2,144,512]{2,1,0:T(8,128)(2,1)S(1)}, bf16[2,144,512]{2,1,0:T(8,128)(2,1)S(1)}, u32[]{:S(2)}, u32[]{:S(2)}) collective-permute-start(bf16[2,144,512]{2,1,0:T(8,128)(2,1)S(1)} %pad_maximum_fusion.1.refs_2_), channel_id=1, source_target_pairs={{0,2},{2,4},{4,6},{6,0},{1,3},{3,5},{5,7},{7,1},{8,10},{10,12},{12... | collective-permute-start | bytes 884744 | tf_op jit(solution)/shard_map/ppermute | solution.py:242
  33.9 16.6 %collective-permute-start.3 = (bf16[2,144,512]{2,1,0:T(8,128)(2,1)S(1)}, bf16[2,144,512]{2,1,0:T(8,128)(2,1)S(1)}, u32[]{:S(2)}, u32[]{:S(2)}) collective-permute-start(bf16[2,144,512]{2,1,0:T(8,128)(2,1)S(1)} %pad_maximum_fusion.1.refs_2_), channel_id=1, source_target_pairs={{0,4},{2,6},{4,0},{6,2},{1,5},{3,7},{5,1},{7,3},{8,12},{10,14},{12... | collective-permute-start | bytes 884744 | tf_op jit(solution)/shard_map/ppermute | solution.py:242
  38.4 12.1 %collective-permute-start.4 = (bf16[2,144,512]{2,1,0:T(8,128)(2,1)S(1)}, bf16[2,144,512]{2,1,0:T(8,128)(2,1)S(1)}, u32[]{:S(2)}, u32[]{:S(2)}) collective-permute-start(bf16[2,144,512]{2,1,0:T(8,128)(2,1)S(1)} %pad_maximum_fusion.1.refs_2_), channel_id=1, source_target_pairs={{0,6},{2,0},{4,2},{6,4},{1,7},{3,1},{5,3},{7,5},{8,14},{10,8},{12,... | collective-permute-start | bytes 884744 | tf_op jit(solution)/shard_map/ppermute | solution.py:242
  48.9 0.9 copy-start.5
  54.2 19.8 %copy-start.11 = (bf16[1,128,2048]{2,1,0:T(8,128)(2,1)S(1)}, bf16[1,128,2048]{2,1,0:T(8,128)(2,1)}, u32[]{:S(2)}) copy-start(bf16[1,128,2048]{2,1,0:T(8,128)(2,1)} %param.17) | copy-start | bytes 1572868
  54.2 19.8 %copy-start.12 = (bf16[1,512,128]{2,1,0:T(8,128)(2,1)S(1)}, bf16[1,512,128]{2,1,0:T(8,128)(2,1)}, u32[]{:S(2)}) copy-start(bf16[1,512,128]{2,1,0:T(8,128)(2,1)} %param.16) | copy-start | bytes 393220
  74.0 7.8 %copy-start.16 = (s32[1,128,6]{1,0,2:T(1,128)S(1)}, s32[1,128,6]{1,0,2:T(1,128)}, u32[]{:S(2)}) copy-start(s32[1,128,6]{1,0,2:T(1,128)} %param.20) | copy-start | bytes 9220
  75.5 12.6 %copy-start.13 = (bf16[1,128,256]{2,1,0:T(8,128)(2,1)S(1)}, bf16[1,128,256]{2,1,0:T(8,128)(2,1)}, u32[]{:S(2)}) copy-start(bf16[1,128,256]{2,1,0:T(8,128)(2,1)} %param.14) | copy-start | bytes 196612
  75.5 12.6 %copy-start.14 = (bf16[64,256]{1,0:T(8,128)(2,1)S(1)}, bf16[64,256]{1,0:T(8,128)(2,1)}, u32[]{:S(2)}) copy-start(bf16[64,256]{1,0:T(8,128)(2,1)} %router_ref.1) | copy-start | bytes 98308
  75.5 12.6 %all-to-all-start.2 = ((bf16[8,128,256]{2,1,0:T(8,128)(2,1)}), bf16[8,128,256]{2,1,0:T(8,128)(2,1)S(1)}, u32[]{:S(2)}, u32[]{:S(2)}) async-start(bf16[8,128,256]{2,1,0:T(8,128)(2,1)} %shard_map.132), calls=%async_computation.2 | async-start | bytes 1048576 | tf_op jit(solution)/shard_map/all_to_all | solution.py:233
  81.8 28.5 %copy-start.2 = (bf16[1,176,2048]{2,1,0:T(8,128)(2,1)S(1)}, bf16[1,176,2048]{2,1,0:T(8,128)(2,1)}, u32[]{:S(2)}) copy-start(bf16[1,176,2048]{2,1,0:T(8,128)(2,1)} %param.22) | copy-start | bytes 2162692
  89.4 54.1 %all-to-all-start.3 = ((bf16[128,8,256]{2,1,0:T(8,128)(2,1)}), bf16[128,8,256]{2,1,0:T(8,128)(2,1)S(1)}, u32[]{:S(2)}, u32[]{:S(2)}) async-start(bf16[128,8,256]{2,1,0:T(8,128)(2,1)} %bitcast.16), calls=%async_computation.3 | async-start | bytes 1048576 | tf_op jit(solution)/shard_map/all_to_all | solution.py:233
  110.3 25.5 %collective-permute-start.5 = (bf16[176,2048]{1,0:T(8,128)(2,1)S(1)}, bf16[176,2048]{1,0:T(8,128)(2,1)S(1)}, u32[]{:S(2)}, u32[]{:S(2)}) collective-permute-start(bf16[176,2048]{1,0:T(8,128)(2,1)S(1)} %bitcast.41), channel_id=1, source_target_pairs={{0,8},{8,0},{1,9},{9,1},{2,10},{10,2},{3,11},{11,3},{4,12},{12,4},... | collective-permute-start | bytes 2162696 | tf_op jit(solution)/shard_map/ppermute | solution.py:246
  113.4 30.3 %collective-permute-start.6 = (bf16[16,256]{1,0:T(8,128)(2,1)S(1)}, bf16[16,256]{1,0:T(8,128)(2,1)S(1)}, u32[]{:S(2)}, u32[]{:S(2)}) collective-permute-start(bf16[16,256]{1,0:T(8,128)(2,1)S(1)} %get-tuple-element.22), channel_id=1, source_target_pairs={{0,8},{8,0},{1,9},{9,1},{2,10},{10,2},{3,11},{11,3},{4,12},{12,4},... | collective-permute-start | bytes 24584 | tf_op jit(solution)/shard_map/ppermute | solution.py:246
  135.8 0.9 copy-start.7
  145.2 30.7 %all-to-all-start.4 = ((bf16[4,1056,256]{2,1,0:T(8,128)(2,1)}), bf16[4,1056,256]{2,1,0:T(8,128)(2,1)S(1)}, u32[]{:S(2)}, u32[]{:S(2)}) async-start(bf16[4,1056,256]{2,1,0:T(8,128)(2,1)} %broadcast_in_dim.42), calls=%async_computation.4 | async-start | bytes 4325376 | tf_op jit(solution)/shard_map/all_to_all | solution.py:233
  148.8 21.5 %collective-permute-start.7 = (bf16[1408,256]{1,0:T(8,128)(2,1)}, bf16[1408,256]{1,0:T(8,128)(2,1)S(1)}, u32[]{:S(2)}, u32[]{:S(2)}) collective-permute-start(bf16[1408,256]{1,0:T(8,128)(2,1)} %bitcast.43), channel_id=1, source_target_pairs={{0,8},{8,0},{1,9},{9,1},{2,10},{10,2},{3,11},{11,3},{4,12},{12,4},... | collective-permute-start | bytes 2162696 | tf_op jit(solution)/shard_map/ppermute | solution.py:246
  170.3 0.9 copy-start.9
  175.9 1.1 copy-start.3
  177.0 1.1 copy-start.6
  178.1 1.1 copy-start.8
  183.3 21.6 %copy-start.4 = (bf16[1,1408,256]{2,1,0:T(8,128)(2,1)S(1)}, bf16[1,1408,256]{2,1,0:T(8,128)(2,1)}, u32[]{:S(2)}) copy-start(bf16[1,1408,256]{2,1,0:T(8,128)(2,1)} %param.23) | copy-start | bytes 2162692
  183.3 21.6 %copy-start.10 = (bf16[1408,256]{1,0:T(8,128)(2,1)S(1)}, bf16[1408,256]{1,0:T(8,128)(2,1)}, u32[]{:S(2)}) copy-start(bf16[1408,256]{1,0:T(8,128)(2,1)} %copy-done.9) | copy-start | bytes 2162692

commit v5 on v4

--- a/solution.py
+++ b/solution.py
@@ -163,22 +163,33 @@
     pick_ref[...] = jnp.concatenate([upper, lower], axis=0).astype(bf16)
 
 
-def gate_kernel(at_ref, rows_ref, gain_ref, gate_ref, up_ref, gate2_ref, up2_ref, out_ref, normed_ref):
-    n_y, _, width = rows_ref.shape
+def gate_kernel(
+    at_ref, own_ref, low_ref, high_ref, far0_ref, far1_ref, gain_ref,
+    gate_ref, up_ref, gate2_ref, up2_ref, out_ref, normed_ref,
+):
     count, features = normed_ref.shape
-    half = at_ref[2]
+    width = own_ref.shape[1]
+    half, own_y = at_ref[2], at_ref[3]
+    n_y = features // width // 2
+    pieces = []
+    for shift, first, second in (
+        (0, own_ref, own_ref),
+        (n_y - 1, low_ref, low_ref),
+        (1, high_ref, high_ref),
+        (2, far0_ref, far1_ref),
+    ):
+        y = (own_y + shift) % n_y
+        pieces.append((y, first, 0))
+        pieces.append((n_y + y, second, second.shape[0] - 32 - count))
     squares = jnp.zeros((count, 1), f32)
-    for x in range(2):
-        for y in range(n_y):
-            wide = rows_ref[y, x * count : (x + 1) * count, :].astype(f32)
-            squares = squares + jnp.sum(wide * wide, axis=1, keepdims=True)
+    for _, ref, at in pieces:
+        wide = ref[at : at + count, :].astype(f32)
+        squares = squares + jnp.sum(wide * wide, axis=1, keepdims=True)
     inverse = lax.rsqrt(squares / features + epsilon)
-    for x in range(2):
-        for y in range(n_y):
-            s = x * n_y + y
-            wide = rows_ref[y, x * count : (x + 1) * count, :].astype(f32)
-            scaled = wide * gain_ref[s, 0:1, :].astype(f32)
-            normed_ref[:, s * width : (s + 1) * width] = (scaled * inverse).astype(bf16)
+    for s, ref, at in pieces:
+        scaled = ref[at : at + count, :].astype(f32) * gain_ref[s][0:1].astype(f32)
+        lanes = pl.ds(pl.multiple_of(s * width, 128), width)
+        normed_ref[:, lanes] = (scaled * inverse).astype(bf16)
     units = gate_ref.shape[0]
     for a, (g_ref, u_ref) in enumerate(((gate_ref, up_ref), (gate2_ref, up2_ref))):
         gate = dot(g_ref[...], normed_ref[...], 1, 1)
@@ -199,12 +210,13 @@
         out_ref[half ^ a] = dot(act_all_ref[...], ref[...], 0, 0).astype(bf16)
 
 
-def combine_kernel(experts, capacity, features, row_ref, routes_ref, place_ref, back_ref, out_ref):
+def combine_kernel(experts, capacity, features, routes_ref, place_ref, back_ref, *refs):
+    row_refs, out_ref = refs[:-1], refs[-1]
     rows = out_ref.shape[0]
     total = jnp.zeros((8, rows), f32)
-    for s in range(row_ref.shape[0]):
-        for at in range(experts * capacity, row_ref.shape[1], 16):
-            terms = row_ref[s, at : at + 16, :].astype(f32)
+    for ref in row_refs:
+        for at in range(ref.shape[0] - 32, ref.shape[0], 16):
+            terms = ref[at : at + 16, :].astype(f32)
             total = total + (terms[0:8, 0:rows] + terms[0:8, rows:] + terms[8:16, 0:rows])
     routes = routes_ref[...]
     top = routes.shape[0]
@@ -338,18 +350,28 @@
     received, up2 = lax.optimization_barrier((received, up2))
     received = received.reshape(experts, n_xh, capacity // n_xh, width).swapaxes(0, 1)
     mine = jnp.concatenate([received.reshape(slots, width), picks, other_half(picks)], axis=0)
-    full_rows, down2 = lax.optimization_barrier((swap(copies(mine, n_y), "y"), down2))
+    up_turn = [(y, (y + 1) % n_y) for y in range(n_y)]
+    down_turn = [(y, (y + n_y - 1) % n_y) for y in range(n_y)]
+    low = lax.ppermute(mine, "y", up_turn)
+    high = lax.ppermute(mine, "y", down_turn)
+    far0 = lax.ppermute(low[0:count], "y", up_turn)
+    far1 = lax.ppermute(high[count:], "y", down_turn)
+    far0, far1, down2 = lax.optimization_barrier((far0, far1, down2))
     act = call(
         gate_kernel,
         shape(n_xh * units, count),
         at,
-        full_rows,
+        mine,
+        low,
+        high,
+        far0,
+        far1,
         gains,
         gate_weight[0],
         up_weight[0],
         gate2,
         up2,
-        specs=[in_smem] + [in_vmem] * 6,
+        specs=[in_smem] + [in_vmem] * 10,
         scratch=[pltpu.VMEM((count, features), bf16)],
     )
     act = swap(copies(act, n_y), "y")
@@ -369,10 +391,13 @@
     routed = call(
         lambda *refs: combine_kernel(experts, capacity, features, *refs),
         shape(rows, width),
-        full_rows,
         routes_t,
         place,
         back,
+        mine,
+        low,
+        high,
+        far1,
     )
     return (hidden[None], routed[None])
 

time: 250 us -> 246 us (0.984)
  starting transfers between devices: 73.5 us -> 81.1 us
  local copies, waits for them, and re-layouts: 9.47 us -> 3.91 us
  blocking collectives: 82.8 us -> 79.1 us
  waiting for transfers between devices: 67.9 us -> 64.2 us
    ppermute x5, waiting for transfers between devices: 49.6 us -> 35.8 us  [other_half(): return lax.ppermute(x, 'xh', [(0, 1), (1, 0)])]
    ppermute x0 -> x4, waiting for transfers between devices: none -> 12.8 us  [the longest x1 8.12 us: body(): high = lax.ppermute(mine, 'y', down_turn)]
    ppermute x0 -> x4, starting transfers between devices: none -> 11.8 us  [the longest x1 4.26 us: body(): far1 = lax.ppermute(high[count:], 'y', down_turn)]
    all_to_all x4 -> x3, waiting for transfers between devices: 18.3 us -> 13.4 us  [swap(): return lax.all_to_all(x, axes, split_axis=0, concat_axis=0, tiled=True)]
    unnamed x37 -> x31, local copies, waits for them, and re-layouts: 6.83 us -> 2.71 us
    all_to_all x3, blocking collectives: 82.8 us -> 79.1 us  [swap(): return lax.all_to_all(x, axes, split_axis=0, concat_axis=0, tiled=True)]
    all_to_all x4 -> x3, starting transfers between devices: 46.8 us -> 43.7 us  [swap(): return lax.all_to_all(x, axes, split_axis=0, concat_axis=0, tiled=True)]
  transfers between devices with their start and end apart: 12 -> 15, of which waited for: 8 -> 11; matrix products, arithmetic and copies ran while one was open for 0% -> 0% of each run, Pallas kernels for 0% -> 0%
where the time goes in v5:
time: 246 us; the launch traced here: 245 us
  starting transfers between devices  81.1 us (33%)
  blocking collectives  79.1 us (32%)
  waiting for transfers between devices  64.2 us (26%)
  Pallas kernels  14.7 us (6%)
  local copies, waits for them, and re-layouts  3.91 us (2%)
    all_to_all x3, blocking collectives, swap(): return lax.all_to_all(x, axes, split_axis=0, concat_axis=0, tiled=True)  79.1 us
    all_to_all x3, starting transfers between devices, swap(): return lax.all_to_all(x, axes, split_axis=0, concat_axis=0, tiled=True)  43.7 us
    ppermute x5, waiting for transfers between devices, other_half(): return lax.ppermute(x, 'xh', [(0, 1), (1, 0)])  35.8 us
    ppermute x5, starting transfers between devices, other_half(): return lax.ppermute(x, 'xh', [(0, 1), (1, 0)])  16.1 us
    pallas_call x7, Pallas kernels, call(): pl.pallas_call(kernel, out_shape=outs, in_specs=specs or [in_vmem] * len(...  14.7 us
    all_to_all x3, waiting for transfers between devices, swap(): return lax.all_to_all(x, axes, split_axis=0, concat_axis=0, tiled=True)  13.4 us
    ppermute x3, starting transfers between devices, all_shifts(): return [x] + [lax.ppermute(x, 'y', turn(k)) for k in range(1, n)]  9.5 us
    ppermute x1, waiting for transfers between devices, body(): high = lax.ppermute(mine, 'y', down_turn)  8.12 us
  transfers between devices with their start and end apart: 15, of which 11 were waited for; matrix products, arithmetic and copies ran while one was open for 0% of the time, Pallas kernels for 0%

profile of v5, /device:TPU:7, one launch (start us, length us, event | category | flops | bytes accessed | tf_op | source)
XLA Modules:
  0.0 244.9 jit_solution(2390335539954990461)
XLA Ops:
  2.4 16.1 %all-to-all-start = ((bf16[32,16,512]{2,1,0:T(8,128)(2,1)}), bf16[32,16,512]{2,1,0:T(8,128)(2,1)S(1)}, u32[]{:S(2)}, u32[]{:S(2)}) async-start(bf16[32,16,512]{2,1,0:T(8,128)(2,1)} %broadcast_in_dim.31), calls=%async_computation | async-start | bytes 1048576 | tf_op jit(solution)/shard_map/all_to_all | solution.py:245
  19.5 3.0 %collective-permute-start = (bf16[144,512]{1,0:T(8,128)(2,1)S(1)}, bf16[144,512]{1,0:T(8,128)(2,1)S(1)}, u32[]{:S(2)}, u32[]{:S(2)}) collective-permute-start(bf16[144,512]{1,0:T(8,128)(2,1)S(1)} %maximum_maximum_fusion), channel_id=1, source_target_pairs={{0,8},{8,0},{1,9},{9,1},{2,10},{10,2},{3,11},{11,3},{4,12},{12,4},... | collective-permute-start | bytes 442376 | tf_op jit(solution)/shard_map/ppermute | solution.py:258
  22.5 4.4 %collective-permute-done = bf16[144,512]{1,0:T(8,128)(2,1)S(1)} collective-permute-done((bf16[144,512]{1,0:T(8,128)(2,1)S(1)}, bf16[144,512]{1,0:T(8,128)(2,1)S(1)}, u32[]{:S(2)}, u32[]{:S(2)}) %collective-permute-start) | collective-permute-done | bytes 147488 | tf_op jit(solution)/shard_map/ppermute | solution.py:258
  26.9 3.6 %collective-permute-start.1 = (bf16[176,2048]{1,0:T(8,128)(2,1)S(1)}, bf16[176,2048]{1,0:T(8,128)(2,1)S(1)}, u32[]{:S(2)}, u32[]{:S(2)}) collective-permute-start(bf16[176,2048]{1,0:T(8,128)(2,1)S(1)} %bitcast.39), channel_id=1, source_target_pairs={{0,8},{8,0},{1,9},{9,1},{2,10},{10,2},{3,11},{11,3},{4,12},{12,4},... | collective-permute-start | bytes 2162696 | tf_op jit(solution)/shard_map/ppermute | solution.py:258
  30.7 4.6 %collective-permute-start.4 = (bf16[2,144,512]{2,1,0:T(8,128)(2,1)S(1)}, bf16[2,144,512]{2,1,0:T(8,128)(2,1)S(1)}, u32[]{:S(2)}, u32[]{:S(2)}) collective-permute-start(bf16[2,144,512]{2,1,0:T(8,128)(2,1)S(1)} %pad_maximum_fusion.1.refs_2_), channel_id=1, source_target_pairs={{0,6},{2,0},{4,2},{6,4},{1,7},{3,1},{5,3},{7,5},{8,14},{10,8},{12,... | collective-permute-start | bytes 884744 | tf_op jit(solution)/shard_map/ppermute | solution.py:254
  35.4 2.3 collective-permute-start.3
  37.6 2.6 %collective-permute-start.2 = (bf16[2,144,512]{2,1,0:T(8,128)(2,1)S(1)}, bf16[2,144,512]{2,1,0:T(8,128)(2,1)S(1)}, u32[]{:S(2)}, u32[]{:S(2)}) collective-permute-start(bf16[2,144,512]{2,1,0:T(8,128)(2,1)S(1)} %pad_maximum_fusion.1.refs_2_), channel_id=1, source_target_pairs={{0,2},{2,4},{4,6},{6,0},{1,3},{3,5},{5,7},{7,1},{8,10},{10,12},{12... | collective-permute-start | bytes 884744 | tf_op jit(solution)/shard_map/ppermute | solution.py:254
  40.3 8.6 %collective-permute-done.1.gate2_ref = bf16[176,2048]{1,0:T(8,128)(2,1)S(1)} collective-permute-done((bf16[176,2048]{1,0:T(8,128)(2,1)S(1)}, bf16[176,2048]{1,0:T(8,128)(2,1)S(1)}, u32[]{:S(2)}, u32[]{:S(2)}) %collective-permute-start.1) | collective-permute-done | bytes 720928 | tf_op jit(solution)/shard_map/ppermute | solution.py:258
  50.6 2.2 collective-permute-done.2.refs_3_
  52.8 3.7 %shard_map.131 = (bf16[8,144,512]{2,1,0:T(8,128)(2,1)S(1)}, bf16[8,16,256]{2,1,0:T(8,128)(2,1)S(1)}) custom-call(s32[4]{0:T(128)S(1)} %pad_add_fusion.refs_0_.at_ref, bf16[512,512]{1,0:T(8,128)(2,1)S(1)} %bitcast.36, bf16[2,144,512]{2,1,0:T(8,128)(2,1)S(1)} %pad_maximum_fusion.1.refs_2_, bf16[2,144,512]{2,1,0:T(8,128)(2,1)S(1)} %collective-permute-done.2.refs_3_, ...), custom_call_target="tpu_custom_call" | custom-call | tf_op jit(solution)/shard_map/pallas_call | solution.py:29
  56.5 17.5 %all_to_all.30.refs_0_ = bf16[8,144,512]{2,1,0:T(8,128)(2,1)S(1)} all-to-all(bf16[8,144,512]{2,1,0:T(8,128)(2,1)S(1)} %get-tuple-element.19), channel_id=1, replica_groups=mesh['z'=16,'xl'=2,'xh'=2,'y'=4,'rep'=2] {'xh','y'}, dimensions={0} | all-to-all | bytes 2359296 | tf_op jit(solution)/shard_map/all_to_all | solution.py:245
  74.0 1.6 shard_map.132
  75.6 6.2 %all-to-all-start.2 = ((bf16[8,128,256]{2,1,0:T(8,128)(2,1)}), bf16[8,128,256]{2,1,0:T(8,128)(2,1)S(1)}, u32[]{:S(2)}, u32[]{:S(2)}) async-start(bf16[8,128,256]{2,1,0:T(8,128)(2,1)} %shard_map.132), calls=%async_computation.2 | async-start | bytes 1048576 | tf_op jit(solution)/shard_map/all_to_all | solution.py:245
  82.2 6.0 %all-to-all-done.2.part_ref = bf16[8,128,256]{2,1,0:T(8,128)(2,1)S(1)} async-done(((bf16[8,128,256]{2,1,0:T(8,128)(2,1)}), bf16[8,128,256]{2,1,0:T(8,128)(2,1)S(1)}, u32[]{:S(2)}, u32[]{:S(2)}) %all-to-all-start.2) | async-done | bytes 524320 | tf_op jit(solution)/shard_map/all_to_all | solution.py:245
  89.5 21.3 %all-to-all-start.3 = ((bf16[128,8,256]{2,1,0:T(8,128)(2,1)}), bf16[128,8,256]{2,1,0:T(8,128)(2,1)S(1)}, u32[]{:S(2)}, u32[]{:S(2)}) async-start(bf16[128,8,256]{2,1,0:T(8,128)(2,1)} %bitcast.16), calls=%async_computation.3 | async-start | bytes 1048576 | tf_op jit(solution)/shard_map/all_to_all | solution.py:245
  110.9 3.2 %collective-permute-start.5 = (bf16[176,2048]{1,0:T(8,128)(2,1)S(1)}, bf16[176,2048]{1,0:T(8,128)(2,1)S(1)}, u32[]{:S(2)}, u32[]{:S(2)}) collective-permute-start(bf16[176,2048]{1,0:T(8,128)(2,1)S(1)} %bitcast.41), channel_id=1, source_target_pairs={{0,8},{8,0},{1,9},{9,1},{2,10},{10,2},{3,11},{11,3},{4,12},{12,4},... | collective-permute-start | bytes 2162696 | tf_op jit(solution)/shard_map/ppermute | solution.py:258
  114.1 3.7 %collective-permute-start.6 = (bf16[16,256]{1,0:T(8,128)(2,1)S(1)}, bf16[16,256]{1,0:T(8,128)(2,1)S(1)}, u32[]{:S(2)}, u32[]{:S(2)}) collective-permute-start(bf16[16,256]{1,0:T(8,128)(2,1)S(1)} %get-tuple-element.23), channel_id=1, source_target_pairs={{0,8},{8,0},{1,9},{9,1},{2,10},{10,2},{3,11},{11,3},{4,12},{12,4},... | collective-permute-start | bytes 24584 | tf_op jit(solution)/shard_map/ppermute | solution.py:258
  117.8 18.8 %collective-permute-done.5.up2_ref = bf16[176,2048]{1,0:T(8,128)(2,1)S(1)} collective-permute-done((bf16[176,2048]{1,0:T(8,128)(2,1)S(1)}, bf16[176,2048]{1,0:T(8,128)(2,1)S(1)}, u32[]{:S(2)}, u32[]{:S(2)}) %collective-permute-start.5) | collective-permute-done | bytes 720928 | tf_op jit(solution)/shard_map/ppermute | solution.py:258
  137.5 6.7 %all-to-all-done.3 = bf16[128,8,256]{2,1,0:T(8,128)(2,1)S(1)} async-done(((bf16[128,8,256]{2,1,0:T(8,128)(2,1)}), bf16[128,8,256]{2,1,0:T(8,128)(2,1)S(1)}, u32[]{:S(2)}, u32[]{:S(2)}) %all-to-all-start.3) | async-done | bytes 524320 | tf_op jit(solution)/shard_map/all_to_all | solution.py:245
  144.3 3.2 %collective-permute-start.8 = (bf16[1056,256]{1,0:T(8,128)(2,1)S(1)}, bf16[1056,256]{1,0:T(8,128)(2,1)S(1)}, u32[]{:S(2)}, u32[]{:S(2)}) collective-permute-start(bf16[1056,256]{1,0:T(8,128)(2,1)S(1)} %pad_maximum_fusion.own_ref.refs_3_), channel_id=1, source_target_pairs={{0,6},{2,0},{4,2},{6,4},{1,7},{3,1},{5,3},{7,5},{8,14},{10,8},{12,... | collective-permute-start | bytes 1622024 | tf_op jit(solution)/shard_map/ppermute | solution.py:356
  147.5 2.2 collective-permute-start.7
  149.7 2.5 %collective-permute-start.11 = (bf16[1408,256]{1,0:T(8,128)(2,1)S(1)}, bf16[1408,256]{1,0:T(8,128)(2,1)S(1)}, u32[]{:S(2)}, u32[]{:S(2)}) collective-permute-start(bf16[1408,256]{1,0:T(8,128)(2,1)S(1)} %bitcast.43), channel_id=1, source_target_pairs={{0,8},{8,0},{1,9},{9,1},{2,10},{10,2},{3,11},{11,3},{4,12},{12,4},... | collective-permute-start | bytes 2162696 | tf_op jit(solution)/shard_map/ppermute | solution.py:258
  152.2 8.1 %collective-permute-done.8.high_ref.refs_5_ = bf16[1056,256]{1,0:T(8,128)(2,1)S(1)} collective-permute-done((bf16[1056,256]{1,0:T(8,128)(2,1)S(1)}, bf16[1056,256]{1,0:T(8,128)(2,1)S(1)}, u32[]{:S(2)}, u32[]{:S(2)}) %collective-permute-start.8) | collective-permute-done | bytes 540704 | tf_op jit(solution)/shard_map/ppermute | solution.py:356
  160.4 4.3 %collective-permute-start.10 = (bf16[544,256]{1,0:T(8,128)(2,1)S(1)}, bf16[544,256]{1,0:T(8,128)(2,1)S(1)}, u32[]{:S(2)}, u32[]{:S(2)}) collective-permute-start(bf16[544,256]{1,0:T(8,128)(2,1)S(1)} %slice.9), channel_id=1, source_target_pairs={{0,6},{2,0},{4,2},{6,4},{1,7},{3,1},{5,3},{7,5},{8,14},{10,8},{12,... | collective-permute-start | bytes 835592 | tf_op jit(solution)/shard_map/ppermute | solution.py:358
  164.9 2.1 collective-permute-start.9
  167.0 4.0 %collective-permute-done.11.down2_ref = bf16[1408,256]{1,0:T(8,128)(2,1)S(1)} collective-permute-done((bf16[1408,256]{1,0:T(8,128)(2,1)S(1)}, bf16[1408,256]{1,0:T(8,128)(2,1)S(1)}, u32[]{:S(2)}, u32[]{:S(2)}) %collective-permute-start.11) | collective-permute-done | bytes 720928 | tf_op jit(solution)/shard_map/ppermute | solution.py:258
  171.0 4.4 %collective-permute-done.9.far0_ref = bf16[512,256]{1,0:T(8,128)(2,1)S(1)} collective-permute-done((bf16[512,256]{1,0:T(8,128)(2,1)S(1)}, bf16[512,256]{1,0:T(8,128)(2,1)S(1)}, u32[]{:S(2)}, u32[]{:S(2)}) %collective-permute-start.9) | collective-permute-done | bytes 262176 | tf_op jit(solution)/shard_map/ppermute | solution.py:357
  175.4 4.8 %shard_map.135 = bf16[352,512]{1,0:T(8,128)(2,1)S(1)} custom-call(s32[4]{0:T(128)S(1)} %pad_add_fusion.refs_0_.at_ref, bf16[1056,256]{1,0:T(8,128)(2,1)S(1)} %pad_maximum_fusion.own_ref.refs_3_, bf16[1056,256]{1,0:T(8,128)(2,1)S(1)} %collective-permute-done.7.low_ref.refs_4_, bf16[1056,256]{1,0:T(8,128)(2,1)S(1)} %collective-permute-done.8.high_ref.refs_5_, ...), custom_call_target="tpu_custom_call" | custom-call | tf_op jit(solution)/shard_map/pallas_call | solution.py:29
  180.3 20.2 %all_to_all.31.act_ref = bf16[4,352,512]{2,1,0:T(8,128)(2,1)S(1)} all-to-all(bf16[4,352,512]{2,1,0:T(8,128)(2,1)S(1)} %broadcast_in_dim.36), channel_id=1, replica_groups=mesh['z'=16,'xl'=2,'xh'=2,'y'=4,'rep'=2] {'y'}, dimensions={0} | all-to-all | bytes 2883584 | tf_op jit(solution)/shard_map/all_to_all | solution.py:245
  200.5 1.6 shard_map.136
  202.2 41.4 %all_to_all.32 = bf16[128,8,256]{2,1,0:T(8,128)(2,1)S(1)} all-to-all(bf16[128,8,256]{2,1,0:T(8,128)(2,1)S(1)} %bitcast.53), channel_id=1, replica_groups=mesh['z'=16,'xl'=2,'xh'=2,'y'=4,'rep'=2] {'z','xl','rep','xh'}, dimensions={0} | all-to-all | bytes 1048576 | tf_op jit(solution)/shard_map/all_to_all | solution.py:245
  243.5 1.4 shard_map.137
  (56 shorter events, 7.5 us)
Async XLA Ops:
  0.6 0.9 copy-start
  0.6 18.0 %copy-start.14 = (bf16[256]{0:T(256)(128)(2,1)S(1)}, bf16[256]{0:T(256)(128)(2,1)}, u32[]{:S(2)}) copy-start(bf16[256]{0:T(256)(128)(2,1)} %param.18) | copy-start | bytes 1540
  0.7 18.8 %copy-start.12 = (bf16[1,128,1,512]{3,1,2,0:T(8,128)(2,1)S(1)}, bf16[1,128,1,512]{3,1,2,0:T(8,128)(2,1)}, u32[]{:S(2)}) copy-start(bf16[1,128,1,512]{3,1,2,0:T(8,128)(2,1)} %param.12) | copy-start | bytes 393220
  0.7 26.3 %copy-start.1 = (bf16[1,176,2048]{2,1,0:T(8,128)(2,1)S(1)}, bf16[1,176,2048]{2,1,0:T(8,128)(2,1)}, u32[]{:S(2)}) copy-start(bf16[1,176,2048]{2,1,0:T(8,128)(2,1)} %param.21) | copy-start | bytes 2162692
  2.4 48.1 %all-to-all-start = ((bf16[32,16,512]{2,1,0:T(8,128)(2,1)}), bf16[32,16,512]{2,1,0:T(8,128)(2,1)S(1)}, u32[]{:S(2)}, u32[]{:S(2)}) async-start(bf16[32,16,512]{2,1,0:T(8,128)(2,1)} %broadcast_in_dim.31), calls=%async_computation | async-start | bytes 1048576 | tf_op jit(solution)/shard_map/all_to_all | solution.py:245
  19.5 7.4 %collective-permute-start = (bf16[144,512]{1,0:T(8,128)(2,1)S(1)}, bf16[144,512]{1,0:T(8,128)(2,1)S(1)}, u32[]{:S(2)}, u32[]{:S(2)}) collective-permute-start(bf16[144,512]{1,0:T(8,128)(2,1)S(1)} %maximum_maximum_fusion), channel_id=1, source_target_pairs={{0,8},{8,0},{1,9},{9,1},{2,10},{10,2},{3,11},{11,3},{4,12},{12,4},... | collective-permute-start | bytes 442376 | tf_op jit(solution)/shard_map/ppermute | solution.py:258
  26.9 22.0 %collective-permute-start.1 = (bf16[176,2048]{1,0:T(8,128)(2,1)S(1)}, bf16[176,2048]{1,0:T(8,128)(2,1)S(1)}, u32[]{:S(2)}, u32[]{:S(2)}) collective-permute-start(bf16[176,2048]{1,0:T(8,128)(2,1)S(1)} %bitcast.39), channel_id=1, source_target_pairs={{0,8},{8,0},{1,9},{9,1},{2,10},{10,2},{3,11},{11,3},{4,12},{12,4},... | collective-permute-start | bytes 2162696 | tf_op jit(solution)/shard_map/ppermute | solution.py:258
  30.7 19.8 %collective-permute-start.4 = (bf16[2,144,512]{2,1,0:T(8,128)(2,1)S(1)}, bf16[2,144,512]{2,1,0:T(8,128)(2,1)S(1)}, u32[]{:S(2)}, u32[]{:S(2)}) collective-permute-start(bf16[2,144,512]{2,1,0:T(8,128)(2,1)S(1)} %pad_maximum_fusion.1.refs_2_), channel_id=1, source_target_pairs={{0,6},{2,0},{4,2},{6,4},{1,7},{3,1},{5,3},{7,5},{8,14},{10,8},{12,... | collective-permute-start | bytes 884744 | tf_op jit(solution)/shard_map/ppermute | solution.py:254
  35.4 15.2 %collective-permute-start.3 = (bf16[2,144,512]{2,1,0:T(8,128)(2,1)S(1)}, bf16[2,144,512]{2,1,0:T(8,128)(2,1)S(1)}, u32[]{:S(2)}, u32[]{:S(2)}) collective-permute-start(bf16[2,144,512]{2,1,0:T(8,128)(2,1)S(1)} %pad_maximum_fusion.1.refs_2_), channel_id=1, source_target_pairs={{0,4},{2,6},{4,0},{6,2},{1,5},{3,7},{5,1},{7,3},{8,12},{10,14},{12... | collective-permute-start | bytes 884744 | tf_op jit(solution)/shard_map/ppermute | solution.py:254
  37.6 15.2 %collective-permute-start.2 = (bf16[2,144,512]{2,1,0:T(8,128)(2,1)S(1)}, bf16[2,144,512]{2,1,0:T(8,128)(2,1)S(1)}, u32[]{:S(2)}, u32[]{:S(2)}) collective-permute-start(bf16[2,144,512]{2,1,0:T(8,128)(2,1)S(1)} %pad_maximum_fusion.1.refs_2_), channel_id=1, source_target_pairs={{0,2},{2,4},{4,6},{6,0},{1,3},{3,5},{5,7},{7,1},{8,10},{10,12},{12... | collective-permute-start | bytes 884744 | tf_op jit(solution)/shard_map/ppermute | solution.py:254
  49.0 0.9 copy-start.4
  56.5 17.5 %copy-start.8 = (bf16[1,128,2048]{2,1,0:T(8,128)(2,1)S(1)}, bf16[1,128,2048]{2,1,0:T(8,128)(2,1)}, u32[]{:S(2)}) copy-start(bf16[1,128,2048]{2,1,0:T(8,128)(2,1)} %param.17) | copy-start | bytes 1572868
  56.5 17.5 %copy-start.9 = (bf16[1,512,128]{2,1,0:T(8,128)(2,1)S(1)}, bf16[1,512,128]{2,1,0:T(8,128)(2,1)}, u32[]{:S(2)}) copy-start(bf16[1,512,128]{2,1,0:T(8,128)(2,1)} %param.16) | copy-start | bytes 393220
  74.0 7.9 %copy-start.13 = (s32[1,128,6]{1,0,2:T(1,128)S(1)}, s32[1,128,6]{1,0,2:T(1,128)}, u32[]{:S(2)}) copy-start(s32[1,128,6]{1,0,2:T(1,128)} %param.20) | copy-start | bytes 9220
  75.6 12.6 %copy-start.10 = (bf16[1,128,256]{2,1,0:T(8,128)(2,1)S(1)}, bf16[1,128,256]{2,1,0:T(8,128)(2,1)}, u32[]{:S(2)}) copy-start(bf16[1,128,256]{2,1,0:T(8,128)(2,1)} %param.14) | copy-start | bytes 196612
  75.6 12.6 %copy-start.11 = (bf16[64,256]{1,0:T(8,128)(2,1)S(1)}, bf16[64,256]{1,0:T(8,128)(2,1)}, u32[]{:S(2)}) copy-start(bf16[64,256]{1,0:T(8,128)(2,1)} %router_ref.1) | copy-start | bytes 98308
  75.6 12.6 %all-to-all-start.2 = ((bf16[8,128,256]{2,1,0:T(8,128)(2,1)}), bf16[8,128,256]{2,1,0:T(8,128)(2,1)S(1)}, u32[]{:S(2)}, u32[]{:S(2)}) async-start(bf16[8,128,256]{2,1,0:T(8,128)(2,1)} %shard_map.132), calls=%async_computation.2 | async-start | bytes 1048576 | tf_op jit(solution)/shard_map/all_to_all | solution.py:245
  81.9 29.0 %copy-start.2 = (bf16[1,176,2048]{2,1,0:T(8,128)(2,1)S(1)}, bf16[1,176,2048]{2,1,0:T(8,128)(2,1)}, u32[]{:S(2)}) copy-start(bf16[1,176,2048]{2,1,0:T(8,128)(2,1)} %param.22) | copy-start | bytes 2162692
  89.5 54.6 %all-to-all-start.3 = ((bf16[128,8,256]{2,1,0:T(8,128)(2,1)}), bf16[128,8,256]{2,1,0:T(8,128)(2,1)S(1)}, u32[]{:S(2)}, u32[]{:S(2)}) async-start(bf16[128,8,256]{2,1,0:T(8,128)(2,1)} %bitcast.16), calls=%async_computation.3 | async-start | bytes 1048576 | tf_op jit(solution)/shard_map/all_to_all | solution.py:245
  110.8 38.9 %copy-start.3 = (bf16[1,1408,256]{2,1,0:T(8,128)(2,1)S(1)}, bf16[1,1408,256]{2,1,0:T(8,128)(2,1)}, u32[]{:S(2)}) copy-start(bf16[1,1408,256]{2,1,0:T(8,128)(2,1)} %param.23) | copy-start | bytes 2162692
  110.9 25.7 %collective-permute-start.5 = (bf16[176,2048]{1,0:T(8,128)(2,1)S(1)}, bf16[176,2048]{1,0:T(8,128)(2,1)S(1)}, u32[]{:S(2)}, u32[]{:S(2)}) collective-permute-start(bf16[176,2048]{1,0:T(8,128)(2,1)S(1)} %bitcast.41), channel_id=1, source_target_pairs={{0,8},{8,0},{1,9},{9,1},{2,10},{10,2},{3,11},{11,3},{4,12},{12,4},... | collective-permute-start | bytes 2162696 | tf_op jit(solution)/shard_map/ppermute | solution.py:258
  114.1 30.1 %collective-permute-start.6 = (bf16[16,256]{1,0:T(8,128)(2,1)S(1)}, bf16[16,256]{1,0:T(8,128)(2,1)S(1)}, u32[]{:S(2)}, u32[]{:S(2)}) collective-permute-start(bf16[16,256]{1,0:T(8,128)(2,1)S(1)} %get-tuple-element.23), channel_id=1, source_target_pairs={{0,8},{8,0},{1,9},{9,1},{2,10},{10,2},{3,11},{11,3},{4,12},{12,4},... | collective-permute-start | bytes 24584 | tf_op jit(solution)/shard_map/ppermute | solution.py:258
  136.6 0.9 copy-start.6
  144.2 31.2 %copy-start.5 = (bf16[176,2048]{1,0:T(8,128)(2,1)S(1)}, bf16[176,2048]{1,0:T(8,128)(2,1)}, u32[]{:S(2)}) copy-start(bf16[176,2048]{1,0:T(8,128)(2,1)} %copy-done.4) | copy-start | bytes 2162692
  144.2 31.2 %copy-start.7 = (bf16[176,2048]{1,0:T(8,128)(2,1)S(1)}, bf16[176,2048]{1,0:T(8,128)(2,1)}, u32[]{:S(2)}) copy-start(bf16[176,2048]{1,0:T(8,128)(2,1)} %copy-done.6) | copy-start | bytes 2162692
  144.3 16.1 %collective-permute-start.8 = (bf16[1056,256]{1,0:T(8,128)(2,1)S(1)}, bf16[1056,256]{1,0:T(8,128)(2,1)S(1)}, u32[]{:S(2)}, u32[]{:S(2)}) collective-permute-start(bf16[1056,256]{1,0:T(8,128)(2,1)S(1)} %pad_maximum_fusion.own_ref.refs_3_), channel_id=1, source_target_pairs={{0,6},{2,0},{4,2},{6,4},{1,7},{3,1},{5,3},{7,5},{8,14},{10,8},{12,... | collective-permute-start | bytes 1622024 | tf_op jit(solution)/shard_map/ppermute | solution.py:356
  147.5 17.4 %collective-permute-start.7 = (bf16[1056,256]{1,0:T(8,128)(2,1)S(1)}, bf16[1056,256]{1,0:T(8,128)(2,1)S(1)}, u32[]{:S(2)}, u32[]{:S(2)}) collective-permute-start(bf16[1056,256]{1,0:T(8,128)(2,1)S(1)} %pad_maximum_fusion.own_ref.refs_3_), channel_id=1, source_target_pairs={{0,2},{2,4},{4,6},{6,0},{1,3},{3,5},{5,7},{7,1},{8,10},{10,12},{12... | collective-permute-start | bytes 1622024 | tf_op jit(solution)/shard_map/ppermute | solution.py:355
  149.7 21.2 %collective-permute-start.11 = (bf16[1408,256]{1,0:T(8,128)(2,1)S(1)}, bf16[1408,256]{1,0:T(8,128)(2,1)S(1)}, u32[]{:S(2)}, u32[]{:S(2)}) collective-permute-start(bf16[1408,256]{1,0:T(8,128)(2,1)S(1)} %bitcast.43), channel_id=1, source_target_pairs={{0,8},{8,0},{1,9},{9,1},{2,10},{10,2},{3,11},{11,3},{4,12},{12,4},... | collective-permute-start | bytes 2162696 | tf_op jit(solution)/shard_map/ppermute | solution.py:258
  160.4 15.0 %collective-permute-start.10 = (bf16[544,256]{1,0:T(8,128)(2,1)S(1)}, bf16[544,256]{1,0:T(8,128)(2,1)S(1)}, u32[]{:S(2)}, u32[]{:S(2)}) collective-permute-start(bf16[544,256]{1,0:T(8,128)(2,1)S(1)} %slice.9), channel_id=1, source_target_pairs={{0,6},{2,0},{4,2},{6,4},{1,7},{3,1},{5,3},{7,5},{8,14},{10,8},{12,... | collective-permute-start | bytes 835592 | tf_op jit(solution)/shard_map/ppermute | solution.py:358
  164.9 10.6 %collective-permute-start.9 = (bf16[512,256]{1,0:T(8,128)(2,1)S(1)}, bf16[512,256]{1,0:T(8,128)(2,1)S(1)}, u32[]{:S(2)}, u32[]{:S(2)}) collective-permute-start(bf16[512,256]{1,0:T(8,128)(2,1)S(1)} %slice.8), channel_id=1, source_target_pairs={{0,2},{2,4},{4,6},{6,0},{1,3},{3,5},{5,7},{7,1},{8,10},{10,12},{12... | collective-permute-start | bytes 786440 | tf_op jit(solution)/shard_map/ppermute | solution.py:357

commit v6 on v5

--- a/solution.py
+++ b/solution.py
@@ -312,7 +312,6 @@
     up2 = other_half(up_weight[0])
     down2 = other_half(down_weight[0])
 
-    keys, gate2 = lax.optimization_barrier((keys, gate2))
 
     routes_t = routes[0].T
     place = call(
@@ -327,6 +326,7 @@
         *all_queries,
         specs=[in_smem] + [in_vmem] * (1 + n_y),
     )
+    partial, gate2 = lax.optimization_barrier((partial, gate2))
     partial = swap(partial, EXP)
     terms = call(
         lambda *refs: project_kernel(rows, *refs),

time: 246 us -> 246 us (level)
    ppermute x3, waiting for transfers between devices: 2.24 us -> 12.5 us  [all_shifts(): return [x] + [lax.ppermute(x, 'y', turn(k)) for k in range(1, n)]]
    ppermute x5, waiting for transfers between devices: 35.8 us -> 27.1 us  [other_half(): return lax.ppermute(x, 'xh', [(0, 1), (1, 0)])]
  transfers between devices with their start and end apart: 15 -> 15, of which waited for: 11 -> 10; matrix products, arithmetic and copies ran while one was open for 0% -> 0% of each run, Pallas kernels for 0% -> 2%
where the time goes in v6:
time: 246 us; the launch traced here: 245 us
  starting transfers between devices  80.3 us (33%)
  blocking collectives  79.5 us (32%)
  waiting for transfers between devices  65.4 us (27%)
  Pallas kernels  14.7 us (6%)
  local copies, waits for them, and re-layouts  2.99 us (1%)
    all_to_all x3, blocking collectives, swap(): return lax.all_to_all(x, axes, split_axis=0, concat_axis=0, tiled=True)  79.5 us
    all_to_all x3, starting transfers between devices, swap(): return lax.all_to_all(x, axes, split_axis=0, concat_axis=0, tiled=True)  43 us
    ppermute x5, waiting for transfers between devices, other_half(): return lax.ppermute(x, 'xh', [(0, 1), (1, 0)])  27.1 us
    ppermute x5, starting transfers between devices, other_half(): return lax.ppermute(x, 'xh', [(0, 1), (1, 0)])  16.1 us
    pallas_call x7, Pallas kernels, call(): pl.pallas_call(kernel, out_shape=outs, in_specs=specs or [in_vmem] * len(...  14.7 us
    all_to_all x3, waiting for transfers between devices, swap(): return lax.all_to_all(x, axes, split_axis=0, concat_axis=0, tiled=True)  13 us
    ppermute x3, waiting for transfers between devices, all_shifts(): return [x] + [lax.ppermute(x, 'y', turn(k)) for k in range(1, n)]  12.5 us
    ppermute x3, starting transfers between devices, all_shifts(): return [x] + [lax.ppermute(x, 'y', turn(k)) for k in range(1, n)]  9.5 us
  transfers between devices with their start and end apart: 15, of which 10 were waited for; matrix products, arithmetic and copies ran while one was open for 0% of the time, Pallas kernels for 2%

profile of v6, /device:TPU:7, one launch (start us, length us, event | category | flops | bytes accessed | tf_op | source)
XLA Modules:
  0.0 244.9 jit_solution(3998434010542425610)
XLA Ops:
  2.4 16.1 %all-to-all-start = ((bf16[32,16,512]{2,1,0:T(8,128)(2,1)}), bf16[32,16,512]{2,1,0:T(8,128)(2,1)S(1)}, u32[]{:S(2)}, u32[]{:S(2)}) async-start(bf16[32,16,512]{2,1,0:T(8,128)(2,1)} %broadcast_in_dim.31), calls=%async_computation | async-start | bytes 1048576 | tf_op jit(solution)/shard_map/all_to_all | solution.py:245
  19.5 3.0 %collective-permute-start = (bf16[144,512]{1,0:T(8,128)(2,1)S(1)}, bf16[144,512]{1,0:T(8,128)(2,1)S(1)}, u32[]{:S(2)}, u32[]{:S(2)}) collective-permute-start(bf16[144,512]{1,0:T(8,128)(2,1)S(1)} %maximum_maximum_fusion), channel_id=1, source_target_pairs={{0,8},{8,0},{1,9},{9,1},{2,10},{10,2},{3,11},{11,3},{4,12},{12,4},... | collective-permute-start | bytes 442376 | tf_op jit(solution)/shard_map/ppermute | solution.py:258
  22.5 4.4 %collective-permute-done = bf16[144,512]{1,0:T(8,128)(2,1)S(1)} collective-permute-done((bf16[144,512]{1,0:T(8,128)(2,1)S(1)}, bf16[144,512]{1,0:T(8,128)(2,1)S(1)}, u32[]{:S(2)}, u32[]{:S(2)}) %collective-permute-start) | collective-permute-done | bytes 147488 | tf_op jit(solution)/shard_map/ppermute | solution.py:258
  26.9 3.6 %collective-permute-start.4 = (bf16[176,2048]{1,0:T(8,128)(2,1)S(1)}, bf16[176,2048]{1,0:T(8,128)(2,1)S(1)}, u32[]{:S(2)}, u32[]{:S(2)}) collective-permute-start(bf16[176,2048]{1,0:T(8,128)(2,1)S(1)} %bitcast.39), channel_id=1, source_target_pairs={{0,8},{8,0},{1,9},{9,1},{2,10},{10,2},{3,11},{11,3},{4,12},{12,4},... | collective-permute-start | bytes 2162696 | tf_op jit(solution)/shard_map/ppermute | solution.py:258
  30.7 4.6 %collective-permute-start.3 = (bf16[2,144,512]{2,1,0:T(8,128)(2,1)S(1)}, bf16[2,144,512]{2,1,0:T(8,128)(2,1)S(1)}, u32[]{:S(2)}, u32[]{:S(2)}) collective-permute-start(bf16[2,144,512]{2,1,0:T(8,128)(2,1)S(1)} %pad_maximum_fusion.1.refs_2_), channel_id=1, source_target_pairs={{0,6},{2,0},{4,2},{6,4},{1,7},{3,1},{5,3},{7,5},{8,14},{10,8},{12,... | collective-permute-start | bytes 884744 | tf_op jit(solution)/shard_map/ppermute | solution.py:254
  35.3 2.3 collective-permute-start.2
  37.6 2.6 %collective-permute-start.1 = (bf16[2,144,512]{2,1,0:T(8,128)(2,1)S(1)}, bf16[2,144,512]{2,1,0:T(8,128)(2,1)S(1)}, u32[]{:S(2)}, u32[]{:S(2)}) collective-permute-start(bf16[2,144,512]{2,1,0:T(8,128)(2,1)S(1)} %pad_maximum_fusion.1.refs_2_), channel_id=1, source_target_pairs={{0,2},{2,4},{4,6},{6,0},{1,3},{3,5},{5,7},{7,1},{8,10},{10,12},{12... | collective-permute-start | bytes 884744 | tf_op jit(solution)/shard_map/ppermute | solution.py:254
  40.3 4.3 %collective-permute-done.2.refs_4_ = bf16[2,144,512]{2,1,0:T(8,128)(2,1)S(1)} collective-permute-done((bf16[2,144,512]{2,1,0:T(8,128)(2,1)S(1)}, bf16[2,144,512]{2,1,0:T(8,128)(2,1)S(1)}, u32[]{:S(2)}, u32[]{:S(2)}) %collective-permute-start.2) | collective-permute-done | bytes 294944 | tf_op jit(solution)/shard_map/ppermute | solution.py:254
  44.6 8.2 %collective-permute-done.1.refs_3_ = bf16[2,144,512]{2,1,0:T(8,128)(2,1)S(1)} collective-permute-done((bf16[2,144,512]{2,1,0:T(8,128)(2,1)S(1)}, bf16[2,144,512]{2,1,0:T(8,128)(2,1)S(1)}, u32[]{:S(2)}, u32[]{:S(2)}) %collective-permute-start.1) | collective-permute-done | bytes 294944 | tf_op jit(solution)/shard_map/ppermute | solution.py:254
  52.8 3.7 %shard_map.131 = (bf16[8,144,512]{2,1,0:T(8,128)(2,1)S(1)}, bf16[8,16,256]{2,1,0:T(8,128)(2,1)S(1)}) custom-call(s32[4]{0:T(128)S(1)} %pad_add_fusion.refs_0_.at_ref, bf16[512,512]{1,0:T(8,128)(2,1)S(1)} %bitcast.36, bf16[2,144,512]{2,1,0:T(8,128)(2,1)S(1)} %pad_maximum_fusion.1.refs_2_, bf16[2,144,512]{2,1,0:T(8,128)(2,1)S(1)} %collective-permute-done.1.refs_3_, ...), custom_call_target="tpu_custom_call" | custom-call | tf_op jit(solution)/shard_map/pallas_call | solution.py:29
  56.5 17.9 %all_to_all.30.refs_0_ = bf16[8,144,512]{2,1,0:T(8,128)(2,1)S(1)} all-to-all(bf16[8,144,512]{2,1,0:T(8,128)(2,1)S(1)} %get-tuple-element.19), channel_id=1, replica_groups=mesh['z'=16,'xl'=2,'xh'=2,'y'=4,'rep'=2] {'xh','y'}, dimensions={0} | all-to-all | bytes 2359296 | tf_op jit(solution)/shard_map/all_to_all | solution.py:245
  74.4 1.6 shard_map.132
  76.0 6.3 %all-to-all-start.2 = ((bf16[8,128,256]{2,1,0:T(8,128)(2,1)}), bf16[8,128,256]{2,1,0:T(8,128)(2,1)S(1)}, u32[]{:S(2)}, u32[]{:S(2)}) async-start(bf16[8,128,256]{2,1,0:T(8,128)(2,1)} %shard_map.132), calls=%async_computation.2 | async-start | bytes 1048576 | tf_op jit(solution)/shard_map/all_to_all | solution.py:245
  82.7 6.3 %all-to-all-done.2.part_ref = bf16[8,128,256]{2,1,0:T(8,128)(2,1)S(1)} async-done(((bf16[8,128,256]{2,1,0:T(8,128)(2,1)}), bf16[8,128,256]{2,1,0:T(8,128)(2,1)S(1)}, u32[]{:S(2)}, u32[]{:S(2)}) %all-to-all-start.2) | async-done | bytes 524320 | tf_op jit(solution)/shard_map/all_to_all | solution.py:245
  90.3 20.6 %all-to-all-start.3 = ((bf16[128,8,256]{2,1,0:T(8,128)(2,1)}), bf16[128,8,256]{2,1,0:T(8,128)(2,1)S(1)}, u32[]{:S(2)}, u32[]{:S(2)}) async-start(bf16[128,8,256]{2,1,0:T(8,128)(2,1)} %bitcast.16), calls=%async_computation.3 | async-start | bytes 1048576 | tf_op jit(solution)/shard_map/all_to_all | solution.py:245
  110.9 3.2 %collective-permute-start.5 = (bf16[176,2048]{1,0:T(8,128)(2,1)S(1)}, bf16[176,2048]{1,0:T(8,128)(2,1)S(1)}, u32[]{:S(2)}, u32[]{:S(2)}) collective-permute-start(bf16[176,2048]{1,0:T(8,128)(2,1)S(1)} %bitcast.41), channel_id=1, source_target_pairs={{0,8},{8,0},{1,9},{9,1},{2,10},{10,2},{3,11},{11,3},{4,12},{12,4},... | collective-permute-start | bytes 2162696 | tf_op jit(solution)/shard_map/ppermute | solution.py:258
  114.1 3.7 %collective-permute-start.6 = (bf16[16,256]{1,0:T(8,128)(2,1)S(1)}, bf16[16,256]{1,0:T(8,128)(2,1)S(1)}, u32[]{:S(2)}, u32[]{:S(2)}) collective-permute-start(bf16[16,256]{1,0:T(8,128)(2,1)S(1)} %get-tuple-element.23), channel_id=1, source_target_pairs={{0,8},{8,0},{1,9},{9,1},{2,10},{10,2},{3,11},{11,3},{4,12},{12,4},... | collective-permute-start | bytes 24584 | tf_op jit(solution)/shard_map/ppermute | solution.py:258
  117.8 18.8 %collective-permute-done.5.up2_ref = bf16[176,2048]{1,0:T(8,128)(2,1)S(1)} collective-permute-done((bf16[176,2048]{1,0:T(8,128)(2,1)S(1)}, bf16[176,2048]{1,0:T(8,128)(2,1)S(1)}, u32[]{:S(2)}, u32[]{:S(2)}) %collective-permute-start.5) | collective-permute-done | bytes 720928 | tf_op jit(solution)/shard_map/ppermute | solution.py:258
  137.5 6.7 %all-to-all-done.3 = bf16[128,8,256]{2,1,0:T(8,128)(2,1)S(1)} async-done(((bf16[128,8,256]{2,1,0:T(8,128)(2,1)}), bf16[128,8,256]{2,1,0:T(8,128)(2,1)S(1)}, u32[]{:S(2)}, u32[]{:S(2)}) %all-to-all-start.3) | async-done | bytes 524320 | tf_op jit(solution)/shard_map/all_to_all | solution.py:245
  144.3 3.2 %collective-permute-start.8 = (bf16[1056,256]{1,0:T(8,128)(2,1)S(1)}, bf16[1056,256]{1,0:T(8,128)(2,1)S(1)}, u32[]{:S(2)}, u32[]{:S(2)}) collective-permute-start(bf16[1056,256]{1,0:T(8,128)(2,1)S(1)} %pad_maximum_fusion.own_ref.refs_3_), channel_id=1, source_target_pairs={{0,6},{2,0},{4,2},{6,4},{1,7},{3,1},{5,3},{7,5},{8,14},{10,8},{12,... | collective-permute-start | bytes 1622024 | tf_op jit(solution)/shard_map/ppermute | solution.py:356
  147.5 2.2 collective-permute-start.7
  149.7 2.5 %collective-permute-start.11 = (bf16[1408,256]{1,0:T(8,128)(2,1)S(1)}, bf16[1408,256]{1,0:T(8,128)(2,1)S(1)}, u32[]{:S(2)}, u32[]{:S(2)}) collective-permute-start(bf16[1408,256]{1,0:T(8,128)(2,1)S(1)} %bitcast.43), channel_id=1, source_target_pairs={{0,8},{8,0},{1,9},{9,1},{2,10},{10,2},{3,11},{11,3},{4,12},{12,4},... | collective-permute-start | bytes 2162696 | tf_op jit(solution)/shard_map/ppermute | solution.py:258
  152.2 8.1 %collective-permute-done.8.high_ref.refs_5_ = bf16[1056,256]{1,0:T(8,128)(2,1)S(1)} collective-permute-done((bf16[1056,256]{1,0:T(8,128)(2,1)S(1)}, bf16[1056,256]{1,0:T(8,128)(2,1)S(1)}, u32[]{:S(2)}, u32[]{:S(2)}) %collective-permute-start.8) | collective-permute-done | bytes 540704 | tf_op jit(solution)/shard_map/ppermute | solution.py:356
  160.4 4.3 %collective-permute-start.10 = (bf16[544,256]{1,0:T(8,128)(2,1)S(1)}, bf16[544,256]{1,0:T(8,128)(2,1)S(1)}, u32[]{:S(2)}, u32[]{:S(2)}) collective-permute-start(bf16[544,256]{1,0:T(8,128)(2,1)S(1)} %slice.9), channel_id=1, source_target_pairs={{0,6},{2,0},{4,2},{6,4},{1,7},{3,1},{5,3},{7,5},{8,14},{10,8},{12,... | collective-permute-start | bytes 835592 | tf_op jit(solution)/shard_map/ppermute | solution.py:358
  164.9 2.1 collective-permute-start.9
  167.0 4.0 %collective-permute-done.11.down2_ref = bf16[1408,256]{1,0:T(8,128)(2,1)S(1)} collective-permute-done((bf16[1408,256]{1,0:T(8,128)(2,1)S(1)}, bf16[1408,256]{1,0:T(8,128)(2,1)S(1)}, u32[]{:S(2)}, u32[]{:S(2)}) %collective-permute-start.11) | collective-permute-done | bytes 720928 | tf_op jit(solution)/shard_map/ppermute | solution.py:258
  171.0 4.4 %collective-permute-done.9.far0_ref = bf16[512,256]{1,0:T(8,128)(2,1)S(1)} collective-permute-done((bf16[512,256]{1,0:T(8,128)(2,1)S(1)}, bf16[512,256]{1,0:T(8,128)(2,1)S(1)}, u32[]{:S(2)}, u32[]{:S(2)}) %collective-permute-start.9) | collective-permute-done | bytes 262176 | tf_op jit(solution)/shard_map/ppermute | solution.py:357
  175.4 4.8 %shard_map.135 = bf16[352,512]{1,0:T(8,128)(2,1)S(1)} custom-call(s32[4]{0:T(128)S(1)} %pad_add_fusion.refs_0_.at_ref, bf16[1056,256]{1,0:T(8,128)(2,1)S(1)} %pad_maximum_fusion.own_ref.refs_3_, bf16[1056,256]{1,0:T(8,128)(2,1)S(1)} %collective-permute-done.7.low_ref.refs_4_, bf16[1056,256]{1,0:T(8,128)(2,1)S(1)} %collective-permute-done.8.high_ref.refs_5_, ...), custom_call_target="tpu_custom_call" | custom-call | tf_op jit(solution)/shard_map/pallas_call | solution.py:29
  180.3 20.2 %all_to_all.31.act_ref = bf16[4,352,512]{2,1,0:T(8,128)(2,1)S(1)} all-to-all(bf16[4,352,512]{2,1,0:T(8,128)(2,1)S(1)} %broadcast_in_dim.36), channel_id=1, replica_groups=mesh['z'=16,'xl'=2,'xh'=2,'y'=4,'rep'=2] {'y'}, dimensions={0} | all-to-all | bytes 2883584 | tf_op jit(solution)/shard_map/all_to_all | solution.py:245
  200.5 1.6 shard_map.136
  202.2 41.4 %all_to_all.32 = bf16[128,8,256]{2,1,0:T(8,128)(2,1)S(1)} all-to-all(bf16[128,8,256]{2,1,0:T(8,128)(2,1)S(1)} %bitcast.53), channel_id=1, replica_groups=mesh['z'=16,'xl'=2,'xh'=2,'y'=4,'rep'=2] {'z','xl','rep','xh'}, dimensions={0} | all-to-all | bytes 1048576 | tf_op jit(solution)/shard_map/all_to_all | solution.py:245
  243.5 1.4 shard_map.137
  (56 shorter events, 5.9 us)
Async XLA Ops:
  0.6 0.9 copy-start
  0.6 17.9 %copy-start.14 = (bf16[256]{0:T(256)(128)(2,1)S(1)}, bf16[256]{0:T(256)(128)(2,1)}, u32[]{:S(2)}) copy-start(bf16[256]{0:T(256)(128)(2,1)} %param.18) | copy-start | bytes 1540
  0.7 18.7 %copy-start.12 = (bf16[1,128,1,512]{3,1,2,0:T(8,128)(2,1)S(1)}, bf16[1,128,1,512]{3,1,2,0:T(8,128)(2,1)}, u32[]{:S(2)}) copy-start(bf16[1,128,1,512]{3,1,2,0:T(8,128)(2,1)} %param.12) | copy-start | bytes 393220
  0.7 26.2 %copy-start.1 = (bf16[1,176,2048]{2,1,0:T(8,128)(2,1)S(1)}, bf16[1,176,2048]{2,1,0:T(8,128)(2,1)}, u32[]{:S(2)}) copy-start(bf16[1,176,2048]{2,1,0:T(8,128)(2,1)} %param.21) | copy-start | bytes 2162692
  2.4 50.4 %all-to-all-start = ((bf16[32,16,512]{2,1,0:T(8,128)(2,1)}), bf16[32,16,512]{2,1,0:T(8,128)(2,1)S(1)}, u32[]{:S(2)}, u32[]{:S(2)}) async-start(bf16[32,16,512]{2,1,0:T(8,128)(2,1)} %broadcast_in_dim.31), calls=%async_computation | async-start | bytes 1048576 | tf_op jit(solution)/shard_map/all_to_all | solution.py:245
  19.5 7.4 %collective-permute-start = (bf16[144,512]{1,0:T(8,128)(2,1)S(1)}, bf16[144,512]{1,0:T(8,128)(2,1)S(1)}, u32[]{:S(2)}, u32[]{:S(2)}) collective-permute-start(bf16[144,512]{1,0:T(8,128)(2,1)S(1)} %maximum_maximum_fusion), channel_id=1, source_target_pairs={{0,8},{8,0},{1,9},{9,1},{2,10},{10,2},{3,11},{11,3},{4,12},{12,4},... | collective-permute-start | bytes 442376 | tf_op jit(solution)/shard_map/ppermute | solution.py:258
  26.9 29.5 %collective-permute-start.4 = (bf16[176,2048]{1,0:T(8,128)(2,1)S(1)}, bf16[176,2048]{1,0:T(8,128)(2,1)S(1)}, u32[]{:S(2)}, u32[]{:S(2)}) collective-permute-start(bf16[176,2048]{1,0:T(8,128)(2,1)S(1)} %bitcast.39), channel_id=1, source_target_pairs={{0,8},{8,0},{1,9},{9,1},{2,10},{10,2},{3,11},{11,3},{4,12},{12,4},... | collective-permute-start | bytes 2162696 | tf_op jit(solution)/shard_map/ppermute | solution.py:258
  30.7 9.6 %collective-permute-start.3 = (bf16[2,144,512]{2,1,0:T(8,128)(2,1)S(1)}, bf16[2,144,512]{2,1,0:T(8,128)(2,1)S(1)}, u32[]{:S(2)}, u32[]{:S(2)}) collective-permute-start(bf16[2,144,512]{2,1,0:T(8,128)(2,1)S(1)} %pad_maximum_fusion.1.refs_2_), channel_id=1, source_target_pairs={{0,6},{2,0},{4,2},{6,4},{1,7},{3,1},{5,3},{7,5},{8,14},{10,8},{12,... | collective-permute-start | bytes 884744 | tf_op jit(solution)/shard_map/ppermute | solution.py:254
  35.3 9.3 %collective-permute-start.2 = (bf16[2,144,512]{2,1,0:T(8,128)(2,1)S(1)}, bf16[2,144,512]{2,1,0:T(8,128)(2,1)S(1)}, u32[]{:S(2)}, u32[]{:S(2)}) collective-permute-start(bf16[2,144,512]{2,1,0:T(8,128)(2,1)S(1)} %pad_maximum_fusion.1.refs_2_), channel_id=1, source_target_pairs={{0,4},{2,6},{4,0},{6,2},{1,5},{3,7},{5,1},{7,3},{8,12},{10,14},{12... | collective-permute-start | bytes 884744 | tf_op jit(solution)/shard_map/ppermute | solution.py:254
  37.6 15.2 %collective-permute-start.1 = (bf16[2,144,512]{2,1,0:T(8,128)(2,1)S(1)}, bf16[2,144,512]{2,1,0:T(8,128)(2,1)S(1)}, u32[]{:S(2)}, u32[]{:S(2)}) collective-permute-start(bf16[2,144,512]{2,1,0:T(8,128)(2,1)S(1)} %pad_maximum_fusion.1.refs_2_), channel_id=1, source_target_pairs={{0,2},{2,4},{4,6},{6,0},{1,3},{3,5},{5,7},{7,1},{8,10},{10,12},{12... | collective-permute-start | bytes 884744 | tf_op jit(solution)/shard_map/ppermute | solution.py:254
  56.4 17.9 %copy-start.4 = (bf16[176,2048]{1,0:T(8,128)(2,1)}, bf16[176,2048]{1,0:T(8,128)(2,1)S(1)}, u32[]{:S(2)}) copy-start(bf16[176,2048]{1,0:T(8,128)(2,1)S(1)} %collective-permute-done.4.gate2_ref) | copy-start | bytes 2162692
  56.4 17.9 %copy-start.8 = (bf16[1,128,2048]{2,1,0:T(8,128)(2,1)S(1)}, bf16[1,128,2048]{2,1,0:T(8,128)(2,1)}, u32[]{:S(2)}) copy-start(bf16[1,128,2048]{2,1,0:T(8,128)(2,1)} %param.17) | copy-start | bytes 1572868
  56.5 17.9 %copy-start.9 = (bf16[1,512,128]{2,1,0:T(8,128)(2,1)S(1)}, bf16[1,512,128]{2,1,0:T(8,128)(2,1)}, u32[]{:S(2)}) copy-start(bf16[1,512,128]{2,1,0:T(8,128)(2,1)} %param.16) | copy-start | bytes 393220
  74.4 7.9 %copy-start.13 = (s32[1,128,6]{1,0,2:T(1,128)S(1)}, s32[1,128,6]{1,0,2:T(1,128)}, u32[]{:S(2)}) copy-start(s32[1,128,6]{1,0,2:T(1,128)} %param.20) | copy-start | bytes 9220
  76.0 12.9 %copy-start.10 = (bf16[1,128,256]{2,1,0:T(8,128)(2,1)S(1)}, bf16[1,128,256]{2,1,0:T(8,128)(2,1)}, u32[]{:S(2)}) copy-start(bf16[1,128,256]{2,1,0:T(8,128)(2,1)} %param.14) | copy-start | bytes 196612
  76.0 12.9 %copy-start.11 = (bf16[64,256]{1,0:T(8,128)(2,1)S(1)}, bf16[64,256]{1,0:T(8,128)(2,1)}, u32[]{:S(2)}) copy-start(bf16[64,256]{1,0:T(8,128)(2,1)} %router_ref.1) | copy-start | bytes 98308
  76.0 12.9 %all-to-all-start.2 = ((bf16[8,128,256]{2,1,0:T(8,128)(2,1)}), bf16[8,128,256]{2,1,0:T(8,128)(2,1)S(1)}, u32[]{:S(2)}, u32[]{:S(2)}) async-start(bf16[8,128,256]{2,1,0:T(8,128)(2,1)} %shard_map.132), calls=%async_computation.2 | async-start | bytes 1048576 | tf_op jit(solution)/shard_map/all_to_all | solution.py:245
  82.3 28.5 %copy-start.2 = (bf16[1,176,2048]{2,1,0:T(8,128)(2,1)S(1)}, bf16[1,176,2048]{2,1,0:T(8,128)(2,1)}, u32[]{:S(2)}) copy-start(bf16[1,176,2048]{2,1,0:T(8,128)(2,1)} %param.22) | copy-start | bytes 2162692
  90.3 53.9 %all-to-all-start.3 = ((bf16[128,8,256]{2,1,0:T(8,128)(2,1)}), bf16[128,8,256]{2,1,0:T(8,128)(2,1)S(1)}, u32[]{:S(2)}, u32[]{:S(2)}) async-start(bf16[128,8,256]{2,1,0:T(8,128)(2,1)} %bitcast.16), calls=%async_computation.3 | async-start | bytes 1048576 | tf_op jit(solution)/shard_map/all_to_all | solution.py:245
  110.8 38.9 %copy-start.3 = (bf16[1,1408,256]{2,1,0:T(8,128)(2,1)S(1)}, bf16[1,1408,256]{2,1,0:T(8,128)(2,1)}, u32[]{:S(2)}) copy-start(bf16[1,1408,256]{2,1,0:T(8,128)(2,1)} %param.23) | copy-start | bytes 2162692
  110.9 25.7 %collective-permute-start.5 = (bf16[176,2048]{1,0:T(8,128)(2,1)S(1)}, bf16[176,2048]{1,0:T(8,128)(2,1)S(1)}, u32[]{:S(2)}, u32[]{:S(2)}) collective-permute-start(bf16[176,2048]{1,0:T(8,128)(2,1)S(1)} %bitcast.41), channel_id=1, source_target_pairs={{0,8},{8,0},{1,9},{9,1},{2,10},{10,2},{3,11},{11,3},{4,12},{12,4},... | collective-permute-start | bytes 2162696 | tf_op jit(solution)/shard_map/ppermute | solution.py:258
  114.1 30.1 %collective-permute-start.6 = (bf16[16,256]{1,0:T(8,128)(2,1)S(1)}, bf16[16,256]{1,0:T(8,128)(2,1)S(1)}, u32[]{:S(2)}, u32[]{:S(2)}) collective-permute-start(bf16[16,256]{1,0:T(8,128)(2,1)S(1)} %get-tuple-element.23), channel_id=1, source_target_pairs={{0,8},{8,0},{1,9},{9,1},{2,10},{10,2},{3,11},{11,3},{4,12},{12,4},... | collective-permute-start | bytes 24584 | tf_op jit(solution)/shard_map/ppermute | solution.py:258
  136.6 0.9 copy-start.6
  144.2 31.2 %copy-start.5 = (bf16[176,2048]{1,0:T(8,128)(2,1)S(1)}, bf16[176,2048]{1,0:T(8,128)(2,1)}, u32[]{:S(2)}) copy-start(bf16[176,2048]{1,0:T(8,128)(2,1)} %copy-done.4) | copy-start | bytes 2162692
  144.2 31.2 %copy-start.7 = (bf16[176,2048]{1,0:T(8,128)(2,1)S(1)}, bf16[176,2048]{1,0:T(8,128)(2,1)}, u32[]{:S(2)}) copy-start(bf16[176,2048]{1,0:T(8,128)(2,1)} %copy-done.6) | copy-start | bytes 2162692
  144.3 16.1 %collective-permute-start.8 = (bf16[1056,256]{1,0:T(8,128)(2,1)S(1)}, bf16[1056,256]{1,0:T(8,128)(2,1)S(1)}, u32[]{:S(2)}, u32[]{:S(2)}) collective-permute-start(bf16[1056,256]{1,0:T(8,128)(2,1)S(1)} %pad_maximum_fusion.own_ref.refs_3_), channel_id=1, source_target_pairs={{0,6},{2,0},{4,2},{6,4},{1,7},{3,1},{5,3},{7,5},{8,14},{10,8},{12,... | collective-permute-start | bytes 1622024 | tf_op jit(solution)/shard_map/ppermute | solution.py:356
  147.5 17.4 %collective-permute-start.7 = (bf16[1056,256]{1,0:T(8,128)(2,1)S(1)}, bf16[1056,256]{1,0:T(8,128)(2,1)S(1)}, u32[]{:S(2)}, u32[]{:S(2)}) collective-permute-start(bf16[1056,256]{1,0:T(8,128)(2,1)S(1)} %pad_maximum_fusion.own_ref.refs_3_), channel_id=1, source_target_pairs={{0,2},{2,4},{4,6},{6,0},{1,3},{3,5},{5,7},{7,1},{8,10},{10,12},{12... | collective-permute-start | bytes 1622024 | tf_op jit(solution)/shard_map/ppermute | solution.py:355
  149.7 21.2 %collective-permute-start.11 = (bf16[1408,256]{1,0:T(8,128)(2,1)S(1)}, bf16[1408,256]{1,0:T(8,128)(2,1)S(1)}, u32[]{:S(2)}, u32[]{:S(2)}) collective-permute-start(bf16[1408,256]{1,0:T(8,128)(2,1)S(1)} %bitcast.43), channel_id=1, source_target_pairs={{0,8},{8,0},{1,9},{9,1},{2,10},{10,2},{3,11},{11,3},{4,12},{12,4},... | collective-permute-start | bytes 2162696 | tf_op jit(solution)/shard_map/ppermute | solution.py:258
  160.4 15.0 %collective-permute-start.10 = (bf16[544,256]{1,0:T(8,128)(2,1)S(1)}, bf16[544,256]{1,0:T(8,128)(2,1)S(1)}, u32[]{:S(2)}, u32[]{:S(2)}) collective-permute-start(bf16[544,256]{1,0:T(8,128)(2,1)S(1)} %slice.9), channel_id=1, source_target_pairs={{0,6},{2,0},{4,2},{6,4},{1,7},{3,1},{5,3},{7,5},{8,14},{10,8},{12,... | collective-permute-start | bytes 835592 | tf_op jit(solution)/shard_map/ppermute | solution.py:358
  164.9 10.6 %collective-permute-start.9 = (bf16[512,256]{1,0:T(8,128)(2,1)S(1)}, bf16[512,256]{1,0:T(8,128)(2,1)S(1)}, u32[]{:S(2)}, u32[]{:S(2)}) collective-permute-start(bf16[512,256]{1,0:T(8,128)(2,1)S(1)} %slice.8), channel_id=1, source_target_pairs={{0,2},{2,4},{4,6},{6,0},{1,3},{3,5},{5,7},{7,1},{8,10},{10,12},{12... | collective-permute-start | bytes 786440 | tf_op jit(solution)/shard_map/ppermute | solution.py:357

commit v7 on v5

--- a/solution.py
+++ b/solution.py
@@ -192,8 +192,9 @@
         normed_ref[:, lanes] = (scaled * inverse).astype(bf16)
     units = gate_ref.shape[0]
     for a, (g_ref, u_ref) in enumerate(((gate_ref, up_ref), (gate2_ref, up2_ref))):
-        gate = dot(g_ref[...], normed_ref[...], 1, 1)
-        up = dot(u_ref[...], normed_ref[...], 1, 1)
+        pair = jnp.concatenate([g_ref[...], u_ref[...]], axis=0)
+        both = dot(pair, normed_ref[...], 1, 1)
+        gate, up = both[0:units], both[units:]
         act = (gate / (1.0 + jnp.exp(-gate)) * up).astype(bf16)
         out_ref[pl.ds(pl.multiple_of((half ^ a) * units, 16), units), :] = act
 

time: 246 us -> 245 us (level)
  no operation moved by 1% of the time
where the time goes in v7:
time: 245 us; the launch traced here: 244 us
  starting transfers between devices  80.9 us (33%)
  blocking collectives  79.1 us (32%)
  waiting for transfers between devices  64.4 us (26%)
  Pallas kernels  13.5 us (6%)
  local copies, waits for them, and re-layouts  3.91 us (2%)
    all_to_all x3, blocking collectives, swap(): return lax.all_to_all(x, axes, split_axis=0, concat_axis=0, tiled=True)  79.1 us
    all_to_all x3, starting transfers between devices, swap(): return lax.all_to_all(x, axes, split_axis=0, concat_axis=0, tiled=True)  43.7 us
    ppermute x5, waiting for transfers between devices, other_half(): return lax.ppermute(x, 'xh', [(0, 1), (1, 0)])  36 us
    ppermute x5, starting transfers between devices, other_half(): return lax.ppermute(x, 'xh', [(0, 1), (1, 0)])  16.1 us
    pallas_call x7, Pallas kernels, call(): pl.pallas_call(kernel, out_shape=outs, in_specs=specs or [in_vmem] * len(...  13.5 us
    all_to_all x3, waiting for transfers between devices, swap(): return lax.all_to_all(x, axes, split_axis=0, concat_axis=0, tiled=True)  13.4 us
    ppermute x3, starting transfers between devices, all_shifts(): return [x] + [lax.ppermute(x, 'y', turn(k)) for k in range(1, n)]  9.5 us
    ppermute x1, waiting for transfers between devices, body(): high = lax.ppermute(mine, 'y', down_turn)  8.12 us
  transfers between devices with their start and end apart: 15, of which 11 were waited for; matrix products, arithmetic and copies ran while one was open for 0% of the time, Pallas kernels for 0%

profile of v7, /device:TPU:7, one launch (start us, length us, event | category | flops | bytes accessed | tf_op | source)
XLA Modules:
  0.0 243.8 jit_solution(3986770287265805048)
XLA Ops:
  2.4 16.1 %all-to-all-start = ((bf16[32,16,512]{2,1,0:T(8,128)(2,1)}), bf16[32,16,512]{2,1,0:T(8,128)(2,1)S(1)}, u32[]{:S(2)}, u32[]{:S(2)}) async-start(bf16[32,16,512]{2,1,0:T(8,128)(2,1)} %broadcast_in_dim.31), calls=%async_computation | async-start | bytes 1048576 | tf_op jit(solution)/shard_map/all_to_all | solution.py:246
  19.5 3.0 %collective-permute-start = (bf16[144,512]{1,0:T(8,128)(2,1)S(1)}, bf16[144,512]{1,0:T(8,128)(2,1)S(1)}, u32[]{:S(2)}, u32[]{:S(2)}) collective-permute-start(bf16[144,512]{1,0:T(8,128)(2,1)S(1)} %maximum_maximum_fusion), channel_id=1, source_target_pairs={{0,8},{8,0},{1,9},{9,1},{2,10},{10,2},{3,11},{11,3},{4,12},{12,4},... | collective-permute-start | bytes 442376 | tf_op jit(solution)/shard_map/ppermute | solution.py:259
  22.5 4.4 %collective-permute-done = bf16[144,512]{1,0:T(8,128)(2,1)S(1)} collective-permute-done((bf16[144,512]{1,0:T(8,128)(2,1)S(1)}, bf16[144,512]{1,0:T(8,128)(2,1)S(1)}, u32[]{:S(2)}, u32[]{:S(2)}) %collective-permute-start) | collective-permute-done | bytes 147488 | tf_op jit(solution)/shard_map/ppermute | solution.py:259
  26.9 3.6 %collective-permute-start.1 = (bf16[176,2048]{1,0:T(8,128)(2,1)S(1)}, bf16[176,2048]{1,0:T(8,128)(2,1)S(1)}, u32[]{:S(2)}, u32[]{:S(2)}) collective-permute-start(bf16[176,2048]{1,0:T(8,128)(2,1)S(1)} %bitcast.39), channel_id=1, source_target_pairs={{0,8},{8,0},{1,9},{9,1},{2,10},{10,2},{3,11},{11,3},{4,12},{12,4},... | collective-permute-start | bytes 2162696 | tf_op jit(solution)/shard_map/ppermute | solution.py:259
  30.7 4.6 %collective-permute-start.4 = (bf16[2,144,512]{2,1,0:T(8,128)(2,1)S(1)}, bf16[2,144,512]{2,1,0:T(8,128)(2,1)S(1)}, u32[]{:S(2)}, u32[]{:S(2)}) collective-permute-start(bf16[2,144,512]{2,1,0:T(8,128)(2,1)S(1)} %pad_maximum_fusion.1.refs_2_), channel_id=1, source_target_pairs={{0,6},{2,0},{4,2},{6,4},{1,7},{3,1},{5,3},{7,5},{8,14},{10,8},{12,... | collective-permute-start | bytes 884744 | tf_op jit(solution)/shard_map/ppermute | solution.py:255
  35.4 2.3 collective-permute-start.3
  37.6 2.6 %collective-permute-start.2 = (bf16[2,144,512]{2,1,0:T(8,128)(2,1)S(1)}, bf16[2,144,512]{2,1,0:T(8,128)(2,1)S(1)}, u32[]{:S(2)}, u32[]{:S(2)}) collective-permute-start(bf16[2,144,512]{2,1,0:T(8,128)(2,1)S(1)} %pad_maximum_fusion.1.refs_2_), channel_id=1, source_target_pairs={{0,2},{2,4},{4,6},{6,0},{1,3},{3,5},{5,7},{7,1},{8,10},{10,12},{12... | collective-permute-start | bytes 884744 | tf_op jit(solution)/shard_map/ppermute | solution.py:255
  40.3 8.6 %collective-permute-done.1.gate2_ref = bf16[176,2048]{1,0:T(8,128)(2,1)S(1)} collective-permute-done((bf16[176,2048]{1,0:T(8,128)(2,1)S(1)}, bf16[176,2048]{1,0:T(8,128)(2,1)S(1)}, u32[]{:S(2)}, u32[]{:S(2)}) %collective-permute-start.1) | collective-permute-done | bytes 720928 | tf_op jit(solution)/shard_map/ppermute | solution.py:259
  50.6 2.2 collective-permute-done.2.refs_3_
  52.8 3.7 %shard_map.131 = (bf16[8,144,512]{2,1,0:T(8,128)(2,1)S(1)}, bf16[8,16,256]{2,1,0:T(8,128)(2,1)S(1)}) custom-call(s32[4]{0:T(128)S(1)} %pad_add_fusion.refs_0_.at_ref, bf16[512,512]{1,0:T(8,128)(2,1)S(1)} %bitcast.36, bf16[2,144,512]{2,1,0:T(8,128)(2,1)S(1)} %pad_maximum_fusion.1.refs_2_, bf16[2,144,512]{2,1,0:T(8,128)(2,1)S(1)} %collective-permute-done.2.refs_3_, ...), custom_call_target="tpu_custom_call" | custom-call | tf_op jit(solution)/shard_map/pallas_call | solution.py:29
  56.5 17.5 %all_to_all.30.refs_0_ = bf16[8,144,512]{2,1,0:T(8,128)(2,1)S(1)} all-to-all(bf16[8,144,512]{2,1,0:T(8,128)(2,1)S(1)} %get-tuple-element.19), channel_id=1, replica_groups=mesh['z'=16,'xl'=2,'xh'=2,'y'=4,'rep'=2] {'xh','y'}, dimensions={0} | all-to-all | bytes 2359296 | tf_op jit(solution)/shard_map/all_to_all | solution.py:246
  74.0 1.6 shard_map.132
  75.6 6.2 %all-to-all-start.2 = ((bf16[8,128,256]{2,1,0:T(8,128)(2,1)}), bf16[8,128,256]{2,1,0:T(8,128)(2,1)S(1)}, u32[]{:S(2)}, u32[]{:S(2)}) async-start(bf16[8,128,256]{2,1,0:T(8,128)(2,1)} %shard_map.132), calls=%async_computation.2 | async-start | bytes 1048576 | tf_op jit(solution)/shard_map/all_to_all | solution.py:246
  82.2 6.0 %all-to-all-done.2.part_ref = bf16[8,128,256]{2,1,0:T(8,128)(2,1)S(1)} async-done(((bf16[8,128,256]{2,1,0:T(8,128)(2,1)}), bf16[8,128,256]{2,1,0:T(8,128)(2,1)S(1)}, u32[]{:S(2)}, u32[]{:S(2)}) %all-to-all-start.2) | async-done | bytes 524320 | tf_op jit(solution)/shard_map/all_to_all | solution.py:246
  89.5 21.3 %all-to-all-start.3 = ((bf16[128,8,256]{2,1,0:T(8,128)(2,1)}), bf16[128,8,256]{2,1,0:T(8,128)(2,1)S(1)}, u32[]{:S(2)}, u32[]{:S(2)}) async-start(bf16[128,8,256]{2,1,0:T(8,128)(2,1)} %bitcast.16), calls=%async_computation.3 | async-start | bytes 1048576 | tf_op jit(solution)/shard_map/all_to_all | solution.py:246
  110.9 3.2 %collective-permute-start.5 = (bf16[176,2048]{1,0:T(8,128)(2,1)S(1)}, bf16[176,2048]{1,0:T(8,128)(2,1)S(1)}, u32[]{:S(2)}, u32[]{:S(2)}) collective-permute-start(bf16[176,2048]{1,0:T(8,128)(2,1)S(1)} %bitcast.41), channel_id=1, source_target_pairs={{0,8},{8,0},{1,9},{9,1},{2,10},{10,2},{3,11},{11,3},{4,12},{12,4},... | collective-permute-start | bytes 2162696 | tf_op jit(solution)/shard_map/ppermute | solution.py:259
  114.1 3.7 %collective-permute-start.6 = (bf16[16,256]{1,0:T(8,128)(2,1)S(1)}, bf16[16,256]{1,0:T(8,128)(2,1)S(1)}, u32[]{:S(2)}, u32[]{:S(2)}) collective-permute-start(bf16[16,256]{1,0:T(8,128)(2,1)S(1)} %get-tuple-element.23), channel_id=1, source_target_pairs={{0,8},{8,0},{1,9},{9,1},{2,10},{10,2},{3,11},{11,3},{4,12},{12,4},... | collective-permute-start | bytes 24584 | tf_op jit(solution)/shard_map/ppermute | solution.py:259
  117.8 18.8 %collective-permute-done.5.up2_ref = bf16[176,2048]{1,0:T(8,128)(2,1)S(1)} collective-permute-done((bf16[176,2048]{1,0:T(8,128)(2,1)S(1)}, bf16[176,2048]{1,0:T(8,128)(2,1)S(1)}, u32[]{:S(2)}, u32[]{:S(2)}) %collective-permute-start.5) | collective-permute-done | bytes 720928 | tf_op jit(solution)/shard_map/ppermute | solution.py:259
  137.5 6.7 %all-to-all-done.3 = bf16[128,8,256]{2,1,0:T(8,128)(2,1)S(1)} async-done(((bf16[128,8,256]{2,1,0:T(8,128)(2,1)}), bf16[128,8,256]{2,1,0:T(8,128)(2,1)S(1)}, u32[]{:S(2)}, u32[]{:S(2)}) %all-to-all-start.3) | async-done | bytes 524320 | tf_op jit(solution)/shard_map/all_to_all | solution.py:246
  144.3 3.2 %collective-permute-start.8 = (bf16[1056,256]{1,0:T(8,128)(2,1)S(1)}, bf16[1056,256]{1,0:T(8,128)(2,1)S(1)}, u32[]{:S(2)}, u32[]{:S(2)}) collective-permute-start(bf16[1056,256]{1,0:T(8,128)(2,1)S(1)} %pad_maximum_fusion.own_ref.refs_3_), channel_id=1, source_target_pairs={{0,6},{2,0},{4,2},{6,4},{1,7},{3,1},{5,3},{7,5},{8,14},{10,8},{12,... | collective-permute-start | bytes 1622024 | tf_op jit(solution)/shard_map/ppermute | solution.py:357
  147.5 2.2 collective-permute-start.7
  149.7 2.5 %collective-permute-start.11 = (bf16[1408,256]{1,0:T(8,128)(2,1)S(1)}, bf16[1408,256]{1,0:T(8,128)(2,1)S(1)}, u32[]{:S(2)}, u32[]{:S(2)}) collective-permute-start(bf16[1408,256]{1,0:T(8,128)(2,1)S(1)} %bitcast.43), channel_id=1, source_target_pairs={{0,8},{8,0},{1,9},{9,1},{2,10},{10,2},{3,11},{11,3},{4,12},{12,4},... | collective-permute-start | bytes 2162696 | tf_op jit(solution)/shard_map/ppermute | solution.py:259
  152.2 8.1 %collective-permute-done.8.high_ref.refs_5_ = bf16[1056,256]{1,0:T(8,128)(2,1)S(1)} collective-permute-done((bf16[1056,256]{1,0:T(8,128)(2,1)S(1)}, bf16[1056,256]{1,0:T(8,128)(2,1)S(1)}, u32[]{:S(2)}, u32[]{:S(2)}) %collective-permute-start.8) | collective-permute-done | bytes 540704 | tf_op jit(solution)/shard_map/ppermute | solution.py:357
  160.4 4.3 %collective-permute-start.10 = (bf16[544,256]{1,0:T(8,128)(2,1)S(1)}, bf16[544,256]{1,0:T(8,128)(2,1)S(1)}, u32[]{:S(2)}, u32[]{:S(2)}) collective-permute-start(bf16[544,256]{1,0:T(8,128)(2,1)S(1)} %slice.9), channel_id=1, source_target_pairs={{0,6},{2,0},{4,2},{6,4},{1,7},{3,1},{5,3},{7,5},{8,14},{10,8},{12,... | collective-permute-start | bytes 835592 | tf_op jit(solution)/shard_map/ppermute | solution.py:359
  164.9 1.9 collective-permute-start.9
  166.8 4.2 %collective-permute-done.11.down2_ref = bf16[1408,256]{1,0:T(8,128)(2,1)S(1)} collective-permute-done((bf16[1408,256]{1,0:T(8,128)(2,1)S(1)}, bf16[1408,256]{1,0:T(8,128)(2,1)S(1)}, u32[]{:S(2)}, u32[]{:S(2)}) %collective-permute-start.11) | collective-permute-done | bytes 720928 | tf_op jit(solution)/shard_map/ppermute | solution.py:259
  171.0 4.4 %collective-permute-done.9.far0_ref = bf16[512,256]{1,0:T(8,128)(2,1)S(1)} collective-permute-done((bf16[512,256]{1,0:T(8,128)(2,1)S(1)}, bf16[512,256]{1,0:T(8,128)(2,1)S(1)}, u32[]{:S(2)}, u32[]{:S(2)}) %collective-permute-start.9) | collective-permute-done | bytes 262176 | tf_op jit(solution)/shard_map/ppermute | solution.py:358
  175.4 3.6 %shard_map.135 = bf16[352,512]{1,0:T(8,128)(2,1)S(1)} custom-call(s32[4]{0:T(128)S(1)} %pad_add_fusion.refs_0_.at_ref, bf16[1056,256]{1,0:T(8,128)(2,1)S(1)} %pad_maximum_fusion.own_ref.refs_3_, bf16[1056,256]{1,0:T(8,128)(2,1)S(1)} %collective-permute-done.7.low_ref.refs_4_, bf16[1056,256]{1,0:T(8,128)(2,1)S(1)} %collective-permute-done.8.high_ref.refs_5_, ...), custom_call_target="tpu_custom_call" | custom-call | tf_op jit(solution)/shard_map/pallas_call | solution.py:29
  179.2 20.2 %all_to_all.31.act_ref = bf16[4,352,512]{2,1,0:T(8,128)(2,1)S(1)} all-to-all(bf16[4,352,512]{2,1,0:T(8,128)(2,1)S(1)} %broadcast_in_dim.36), channel_id=1, replica_groups=mesh['z'=16,'xl'=2,'xh'=2,'y'=4,'rep'=2] {'y'}, dimensions={0} | all-to-all | bytes 2883584 | tf_op jit(solution)/shard_map/all_to_all | solution.py:246
  199.4 1.6 shard_map.136
  201.0 41.4 %all_to_all.32 = bf16[128,8,256]{2,1,0:T(8,128)(2,1)S(1)} all-to-all(bf16[128,8,256]{2,1,0:T(8,128)(2,1)S(1)} %bitcast.53), channel_id=1, replica_groups=mesh['z'=16,'xl'=2,'xh'=2,'y'=4,'rep'=2] {'z','xl','rep','xh'}, dimensions={0} | all-to-all | bytes 1048576 | tf_op jit(solution)/shard_map/all_to_all | solution.py:246
  242.4 1.4 shard_map.137
  (56 shorter events, 7.5 us)
Async XLA Ops:
  0.6 0.9 copy-start
  0.6 18.0 %copy-start.14 = (bf16[256]{0:T(256)(128)(2,1)S(1)}, bf16[256]{0:T(256)(128)(2,1)}, u32[]{:S(2)}) copy-start(bf16[256]{0:T(256)(128)(2,1)} %param.18) | copy-start | bytes 1540
  0.7 18.8 %copy-start.12 = (bf16[1,128,1,512]{3,1,2,0:T(8,128)(2,1)S(1)}, bf16[1,128,1,512]{3,1,2,0:T(8,128)(2,1)}, u32[]{:S(2)}) copy-start(bf16[1,128,1,512]{3,1,2,0:T(8,128)(2,1)} %param.12) | copy-start | bytes 393220
  0.7 26.3 %copy-start.1 = (bf16[1,176,2048]{2,1,0:T(8,128)(2,1)S(1)}, bf16[1,176,2048]{2,1,0:T(8,128)(2,1)}, u32[]{:S(2)}) copy-start(bf16[1,176,2048]{2,1,0:T(8,128)(2,1)} %param.21) | copy-start | bytes 2162692
  2.4 48.1 %all-to-all-start = ((bf16[32,16,512]{2,1,0:T(8,128)(2,1)}), bf16[32,16,512]{2,1,0:T(8,128)(2,1)S(1)}, u32[]{:S(2)}, u32[]{:S(2)}) async-start(bf16[32,16,512]{2,1,0:T(8,128)(2,1)} %broadcast_in_dim.31), calls=%async_computation | async-start | bytes 1048576 | tf_op jit(solution)/shard_map/all_to_all | solution.py:246
  19.5 7.4 %collective-permute-start = (bf16[144,512]{1,0:T(8,128)(2,1)S(1)}, bf16[144,512]{1,0:T(8,128)(2,1)S(1)}, u32[]{:S(2)}, u32[]{:S(2)}) collective-permute-start(bf16[144,512]{1,0:T(8,128)(2,1)S(1)} %maximum_maximum_fusion), channel_id=1, source_target_pairs={{0,8},{8,0},{1,9},{9,1},{2,10},{10,2},{3,11},{11,3},{4,12},{12,4},... | collective-permute-start | bytes 442376 | tf_op jit(solution)/shard_map/ppermute | solution.py:259
  26.9 22.0 %collective-permute-start.1 = (bf16[176,2048]{1,0:T(8,128)(2,1)S(1)}, bf16[176,2048]{1,0:T(8,128)(2,1)S(1)}, u32[]{:S(2)}, u32[]{:S(2)}) collective-permute-start(bf16[176,2048]{1,0:T(8,128)(2,1)S(1)} %bitcast.39), channel_id=1, source_target_pairs={{0,8},{8,0},{1,9},{9,1},{2,10},{10,2},{3,11},{11,3},{4,12},{12,4},... | collective-permute-start | bytes 2162696 | tf_op jit(solution)/shard_map/ppermute | solution.py:259
  30.7 19.8 %collective-permute-start.4 = (bf16[2,144,512]{2,1,0:T(8,128)(2,1)S(1)}, bf16[2,144,512]{2,1,0:T(8,128)(2,1)S(1)}, u32[]{:S(2)}, u32[]{:S(2)}) collective-permute-start(bf16[2,144,512]{2,1,0:T(8,128)(2,1)S(1)} %pad_maximum_fusion.1.refs_2_), channel_id=1, source_target_pairs={{0,6},{2,0},{4,2},{6,4},{1,7},{3,1},{5,3},{7,5},{8,14},{10,8},{12,... | collective-permute-start | bytes 884744 | tf_op jit(solution)/shard_map/ppermute | solution.py:255
  35.4 15.2 %collective-permute-start.3 = (bf16[2,144,512]{2,1,0:T(8,128)(2,1)S(1)}, bf16[2,144,512]{2,1,0:T(8,128)(2,1)S(1)}, u32[]{:S(2)}, u32[]{:S(2)}) collective-permute-start(bf16[2,144,512]{2,1,0:T(8,128)(2,1)S(1)} %pad_maximum_fusion.1.refs_2_), channel_id=1, source_target_pairs={{0,4},{2,6},{4,0},{6,2},{1,5},{3,7},{5,1},{7,3},{8,12},{10,14},{12... | collective-permute-start | bytes 884744 | tf_op jit(solution)/shard_map/ppermute | solution.py:255
  37.6 15.2 %collective-permute-start.2 = (bf16[2,144,512]{2,1,0:T(8,128)(2,1)S(1)}, bf16[2,144,512]{2,1,0:T(8,128)(2,1)S(1)}, u32[]{:S(2)}, u32[]{:S(2)}) collective-permute-start(bf16[2,144,512]{2,1,0:T(8,128)(2,1)S(1)} %pad_maximum_fusion.1.refs_2_), channel_id=1, source_target_pairs={{0,2},{2,4},{4,6},{6,0},{1,3},{3,5},{5,7},{7,1},{8,10},{10,12},{12... | collective-permute-start | bytes 884744 | tf_op jit(solution)/shard_map/ppermute | solution.py:255
  49.0 0.9 copy-start.4
  56.5 17.5 %copy-start.8 = (bf16[1,128,2048]{2,1,0:T(8,128)(2,1)S(1)}, bf16[1,128,2048]{2,1,0:T(8,128)(2,1)}, u32[]{:S(2)}) copy-start(bf16[1,128,2048]{2,1,0:T(8,128)(2,1)} %param.17) | copy-start | bytes 1572868
  56.5 17.5 %copy-start.9 = (bf16[1,512,128]{2,1,0:T(8,128)(2,1)S(1)}, bf16[1,512,128]{2,1,0:T(8,128)(2,1)}, u32[]{:S(2)}) copy-start(bf16[1,512,128]{2,1,0:T(8,128)(2,1)} %param.16) | copy-start | bytes 393220
  74.0 7.9 %copy-start.13 = (s32[1,128,6]{1,0,2:T(1,128)S(1)}, s32[1,128,6]{1,0,2:T(1,128)}, u32[]{:S(2)}) copy-start(s32[1,128,6]{1,0,2:T(1,128)} %param.20) | copy-start | bytes 9220
  75.6 12.6 %copy-start.10 = (bf16[1,128,256]{2,1,0:T(8,128)(2,1)S(1)}, bf16[1,128,256]{2,1,0:T(8,128)(2,1)}, u32[]{:S(2)}) copy-start(bf16[1,128,256]{2,1,0:T(8,128)(2,1)} %param.14) | copy-start | bytes 196612
  75.6 12.6 %copy-start.11 = (bf16[64,256]{1,0:T(8,128)(2,1)S(1)}, bf16[64,256]{1,0:T(8,128)(2,1)}, u32[]{:S(2)}) copy-start(bf16[64,256]{1,0:T(8,128)(2,1)} %router_ref.1) | copy-start | bytes 98308
  75.6 12.6 %all-to-all-start.2 = ((bf16[8,128,256]{2,1,0:T(8,128)(2,1)}), bf16[8,128,256]{2,1,0:T(8,128)(2,1)S(1)}, u32[]{:S(2)}, u32[]{:S(2)}) async-start(bf16[8,128,256]{2,1,0:T(8,128)(2,1)} %shard_map.132), calls=%async_computation.2 | async-start | bytes 1048576 | tf_op jit(solution)/shard_map/all_to_all | solution.py:246
  81.9 29.0 %copy-start.2 = (bf16[1,176,2048]{2,1,0:T(8,128)(2,1)S(1)}, bf16[1,176,2048]{2,1,0:T(8,128)(2,1)}, u32[]{:S(2)}) copy-start(bf16[1,176,2048]{2,1,0:T(8,128)(2,1)} %param.22) | copy-start | bytes 2162692
  89.5 54.6 %all-to-all-start.3 = ((bf16[128,8,256]{2,1,0:T(8,128)(2,1)}), bf16[128,8,256]{2,1,0:T(8,128)(2,1)S(1)}, u32[]{:S(2)}, u32[]{:S(2)}) async-start(bf16[128,8,256]{2,1,0:T(8,128)(2,1)} %bitcast.16), calls=%async_computation.3 | async-start | bytes 1048576 | tf_op jit(solution)/shard_map/all_to_all | solution.py:246
  110.8 38.9 %copy-start.3 = (bf16[1,1408,256]{2,1,0:T(8,128)(2,1)S(1)}, bf16[1,1408,256]{2,1,0:T(8,128)(2,1)}, u32[]{:S(2)}) copy-start(bf16[1,1408,256]{2,1,0:T(8,128)(2,1)} %param.23) | copy-start | bytes 2162692
  110.9 25.7 %collective-permute-start.5 = (bf16[176,2048]{1,0:T(8,128)(2,1)S(1)}, bf16[176,2048]{1,0:T(8,128)(2,1)S(1)}, u32[]{:S(2)}, u32[]{:S(2)}) collective-permute-start(bf16[176,2048]{1,0:T(8,128)(2,1)S(1)} %bitcast.41), channel_id=1, source_target_pairs={{0,8},{8,0},{1,9},{9,1},{2,10},{10,2},{3,11},{11,3},{4,12},{12,4},... | collective-permute-start | bytes 2162696 | tf_op jit(solution)/shard_map/ppermute | solution.py:259
  114.1 30.1 %collective-permute-start.6 = (bf16[16,256]{1,0:T(8,128)(2,1)S(1)}, bf16[16,256]{1,0:T(8,128)(2,1)S(1)}, u32[]{:S(2)}, u32[]{:S(2)}) collective-permute-start(bf16[16,256]{1,0:T(8,128)(2,1)S(1)} %get-tuple-element.23), channel_id=1, source_target_pairs={{0,8},{8,0},{1,9},{9,1},{2,10},{10,2},{3,11},{11,3},{4,12},{12,4},... | collective-permute-start | bytes 24584 | tf_op jit(solution)/shard_map/ppermute | solution.py:259
  136.6 0.9 copy-start.6
  144.2 31.2 %copy-start.5 = (bf16[176,2048]{1,0:T(8,128)(2,1)S(1)}, bf16[176,2048]{1,0:T(8,128)(2,1)}, u32[]{:S(2)}) copy-start(bf16[176,2048]{1,0:T(8,128)(2,1)} %copy-done.4) | copy-start | bytes 2162692
  144.2 31.2 %copy-start.7 = (bf16[176,2048]{1,0:T(8,128)(2,1)S(1)}, bf16[176,2048]{1,0:T(8,128)(2,1)}, u32[]{:S(2)}) copy-start(bf16[176,2048]{1,0:T(8,128)(2,1)} %copy-done.6) | copy-start | bytes 2162692
  144.3 16.1 %collective-permute-start.8 = (bf16[1056,256]{1,0:T(8,128)(2,1)S(1)}, bf16[1056,256]{1,0:T(8,128)(2,1)S(1)}, u32[]{:S(2)}, u32[]{:S(2)}) collective-permute-start(bf16[1056,256]{1,0:T(8,128)(2,1)S(1)} %pad_maximum_fusion.own_ref.refs_3_), channel_id=1, source_target_pairs={{0,6},{2,0},{4,2},{6,4},{1,7},{3,1},{5,3},{7,5},{8,14},{10,8},{12,... | collective-permute-start | bytes 1622024 | tf_op jit(solution)/shard_map/ppermute | solution.py:357
  147.5 17.4 %collective-permute-start.7 = (bf16[1056,256]{1,0:T(8,128)(2,1)S(1)}, bf16[1056,256]{1,0:T(8,128)(2,1)S(1)}, u32[]{:S(2)}, u32[]{:S(2)}) collective-permute-start(bf16[1056,256]{1,0:T(8,128)(2,1)S(1)} %pad_maximum_fusion.own_ref.refs_3_), channel_id=1, source_target_pairs={{0,2},{2,4},{4,6},{6,0},{1,3},{3,5},{5,7},{7,1},{8,10},{10,12},{12... | collective-permute-start | bytes 1622024 | tf_op jit(solution)/shard_map/ppermute | solution.py:356
  149.7 21.2 %collective-permute-start.11 = (bf16[1408,256]{1,0:T(8,128)(2,1)S(1)}, bf16[1408,256]{1,0:T(8,128)(2,1)S(1)}, u32[]{:S(2)}, u32[]{:S(2)}) collective-permute-start(bf16[1408,256]{1,0:T(8,128)(2,1)S(1)} %bitcast.43), channel_id=1, source_target_pairs={{0,8},{8,0},{1,9},{9,1},{2,10},{10,2},{3,11},{11,3},{4,12},{12,4},... | collective-permute-start | bytes 2162696 | tf_op jit(solution)/shard_map/ppermute | solution.py:259
  160.4 15.0 %collective-permute-start.10 = (bf16[544,256]{1,0:T(8,128)(2,1)S(1)}, bf16[544,256]{1,0:T(8,128)(2,1)S(1)}, u32[]{:S(2)}, u32[]{:S(2)}) collective-permute-start(bf16[544,256]{1,0:T(8,128)(2,1)S(1)} %slice.9), channel_id=1, source_target_pairs={{0,6},{2,0},{4,2},{6,4},{1,7},{3,1},{5,3},{7,5},{8,14},{10,8},{12,... | collective-permute-start | bytes 835592 | tf_op jit(solution)/shard_map/ppermute | solution.py:359
  164.9 10.6 %collective-permute-start.9 = (bf16[512,256]{1,0:T(8,128)(2,1)S(1)}, bf16[512,256]{1,0:T(8,128)(2,1)S(1)}, u32[]{:S(2)}, u32[]{:S(2)}) collective-permute-start(bf16[512,256]{1,0:T(8,128)(2,1)S(1)} %slice.8), channel_id=1, source_target_pairs={{0,2},{2,4},{4,6},{6,0},{1,3},{3,5},{5,7},{7,1},{8,10},{10,12},{12... | collective-permute-start | bytes 786440 | tf_op jit(solution)/shard_map/ppermute | solution.py:358
